TPU v7x, 32 devices: a whole 2x2x4 slice. The times are simulated.
32 devices in a mesh: scene: 2 (over core), tile: 16 (over z, y, x).
Axes of the slice: x: 2, y: 2, z: 4, core: 2. Of those that a mesh axis runs over, the one named last changes fastest.
Arguments:
- gaussians: float32 [2, 32, 59, 128], P('scene', 'tile'), as said below
- consensus: float32 [2, 32, 59, 128], P('scene', 'tile'), as said below
- duals: float32 [2, 32, 59, 128], P('scene', 'tile'), may hold values from -0.6 to 0.6
- step_sizes: float32 [59], replicated, may hold values from 0.02 to 0.2
- cameras: float32 [16, 16], replicated, as said below
- camera_ids: int32 [2, 16], P('scene', 'tile'), may hold values from 0 to 15
- block_lists: int32 [2, 16, 16], P('scene', 'tile'), may hold values from 0 to 31, as said below
- depth_order: int32 [2, 16, 16], P('scene', 'tile'), may hold values from 0 to 15, as said below
- block_counts: int32 [2, 16], P('scene', 'tile'), may hold values from 1 to 16, as said below
- targets: float32 [2, 16, 3, 1024], P('scene', 'tile'), may hold values from 0 to 1
- intersection: int32 [2, 16, 2, 64], P('scene', 'tile'), may hold values from 0 to 255, as said below
Outputs:
- updated: float32 [2, 32, 59, 128], P('scene', 'tile')
- new_duals: float32 [2, 32, 59, 128], P('scene', 'tile')
Inputs may be any that keep to these rules, and one draw needn't show every extreme that they name: `gaussians`: rows 0 and 1 of each Gaussian lie in -1.5 to 1.5, row 2 in 3 to 6, rows 3 to 5 in log 0.1 to log 0.5, row 6 in 0.8 to 1.2, row 10 in -2 to 6. `consensus`: drawn like gaussians. `cameras`: rotations within 0.15 of the identity about each axis, translations within 0.3, focal lengths 80 to 120, principal point x 40 to 88, y 16 to 48. `block_lists`: each strip lists 16 block numbers whose quotients by 2 all differ. `depth_order`: each strip's entries are a permutation of its slots. `block_counts`: some strip of every group has all 16 slots live. `intersection`: the 128 entries of a device are different local Gaussian numbers and include 0 and 255.
All inputs are finite; a program needn't handle non-finite values.
Results may differ from a plain program's by a relative error of at most 0.0003.
Values sent between devices are 32-bit elements; how exact they have to be, the bound alone decides.
No kernel may reach another device: no remote copies, remote signals or barrier semaphores. Data moves between devices by JAX's collectives and lax.ppermute only.
A program may use at most 64 MiB of HBM per device.

v0:
```python
import jax
import jax.numpy as jnp
from jax import lax
from jax.sharding import PartitionSpec as P

highest = lax.Precision.HIGHEST
penalty_weight = 0.5
blur_floor = 0.3
alpha_ceiling = 0.99
sh_zero = 0.28209479177387814
sh_one = 0.4886025119029199
sh_two = (
    1.0925484305920792,
    -1.0925484305920792,
    0.31539156525252005,
    -1.0925484305920792,
    0.5462742152960396,
)
sh_three = (
    -0.5900435899266435,
    2.890611442640554,
    -0.4570457994644658,
    0.3731763325901154,
    -0.4570457994644658,
    1.445305721320277,
    -0.5900435899266435,
)


def passed_along(value, axis, steps):
    count = lax.axis_size(axis)
    first, last = (max(0, -steps), min(count, count - steps))
    return lax.ppermute(value, axis, [(source, source + steps) for source in range(first, last)])


def harmonic_basis(toward):
    comp_x, comp_y, comp_z = (toward[0], toward[1], toward[2])
    sq_x, sq_y, sq_z = (comp_x * comp_x, comp_y * comp_y, comp_z * comp_z)
    return jnp.stack(
        [
            sh_zero + 0.0 * comp_x,
            -sh_one * comp_y,
            sh_one * comp_z,
            -sh_one * comp_x,
            sh_two[0] * comp_x * comp_y,
            sh_two[1] * comp_y * comp_z,
            sh_two[2] * (2.0 * sq_z - sq_x - sq_y),
            sh_two[3] * comp_x * comp_z,
            sh_two[4] * (sq_x - sq_y),
            sh_three[0] * comp_y * (3.0 * sq_x - sq_y),
            sh_three[1] * comp_x * comp_y * comp_z,
            sh_three[2] * comp_y * (4.0 * sq_z - sq_x - sq_y),
            sh_three[3] * comp_z * (2.0 * sq_z - 3.0 * sq_x - 3.0 * sq_y),
            sh_three[4] * comp_x * (4.0 * sq_z - sq_x - sq_y),
            sh_three[5] * comp_z * (sq_x - sq_y),
            sh_three[6] * comp_x * (sq_x - 3.0 * sq_y),
        ]
    )


def gauss_features(gauss_block, camera):
    rotation = camera[0:9].reshape(3, 3)
    shift_vec = camera[9:12]
    focal_x, focal_y, center_x, center_y = (camera[12], camera[13], camera[14], camera[15])
    centre = gauss_block[0:3]
    viewed = jnp.dot(rotation, centre, precision=highest) + shift_vec[:, None]
    inverse = 1.0 / viewed[2]
    screen_x = focal_x * viewed[0] * inverse + center_x
    screen_y = focal_y * viewed[1] * inverse + center_y
    quater = gauss_block[6:10]
    quater = quater / jnp.sqrt(jnp.sum(quater * quater, 0))
    quat_w, quat_x, quat_y, quat_z = (quater[0], quater[1], quater[2], quater[3])
    rot_rows = jnp.stack(
        [
            jnp.stack(
                [
                    1.0 - 2.0 * (quat_y * quat_y + quat_z * quat_z),
                    2.0 * (quat_x * quat_y - quat_w * quat_z),
                    2.0 * (quat_x * quat_z + quat_w * quat_y),
                ]
            ),
            jnp.stack(
                [
                    2.0 * (quat_x * quat_y + quat_w * quat_z),
                    1.0 - 2.0 * (quat_x * quat_x + quat_z * quat_z),
                    2.0 * (quat_y * quat_z - quat_w * quat_x),
                ]
            ),
            jnp.stack(
                [
                    2.0 * (quat_x * quat_z - quat_w * quat_y),
                    2.0 * (quat_y * quat_z + quat_w * quat_x),
                    1.0 - 2.0 * (quat_x * quat_x + quat_y * quat_y),
                ]
            ),
        ]
    )
    scales = jnp.exp(gauss_block[3:6])
    spread = rot_rows * scales[None, :, :]
    world_axes = jnp.einsum("ij,jkg->ikg", rotation, spread, precision=highest)
    row_one = (
        focal_x * inverse * world_axes[0] - focal_x * viewed[0] * inverse * inverse * world_axes[2]
    )
    row_two = (
        focal_y * inverse * world_axes[1] - focal_y * viewed[1] * inverse * inverse * world_axes[2]
    )
    cov_xx = jnp.sum(row_one * row_one, 0) + blur_floor
    cov_xy = jnp.sum(row_one * row_two, 0)
    cov_yy = jnp.sum(row_two * row_two, 0) + blur_floor
    determ = cov_xx * cov_yy - cov_xy * cov_xy
    conic_a = cov_yy / determ
    conic_b = -cov_xy / determ
    conic_c = cov_xx / determ
    opacity = jax.nn.sigmoid(gauss_block[10])
    eye_pos = -jnp.dot(rotation.T, shift_vec, precision=highest)
    toward = centre - eye_pos[:, None]
    toward = toward / jnp.sqrt(jnp.sum(toward * toward, 0))
    coeffs = gauss_block[11:59].reshape(16, 3, -1)
    colour = jnp.sum(harmonic_basis(toward)[:, None, :] * coeffs, 0) + 0.5
    return (screen_x, screen_y, conic_a, conic_b, conic_c, opacity, colour)


def blend_block(state_pair, gauss_block, camera, pixel_x, pixel_y, strict):
    transmit, colour_sum = state_pair
    screen_x, screen_y, conic_a, conic_b, conic_c, opacity, colour = gauss_features(
        gauss_block, camera
    )
    delta_x = pixel_x[:, None] - screen_x[None, :]
    delta_y = pixel_y[:, None] - screen_y[None, :]
    exponent = (
        -0.5 * (conic_a * delta_x * delta_x + conic_c * delta_y * delta_y)
        - conic_b * delta_x * delta_y
    )
    alpha_px = jnp.minimum(alpha_ceiling, opacity * jnp.exp(exponent))
    logs_kept = jnp.log1p(-alpha_px)
    before = jnp.dot(logs_kept, strict, precision=highest)
    weight = alpha_px * transmit[:, None] * jnp.exp(before)
    colour_sum = colour_sum + jnp.einsum("cg,pg->cp", colour, weight, precision=highest)
    transmit = transmit * jnp.exp(jnp.sum(logs_kept, 1))
    return (transmit, colour_sum)


def strip_loss(listed, camera, strip_index, depth_steps, active_count, target):
    pixels = target.shape[1]
    strip_rows = pixels // 128
    pixel_index = jnp.arange(pixels, dtype=jnp.int32)
    pixel_x = (pixel_index % 128).astype(jnp.float32)
    pixel_y = (pixel_index // 128 + strip_rows * (strip_index % 4)).astype(jnp.float32)
    lane_index = jnp.arange(listed.shape[2], dtype=jnp.int32)
    strict = (lane_index[:, None] < lane_index[None, :]).astype(jnp.float32)
    blender = jax.checkpoint(
        lambda current, gauss_block: blend_block(
            current, gauss_block, camera, pixel_x, pixel_y, strict
        )
    )

    def advance(current, slot_index):
        gauss_block = listed[slot_index]
        current = lax.cond(
            slot_index < active_count,
            lambda status: blender(status, gauss_block),
            lambda status: status,
            current,
        )
        return (current, None)

    initial = (jnp.ones((pixels,), jnp.float32), jnp.zeros((3, pixels), jnp.float32))
    final_pair, unused = lax.scan(advance, initial, depth_steps)
    residual = final_pair[1] - target
    return 0.5 * jnp.sum(residual * residual)


def on_device(
    gaussians,
    consensus,
    duals,
    step_sizes,
    cameras,
    camera_ids,
    block_lists,
    depth_order,
    block_counts,
    targets,
    intersection,
):
    own_blocks = gaussians[0]
    blocks_here = own_blocks.shape[0]
    listed_ids = block_lists[0, 0]
    camera = cameras[camera_ids[0, 0]]
    strip_index = lax.axis_index("tile")
    everything = lax.all_gather(own_blocks, "tile", axis=0, tiled=True)
    listed = everything[listed_ids]
    loss_value, pullback = jax.vjp(
        lambda blocks: strip_loss(
            blocks, camera, strip_index, depth_order[0, 0], block_counts[0, 0], targets[0, 0]
        ),
        listed,
    )
    gradients = pullback(jnp.ones_like(loss_value))[0]
    peers = lax.axis_size("tile")
    owner_of = listed_ids // blocks_here
    place_in = (listed_ids % blocks_here).astype(jnp.float32)
    route = (owner_of[:, None] == jnp.arange(peers, dtype=jnp.int32)[None, :]).astype(jnp.float32)
    outgoing = jnp.einsum("kp,kgc->pgc", route, gradients, precision=highest)
    out_places = jnp.dot(place_in, route, precision=highest)
    incoming, in_places = (
        lax.all_to_all(outgoing, "tile", split_axis=0, concat_axis=0, tiled=True),
        lax.all_to_all(out_places, "tile", split_axis=0, concat_axis=0, tiled=True),
    )
    own_range = jnp.arange(blocks_here, dtype=jnp.float32)
    placer = (in_places[:, None] == own_range[None, :]).astype(jnp.float32)
    owned_grad = jnp.einsum("sb,sgc->bgc", placer, incoming, precision=highest)
    updated = own_blocks - step_sizes[None, :, None] * (
        owned_grad + penalty_weight * (own_blocks - consensus[0] + duals[0])
    )
    shifted = updated + duals[0]
    param_rows = shifted.shape[1]
    local_view = shifted.transpose(1, 0, 2).reshape(param_rows, -1)
    index_up = intersection[0, 0, 0]
    index_down = intersection[0, 0, 1]
    up_vals = local_view[:, index_up]
    down_vals = local_view[:, index_down]
    from_below = passed_along(up_vals, "scene", 1)
    from_above = passed_along(down_vals, "scene", -1)
    group_index = lax.axis_index("scene")
    group_total = lax.axis_size("scene")
    agreed_up = jnp.where(group_index < group_total - 1, 0.5 * (up_vals + from_above), up_vals)
    agreed_down = jnp.where(group_index > 0, 0.5 * (down_vals + from_below), down_vals)
    agreed = local_view.at[:, index_up].set(agreed_up).at[:, index_down].set(agreed_down)
    dual_local = local_view - agreed
    new_duals = dual_local.reshape(param_rows, blocks_here, -1).transpose(1, 0, 2)
    return (updated[None], new_duals[None])


def solution(mesh):
    placed = (
        P("scene", "tile", None, None),
        P("scene", "tile", None, None),
        P("scene", "tile", None, None),
        P(),
        P(),
        P("scene", "tile"),
        P("scene", "tile", None),
        P("scene", "tile", None),
        P("scene", "tile"),
        P("scene", "tile", None, None),
        P("scene", "tile", None, None),
    )
    return jax.shard_map(
        on_device,
        mesh=mesh,
        in_specs=placed,
        out_specs=(P("scene", "tile", None, None), P("scene", "tile", None, None)),
        check_vma=False,
    )
```

profile of v0, /device:TPU:0, one launch (start us, length us, event | category | flops | bytes accessed | tf_op | source)
XLA Modules:
  0.0 537.7 jit_solution(7253955119205149755)
XLA Ops:
  2.1 8.3 %all-to-all-start = ((f32[16,1,1]{2,1,0:T(1,128)}), f32[16,1,1]{2,1,0:T(1,128)S(1)}, u32[]{:S(2)}, u32[]{:S(2)}) async-start(f32[16,1,1]{2,1,0:T(1,128)} %bitcast.113), calls=%async_computation | async-start | bytes 16384 | tf_op jit(solution)/shard_map/all_to_all | solution.py:208
  11.3 46.8 %all-gather = f32[1,32,59,128]{3,0,2,1:T(1,128)S(1)} all-gather(f32[1,2,59,128]{3,0,2,1:T(1,128)S(1)} %copy.63), channel_id=2, replica_groups=mesh['scene'=2,'tile'=16] {'tile'}, dimensions={1}, use_global_device_ids=true | all-gather | bytes 1027072 | tf_op jit(solution)/shard_map/all_gather | solution.py:191
  59.5 189.1 %while.51 = (s32[]{:T(128)}, f32[1024]{0:T(1024)S(1)}, f32[3,1024]{1,0:T(4,128)S(1)}, s32[16]{0:T(128)S(1)}, s32[16]{0:T(128)S(1)}, /*index=5*/f32[16,16]{1,0:T(...) while((s32[]{:T(128)}, f32[1024]{0:T(1024)S(1)}, ...), condition=%wide.region_10.11_spmd.clone.clone.clone, body=%wide.region_0.10_spmd.clone.clone.sunk.clone | while | flops 211959152 | bytes 1800853 | solution.py:168
  63.4 7.3 %conditional.9 = (f32[1024]{0:T(1024)S(1)}, f32[3,1024]{1,0:T(4,128)S(1)}, f32[1,16]{1,0:T(1,128)S(1)}, f32[1,1024]{1,0:T(1,128)S(1)}, f32[1,1024]{1,0:T(1,128)S...) conditional(s32[]{:T(128)} %convert_element_type.54, ...), branch_computations={%region_1.1_spmd, %region_2.9_spmd} | conditional | flops 211911024 | bytes 1505456 | solution.py:159
  75.2 7.3 %conditional.9 = (f32[1024]{0:T(1024)S(1)}, f32[3,1024]{1,0:T(4,128)S(1)}, f32[1,16]{1,0:T(1,128)S(1)}, f32[1,1024]{1,0:T(1,128)S(1)}, f32[1,1024]{1,0:T(1,128)S...) conditional(s32[]{:T(128)} %convert_element_type.54, ...), branch_computations={%region_1.1_spmd, %region_2.9_spmd} | conditional | flops 211911024 | bytes 1505456 | solution.py:159
  87.0 7.3 %conditional.9 = (f32[1024]{0:T(1024)S(1)}, f32[3,1024]{1,0:T(4,128)S(1)}, f32[1,16]{1,0:T(1,128)S(1)}, f32[1,1024]{1,0:T(1,128)S(1)}, f32[1,1024]{1,0:T(1,128)S...) conditional(s32[]{:T(128)} %convert_element_type.54, ...), branch_computations={%region_1.1_spmd, %region_2.9_spmd} | conditional | flops 211911024 | bytes 1505456 | solution.py:159
  98.8 7.3 %conditional.9 = (f32[1024]{0:T(1024)S(1)}, f32[3,1024]{1,0:T(4,128)S(1)}, f32[1,16]{1,0:T(1,128)S(1)}, f32[1,1024]{1,0:T(1,128)S(1)}, f32[1,1024]{1,0:T(1,128)S...) conditional(s32[]{:T(128)} %convert_element_type.54, ...), branch_computations={%region_1.1_spmd, %region_2.9_spmd} | conditional | flops 211911024 | bytes 1505456 | solution.py:159
  110.6 7.3 %conditional.9 = (f32[1024]{0:T(1024)S(1)}, f32[3,1024]{1,0:T(4,128)S(1)}, f32[1,16]{1,0:T(1,128)S(1)}, f32[1,1024]{1,0:T(1,128)S(1)}, f32[1,1024]{1,0:T(1,128)S...) conditional(s32[]{:T(128)} %convert_element_type.54, ...), branch_computations={%region_1.1_spmd, %region_2.9_spmd} | conditional | flops 211911024 | bytes 1505456 | solution.py:159
  122.5 7.3 %conditional.9 = (f32[1024]{0:T(1024)S(1)}, f32[3,1024]{1,0:T(4,128)S(1)}, f32[1,16]{1,0:T(1,128)S(1)}, f32[1,1024]{1,0:T(1,128)S(1)}, f32[1,1024]{1,0:T(1,128)S...) conditional(s32[]{:T(128)} %convert_element_type.54, ...), branch_computations={%region_1.1_spmd, %region_2.9_spmd} | conditional | flops 211911024 | bytes 1505456 | solution.py:159
  134.3 7.3 %conditional.9 = (f32[1024]{0:T(1024)S(1)}, f32[3,1024]{1,0:T(4,128)S(1)}, f32[1,16]{1,0:T(1,128)S(1)}, f32[1,1024]{1,0:T(1,128)S(1)}, f32[1,1024]{1,0:T(1,128)S...) conditional(s32[]{:T(128)} %convert_element_type.54, ...), branch_computations={%region_1.1_spmd, %region_2.9_spmd} | conditional | flops 211911024 | bytes 1505456 | solution.py:159
  146.1 7.3 %conditional.9 = (f32[1024]{0:T(1024)S(1)}, f32[3,1024]{1,0:T(4,128)S(1)}, f32[1,16]{1,0:T(1,128)S(1)}, f32[1,1024]{1,0:T(1,128)S(1)}, f32[1,1024]{1,0:T(1,128)S...) conditional(s32[]{:T(128)} %convert_element_type.54, ...), branch_computations={%region_1.1_spmd, %region_2.9_spmd} | conditional | flops 211911024 | bytes 1505456 | solution.py:159
  157.9 7.3 %conditional.9 = (f32[1024]{0:T(1024)S(1)}, f32[3,1024]{1,0:T(4,128)S(1)}, f32[1,16]{1,0:T(1,128)S(1)}, f32[1,1024]{1,0:T(1,128)S(1)}, f32[1,1024]{1,0:T(1,128)S...) conditional(s32[]{:T(128)} %convert_element_type.54, ...), branch_computations={%region_1.1_spmd, %region_2.9_spmd} | conditional | flops 211911024 | bytes 1505456 | solution.py:159
  169.7 7.3 %conditional.9 = (f32[1024]{0:T(1024)S(1)}, f32[3,1024]{1,0:T(4,128)S(1)}, f32[1,16]{1,0:T(1,128)S(1)}, f32[1,1024]{1,0:T(1,128)S(1)}, f32[1,1024]{1,0:T(1,128)S...) conditional(s32[]{:T(128)} %convert_element_type.54, ...), branch_computations={%region_1.1_spmd, %region_2.9_spmd} | conditional | flops 211911024 | bytes 1505456 | solution.py:159
  181.6 7.3 %conditional.9 = (f32[1024]{0:T(1024)S(1)}, f32[3,1024]{1,0:T(4,128)S(1)}, f32[1,16]{1,0:T(1,128)S(1)}, f32[1,1024]{1,0:T(1,128)S(1)}, f32[1,1024]{1,0:T(1,128)S...) conditional(s32[]{:T(128)} %convert_element_type.54, ...), branch_computations={%region_1.1_spmd, %region_2.9_spmd} | conditional | flops 211911024 | bytes 1505456 | solution.py:159
  193.4 7.3 %conditional.9 = (f32[1024]{0:T(1024)S(1)}, f32[3,1024]{1,0:T(4,128)S(1)}, f32[1,16]{1,0:T(1,128)S(1)}, f32[1,1024]{1,0:T(1,128)S(1)}, f32[1,1024]{1,0:T(1,128)S...) conditional(s32[]{:T(128)} %convert_element_type.54, ...), branch_computations={%region_1.1_spmd, %region_2.9_spmd} | conditional | flops 211911024 | bytes 1505456 | solution.py:159
  205.2 7.3 %conditional.9 = (f32[1024]{0:T(1024)S(1)}, f32[3,1024]{1,0:T(4,128)S(1)}, f32[1,16]{1,0:T(1,128)S(1)}, f32[1,1024]{1,0:T(1,128)S(1)}, f32[1,1024]{1,0:T(1,128)S...) conditional(s32[]{:T(128)} %convert_element_type.54, ...), branch_computations={%region_1.1_spmd, %region_2.9_spmd} | conditional | flops 211911024 | bytes 1505456 | solution.py:159
  217.0 7.3 %conditional.9 = (f32[1024]{0:T(1024)S(1)}, f32[3,1024]{1,0:T(4,128)S(1)}, f32[1,16]{1,0:T(1,128)S(1)}, f32[1,1024]{1,0:T(1,128)S(1)}, f32[1,1024]{1,0:T(1,128)S...) conditional(s32[]{:T(128)} %convert_element_type.54, ...), branch_computations={%region_1.1_spmd, %region_2.9_spmd} | conditional | flops 211911024 | bytes 1505456 | solution.py:159
  228.8 7.3 %conditional.9 = (f32[1024]{0:T(1024)S(1)}, f32[3,1024]{1,0:T(4,128)S(1)}, f32[1,16]{1,0:T(1,128)S(1)}, f32[1,1024]{1,0:T(1,128)S(1)}, f32[1,1024]{1,0:T(1,128)S...) conditional(s32[]{:T(128)} %convert_element_type.54, ...), branch_computations={%region_1.1_spmd, %region_2.9_spmd} | conditional | flops 211911024 | bytes 1505456 | solution.py:159
  240.6 7.3 %conditional.9 = (f32[1024]{0:T(1024)S(1)}, f32[3,1024]{1,0:T(4,128)S(1)}, f32[1,16]{1,0:T(1,128)S(1)}, f32[1,1024]{1,0:T(1,128)S(1)}, f32[1,1024]{1,0:T(1,128)S...) conditional(s32[]{:T(128)} %convert_element_type.54, ...), branch_computations={%region_1.1_spmd, %region_2.9_spmd} | conditional | flops 211911024 | bytes 1505456 | solution.py:159
  248.7 263.9 %while.50 = (s32[]{:T(128)}, f32[16,59,128]{2,0,1:T(8,128)S(1)}, f32[1024]{0:T(1024)S(1)}, f32[3,1024]{1,0:T(4,128)S(1)}, s32[16]{0:T(128)S(1)}, /*index=5*/s32[...) while((s32[]{:T(128)}, f32[16,59,128]{2,0,1:T(8,128)S(1)}, ...), condition=%wide.region_36.37_spmd.clone, body=%wide.region_11.36_spmd.sunk.clone | while | flops 427448832 | bytes 3940749 | solution.py:168
  249.3 14.0 %conditional.8 = (f32[1024]{0:T(1024)S(1)}, f32[3,1024]{1,0:T(4,128)S(1)}, f32[1,59,128]{2,1,0:T(8,128)S(1)}) conditional(s32[]{:T(128)} %bitcast.440, (f32[1024]{0:T(1024)S(1)}, f32[3,1024]{1,0:T(4,128)S(1)}) %tuple.222, (f32[16,16]{1,0:T(8,128)S(1)}, s32[]{:T(128)}, f32[16,1024]{1,0:T(8,128)S(1)}, f32[16,1024]{1,0:T(8,128)S(1)}, ...), branch_computations={%region_12.12_spmd, %region_13.35_spmd} | conditional | flops 427441280 | bytes 3668628 | solution.py:159
  252.2 1.9 add_bitcast_fusion.3
  258.4 2.6 fusion.45
  265.8 14.0 %conditional.8 = (f32[1024]{0:T(1024)S(1)}, f32[3,1024]{1,0:T(4,128)S(1)}, f32[1,59,128]{2,1,0:T(8,128)S(1)}) conditional(s32[]{:T(128)} %bitcast.440, (f32[1024]{0:T(1024)S(1)}, f32[3,1024]{1,0:T(4,128)S(1)}) %tuple.222, (f32[16,16]{1,0:T(8,128)S(1)}, s32[]{:T(128)}, f32[16,1024]{1,0:T(8,128)S(1)}, f32[16,1024]{1,0:T(8,128)S(1)}, ...), branch_computations={%region_12.12_spmd, %region_13.35_spmd} | conditional | flops 427441280 | bytes 3668628 | solution.py:159
  268.7 1.9 add_bitcast_fusion.3
  274.9 2.6 fusion.45
  282.3 14.0 %conditional.8 = (f32[1024]{0:T(1024)S(1)}, f32[3,1024]{1,0:T(4,128)S(1)}, f32[1,59,128]{2,1,0:T(8,128)S(1)}) conditional(s32[]{:T(128)} %bitcast.440, (f32[1024]{0:T(1024)S(1)}, f32[3,1024]{1,0:T(4,128)S(1)}) %tuple.222, (f32[16,16]{1,0:T(8,128)S(1)}, s32[]{:T(128)}, f32[16,1024]{1,0:T(8,128)S(1)}, f32[16,1024]{1,0:T(8,128)S(1)}, ...), branch_computations={%region_12.12_spmd, %region_13.35_spmd} | conditional | flops 427441280 | bytes 3668628 | solution.py:159
  285.2 1.9 add_bitcast_fusion.3
  291.4 2.6 fusion.45
  298.8 14.0 %conditional.8 = (f32[1024]{0:T(1024)S(1)}, f32[3,1024]{1,0:T(4,128)S(1)}, f32[1,59,128]{2,1,0:T(8,128)S(1)}) conditional(s32[]{:T(128)} %bitcast.440, (f32[1024]{0:T(1024)S(1)}, f32[3,1024]{1,0:T(4,128)S(1)}) %tuple.222, (f32[16,16]{1,0:T(8,128)S(1)}, s32[]{:T(128)}, f32[16,1024]{1,0:T(8,128)S(1)}, f32[16,1024]{1,0:T(8,128)S(1)}, ...), branch_computations={%region_12.12_spmd, %region_13.35_spmd} | conditional | flops 427441280 | bytes 3668628 | solution.py:159
  301.7 1.9 add_bitcast_fusion.3
  307.9 2.6 fusion.45
  315.3 14.0 %conditional.8 = (f32[1024]{0:T(1024)S(1)}, f32[3,1024]{1,0:T(4,128)S(1)}, f32[1,59,128]{2,1,0:T(8,128)S(1)}) conditional(s32[]{:T(128)} %bitcast.440, (f32[1024]{0:T(1024)S(1)}, f32[3,1024]{1,0:T(4,128)S(1)}) %tuple.222, (f32[16,16]{1,0:T(8,128)S(1)}, s32[]{:T(128)}, f32[16,1024]{1,0:T(8,128)S(1)}, f32[16,1024]{1,0:T(8,128)S(1)}, ...), branch_computations={%region_12.12_spmd, %region_13.35_spmd} | conditional | flops 427441280 | bytes 3668628 | solution.py:159
  318.1 1.9 add_bitcast_fusion.3
  324.4 2.6 fusion.45
  331.8 14.0 %conditional.8 = (f32[1024]{0:T(1024)S(1)}, f32[3,1024]{1,0:T(4,128)S(1)}, f32[1,59,128]{2,1,0:T(8,128)S(1)}) conditional(s32[]{:T(128)} %bitcast.440, (f32[1024]{0:T(1024)S(1)}, f32[3,1024]{1,0:T(4,128)S(1)}) %tuple.222, (f32[16,16]{1,0:T(8,128)S(1)}, s32[]{:T(128)}, f32[16,1024]{1,0:T(8,128)S(1)}, f32[16,1024]{1,0:T(8,128)S(1)}, ...), branch_computations={%region_12.12_spmd, %region_13.35_spmd} | conditional | flops 427441280 | bytes 3668628 | solution.py:159
  334.6 1.9 add_bitcast_fusion.3
  340.9 2.6 fusion.45
  348.2 14.0 %conditional.8 = (f32[1024]{0:T(1024)S(1)}, f32[3,1024]{1,0:T(4,128)S(1)}, f32[1,59,128]{2,1,0:T(8,128)S(1)}) conditional(s32[]{:T(128)} %bitcast.440, (f32[1024]{0:T(1024)S(1)}, f32[3,1024]{1,0:T(4,128)S(1)}) %tuple.222, (f32[16,16]{1,0:T(8,128)S(1)}, s32[]{:T(128)}, f32[16,1024]{1,0:T(8,128)S(1)}, f32[16,1024]{1,0:T(8,128)S(1)}, ...), branch_computations={%region_12.12_spmd, %region_13.35_spmd} | conditional | flops 427441280 | bytes 3668628 | solution.py:159
  351.1 1.9 add_bitcast_fusion.3
  357.4 2.6 fusion.45
  364.7 14.0 %conditional.8 = (f32[1024]{0:T(1024)S(1)}, f32[3,1024]{1,0:T(4,128)S(1)}, f32[1,59,128]{2,1,0:T(8,128)S(1)}) conditional(s32[]{:T(128)} %bitcast.440, (f32[1024]{0:T(1024)S(1)}, f32[3,1024]{1,0:T(4,128)S(1)}) %tuple.222, (f32[16,16]{1,0:T(8,128)S(1)}, s32[]{:T(128)}, f32[16,1024]{1,0:T(8,128)S(1)}, f32[16,1024]{1,0:T(8,128)S(1)}, ...), branch_computations={%region_12.12_spmd, %region_13.35_spmd} | conditional | flops 427441280 | bytes 3668628 | solution.py:159
  367.6 1.9 add_bitcast_fusion.3
  373.9 2.6 fusion.45
  381.2 14.0 %conditional.8 = (f32[1024]{0:T(1024)S(1)}, f32[3,1024]{1,0:T(4,128)S(1)}, f32[1,59,128]{2,1,0:T(8,128)S(1)}) conditional(s32[]{:T(128)} %bitcast.440, (f32[1024]{0:T(1024)S(1)}, f32[3,1024]{1,0:T(4,128)S(1)}) %tuple.222, (f32[16,16]{1,0:T(8,128)S(1)}, s32[]{:T(128)}, f32[16,1024]{1,0:T(8,128)S(1)}, f32[16,1024]{1,0:T(8,128)S(1)}, ...), branch_computations={%region_12.12_spmd, %region_13.35_spmd} | conditional | flops 427441280 | bytes 3668628 | solution.py:159
  384.1 1.9 add_bitcast_fusion.3
  390.4 2.6 fusion.45
  397.7 14.0 %conditional.8 = (f32[1024]{0:T(1024)S(1)}, f32[3,1024]{1,0:T(4,128)S(1)}, f32[1,59,128]{2,1,0:T(8,128)S(1)}) conditional(s32[]{:T(128)} %bitcast.440, (f32[1024]{0:T(1024)S(1)}, f32[3,1024]{1,0:T(4,128)S(1)}) %tuple.222, (f32[16,16]{1,0:T(8,128)S(1)}, s32[]{:T(128)}, f32[16,1024]{1,0:T(8,128)S(1)}, f32[16,1024]{1,0:T(8,128)S(1)}, ...), branch_computations={%region_12.12_spmd, %region_13.35_spmd} | conditional | flops 427441280 | bytes 3668628 | solution.py:159
  406.8 2.6 fusion.45
  414.2 14.0 %conditional.8 = (f32[1024]{0:T(1024)S(1)}, f32[3,1024]{1,0:T(4,128)S(1)}, f32[1,59,128]{2,1,0:T(8,128)S(1)}) conditional(s32[]{:T(128)} %bitcast.440, (f32[1024]{0:T(1024)S(1)}, f32[3,1024]{1,0:T(4,128)S(1)}) %tuple.222, (f32[16,16]{1,0:T(8,128)S(1)}, s32[]{:T(128)}, f32[16,1024]{1,0:T(8,128)S(1)}, f32[16,1024]{1,0:T(8,128)S(1)}, ...), branch_computations={%region_12.12_spmd, %region_13.35_spmd} | conditional | flops 427441280 | bytes 3668628 | solution.py:159
  423.3 2.6 fusion.45
  430.7 14.0 %conditional.8 = (f32[1024]{0:T(1024)S(1)}, f32[3,1024]{1,0:T(4,128)S(1)}, f32[1,59,128]{2,1,0:T(8,128)S(1)}) conditional(s32[]{:T(128)} %bitcast.440, (f32[1024]{0:T(1024)S(1)}, f32[3,1024]{1,0:T(4,128)S(1)}) %tuple.222, (f32[16,16]{1,0:T(8,128)S(1)}, s32[]{:T(128)}, f32[16,1024]{1,0:T(8,128)S(1)}, f32[16,1024]{1,0:T(8,128)S(1)}, ...), branch_computations={%region_12.12_spmd, %region_13.35_spmd} | conditional | flops 427441280 | bytes 3668628 | solution.py:159
  439.8 2.6 fusion.45
  447.2 14.0 %conditional.8 = (f32[1024]{0:T(1024)S(1)}, f32[3,1024]{1,0:T(4,128)S(1)}, f32[1,59,128]{2,1,0:T(8,128)S(1)}) conditional(s32[]{:T(128)} %bitcast.440, (f32[1024]{0:T(1024)S(1)}, f32[3,1024]{1,0:T(4,128)S(1)}) %tuple.222, (f32[16,16]{1,0:T(8,128)S(1)}, s32[]{:T(128)}, f32[16,1024]{1,0:T(8,128)S(1)}, f32[16,1024]{1,0:T(8,128)S(1)}, ...), branch_computations={%region_12.12_spmd, %region_13.35_spmd} | conditional | flops 427441280 | bytes 3668628 | solution.py:159
  456.3 2.6 fusion.45
  463.7 14.0 %conditional.8 = (f32[1024]{0:T(1024)S(1)}, f32[3,1024]{1,0:T(4,128)S(1)}, f32[1,59,128]{2,1,0:T(8,128)S(1)}) conditional(s32[]{:T(128)} %bitcast.440, (f32[1024]{0:T(1024)S(1)}, f32[3,1024]{1,0:T(4,128)S(1)}) %tuple.222, (f32[16,16]{1,0:T(8,128)S(1)}, s32[]{:T(128)}, f32[16,1024]{1,0:T(8,128)S(1)}, f32[16,1024]{1,0:T(8,128)S(1)}, ...), branch_computations={%region_12.12_spmd, %region_13.35_spmd} | conditional | flops 427441280 | bytes 3668628 | solution.py:159
  472.8 2.6 fusion.45
  480.2 14.0 %conditional.8 = (f32[1024]{0:T(1024)S(1)}, f32[3,1024]{1,0:T(4,128)S(1)}, f32[1,59,128]{2,1,0:T(8,128)S(1)}) conditional(s32[]{:T(128)} %bitcast.440, (f32[1024]{0:T(1024)S(1)}, f32[3,1024]{1,0:T(4,128)S(1)}) %tuple.222, (f32[16,16]{1,0:T(8,128)S(1)}, s32[]{:T(128)}, f32[16,1024]{1,0:T(8,128)S(1)}, f32[16,1024]{1,0:T(8,128)S(1)}, ...), branch_computations={%region_12.12_spmd, %region_13.35_spmd} | conditional | flops 427441280 | bytes 3668628 | solution.py:159
  489.3 2.6 fusion.45
  496.7 14.0 %conditional.8 = (f32[1024]{0:T(1024)S(1)}, f32[3,1024]{1,0:T(4,128)S(1)}, f32[1,59,128]{2,1,0:T(8,128)S(1)}) conditional(s32[]{:T(128)} %bitcast.440, (f32[1024]{0:T(1024)S(1)}, f32[3,1024]{1,0:T(4,128)S(1)}) %tuple.222, (f32[16,16]{1,0:T(8,128)S(1)}, s32[]{:T(128)}, f32[16,1024]{1,0:T(8,128)S(1)}, f32[16,1024]{1,0:T(8,128)S(1)}, ...), branch_computations={%region_12.12_spmd, %region_13.35_spmd} | conditional | flops 427441280 | bytes 3668628 | solution.py:159
  505.8 2.6 fusion.45
  513.9 3.7 all-to-all-start.1
  517.9 10.5 %all-to-all-done.1 = f32[16,59,128]{2,1,0:T(8,128)S(1)} async-done(((f32[16,59,128]{2,1,0:T(8,128)}), f32[16,59,128]{2,1,0:T(8,128)S(1)}, u32[]{:S(2)}, u32[]{:S(2)}) %all-to-all-start.1) | async-done | bytes 483360 | tf_op jit(solution)/shard_map/all_to_all | solution.py:207
  532.2 3.0 collective-permute-start.1
  (2052 shorter events, 334.5 us)
Async XLA Ops:
  0.6 57.6 %copy-start = (f32[16,16]{1,0:T(8,128)S(1)}, f32[16,16]{1,0:T(8,128)}, u32[]{:S(2)}) copy-start(f32[16,16]{1,0:T(8,128)} %param.23) | copy-start | bytes 3076
  0.6 0.7 copy-start.8
  0.7 10.5 %copy-start.3 = (f32[1,2,59,128]{3,1,2,0:T(2,128)S(1)}, f32[1,2,59,128]{3,1,2,0:T(2,128)}, u32[]{:S(2)}) copy-start(f32[1,2,59,128]{3,1,2,0:T(2,128)} %param.19) | copy-start | bytes 181252
  2.1 511.8 %all-to-all-start = ((f32[16,1,1]{2,1,0:T(1,128)}), f32[16,1,1]{2,1,0:T(1,128)S(1)}, u32[]{:S(2)}, u32[]{:S(2)}) async-start(f32[16,1,1]{2,1,0:T(1,128)} %bitcast.113), calls=%async_computation | async-start | bytes 16384 | tf_op jit(solution)/shard_map/all_to_all | solution.py:208
  58.9 0.7 copy-start.9
  59.5 189.1 %copy-start.5 = (f32[1,1,3,1024]{3,1,2,0:T(1,128)S(1)}, f32[1,1,3,1024]{3,1,2,0:T(1,128)}, u32[]{:S(2)}) copy-start(f32[1,1,3,1024]{3,1,2,0:T(1,128)} %param.28) | copy-start | bytes 36868
  512.9 15.4 %copy-start.1 = (f32[1,2,59,128]{3,1,2,0:T(2,128)S(1)}, f32[1,2,59,128]{3,1,2,0:T(2,128)}, u32[]{:S(2)}) copy-start(f32[1,2,59,128]{3,1,2,0:T(2,128)} %param.21) | copy-start | bytes 181252
  513.0 15.4 %copy-start.4 = (f32[1,2,59,128]{3,1,2,0:T(2,128)S(1)}, f32[1,2,59,128]{3,1,2,0:T(2,128)}, u32[]{:S(2)}) copy-start(f32[1,2,59,128]{3,1,2,0:T(2,128)} %param.20) | copy-start | bytes 181252
  513.9 3.7 copy-start.6
  513.9 14.4 %all-to-all-start.1 = ((f32[16,59,128]{2,1,0:T(8,128)}), f32[16,59,128]{2,1,0:T(8,128)S(1)}, u32[]{:S(2)}, u32[]{:S(2)}) async-start(f32[16,59,128]{2,1,0:T(8,128)} %copy.67), calls=%async_computation.1 | async-start | bytes 1048576 | tf_op jit(solution)/shard_map/all_to_all | solution.py:207
  517.7 10.7 %copy-start.7 = (f32[59]{0:T(128)S(1)}, f32[59]{0:T(128)}, u32[]{:S(2)}) copy-start(f32[59]{0:T(128)} %param.22) | copy-start | bytes 712
  529.0 0.6 copy-start.2
  530.3 5.0 collective-permute-start
  532.2 3.9 collective-permute-start.1
where the time goes:
time: 541 us; the launch traced here: 538 us
  other arithmetic  159 us (29%)
  matrix products  133 us (25%)
  local copies, waits for them, and re-layouts  100 us (18%)
  loops' own time  70.3 us (13%)
  blocking collectives  46.8 us (9%)
  starting transfers between devices  16.3 us (3%)
  waiting for transfers between devices  10.5 us (2%)
    dot_general x48, matrix products, blend_block(): before = jnp.dot(logs_kept, strict, precision=highest)  75.2 us
    sub x32, other arithmetic, blend_block(): delta_y = pixel_y[:, None] - screen_y[None, :]  59.6 us
    another operation x2, loops' own time, strip_loss(): final_pair, unused = lax.scan(advance, initial, depth_steps)  53 us
    all_gather x1, blocking collectives, on_device(): everything = lax.all_gather(own_blocks, 'tile', axis=0, tiled=True)  46.8 us
    sub x32, other arithmetic, blend_block(): delta_x = pixel_x[:, None] - screen_x[None, :]  38.8 us
    dot_general x48, matrix products, blend_block(): jnp.einsum('cg,pg->cp', colour, weight, precision=highest)  36.4 us
    dynamic_slice x80, local copies, waits for them, and re-layouts, strip_loss(): final_pair, unused = lax.scan(advance, initial, depth_steps)  28.8 us
    slice x32, local copies, waits for them, and re-layouts, gauss_features(): camera[15]  23 us
  transfers between devices with their start and end apart: 4, of which 1 were waited for; matrix products, arithmetic and copies ran while one was open for 72% of the time, Pallas kernels for 0%

commit v1 on v0

v1 whole, which is shorter than its diff:
```python
import functools

import jax
import jax.numpy as jnp
import numpy as np
from jax import lax
from jax.experimental import pallas as pl
from jax.experimental.pallas import tpu as pltpu
from jax.sharding import PartitionSpec as P

penalty_weight = 0.5
blur_floor = 0.3
alpha_ceiling = 0.99
log2e = 1.4426950408889634
sh_zero = 0.28209479177387814
sh_one = 0.4886025119029199
sh_two = (
    1.0925484305920792,
    -1.0925484305920792,
    0.31539156525252005,
    -1.0925484305920792,
    0.5462742152960396,
)
sh_three = (
    -0.5900435899266435,
    2.890611442640554,
    -0.4570457994644658,
    0.3731763325901154,
    -0.4570457994644658,
    1.445305721320277,
    -0.5900435899266435,
)

LANES = 128
SUB = 8
ROWS = 64
KDIM = 32
SEGS = 8
MOMENTS = 6
MSG = 16
highest = lax.Precision.HIGHEST


def harmonic_basis(x, y, z):
    xx, yy, zz = x * x, y * y, z * z
    return [
        sh_zero + 0.0 * x,
        -sh_one * y,
        sh_one * z,
        -sh_one * x,
        sh_two[0] * x * y,
        sh_two[1] * y * z,
        sh_two[2] * (2.0 * zz - xx - yy),
        sh_two[3] * x * z,
        sh_two[4] * (xx - yy),
        sh_three[0] * y * (3.0 * xx - yy),
        sh_three[1] * x * y * z,
        sh_three[2] * y * (4.0 * zz - xx - yy),
        sh_three[3] * z * (2.0 * zz - 3.0 * xx - 3.0 * yy),
        sh_three[4] * x * (4.0 * zz - xx - yy),
        sh_three[5] * z * (xx - yy),
        sh_three[6] * x * (xx - 3.0 * yy),
    ]


def geometry(row, cam):
    mean = [row(0), row(1), row(2)]
    rot = [[cam[3 * i + j] for j in range(3)] for i in range(3)]
    shift = [cam[9 + i] for i in range(3)]
    focal_x, focal_y = cam[12], cam[13]
    view = [
        rot[i][0] * mean[0] + rot[i][1] * mean[1] + rot[i][2] * mean[2] + shift[i] for i in range(3)
    ]
    inverse = 1.0 / view[2]
    u = view[0] * inverse
    v = view[1] * inverse
    quat = [row(6 + i) for i in range(4)]
    norm = lax.rsqrt(sum(q * q for q in quat))
    w, x, y, z = [q * norm for q in quat]
    turn = [
        [1.0 - 2.0 * (y * y + z * z), 2.0 * (x * y - w * z), 2.0 * (x * z + w * y)],
        [2.0 * (x * y + w * z), 1.0 - 2.0 * (x * x + z * z), 2.0 * (y * z - w * x)],
        [2.0 * (x * z - w * y), 2.0 * (y * z + w * x), 1.0 - 2.0 * (x * x + y * y)],
    ]
    scales = [jnp.exp(row(3 + k)) for k in range(3)]
    spread = [[turn[j][k] * scales[k] for k in range(3)] for j in range(3)]
    axes = [
        [sum(rot[i][j] * spread[j][k] for j in range(3)) for k in range(3)] for i in range(3)
    ]
    scale_x = focal_x * inverse
    scale_y = focal_y * inverse
    lean_x = [axes[0][k] - u * axes[2][k] for k in range(3)]
    lean_y = [axes[1][k] - v * axes[2][k] for k in range(3)]
    row_one = [scale_x * lean_x[k] for k in range(3)]
    row_two = [scale_y * lean_y[k] for k in range(3)]
    cov_xx = sum(a * a for a in row_one) + blur_floor
    cov_xy = sum(a * b for a, b in zip(row_one, row_two))
    cov_yy = sum(b * b for b in row_two) + blur_floor
    scale = 1.0 / (cov_xx * cov_yy - cov_xy * cov_xy)
    conic = (cov_yy * scale, -cov_xy * scale, cov_xx * scale)
    eye = [-(rot[0][i] * shift[0] + rot[1][i] * shift[1] + rot[2][i] * shift[2]) for i in range(3)]
    away = [mean[i] - eye[i] for i in range(3)]
    shrink = lax.rsqrt(sum(a * a for a in away))
    toward = [a * shrink for a in away]
    return dict(
        rot=rot,
        view=view,
        inverse=inverse,
        u=u,
        v=v,
        norm=norm,
        unit=(w, x, y, z),
        scales=scales,
        spread=spread,
        axes=axes,
        scale_x=scale_x,
        scale_y=scale_y,
        lean_x=lean_x,
        lean_y=lean_y,
        row_one=row_one,
        row_two=row_two,
        conic=conic,
        shrink=shrink,
        toward=toward,
    )


def three_parts(value):
    high = value.astype(jnp.bfloat16).astype(jnp.float32)
    rest = value - high
    mid = rest.astype(jnp.bfloat16).astype(jnp.float32)
    return high, mid, rest - mid


def sub_roll(value, shift):
    return pltpu.roll(value, shift % SUB, 0)


def render_kernel(
    pixels, hop_bits, me_ref, cam_id_ref, count_ref, list_ref, depth_ref, cameras_ref,
    blocks_ref, target_ref, basis_ref, xmom_ref, order_ref, back_ref, out_ref,
    raw, feat, coef, expo, shade, alphas, weights, carry, before, passed, colours,
    resid, behind, sums, found, rows, slots,
):
    listed = list_ref.shape[0]
    peers = out_ref.shape[0]
    per_owner = blocks_ref.shape[0] // peers
    yrows = pixels // LANES
    groups = LANES // SUB
    me = me_ref[0]
    count = count_ref[0]
    cam_id = cam_id_ref[0]
    cam = [cameras_ref[cam_id, k] for k in range(16)]
    top = ((me % 4) * yrows).astype(jnp.float32)

    def place_slot(j, ends):
        live_end, dead_end = ends
        slot = depth_ref[j]
        live = slot < count
        slots[jnp.where(live, live_end, dead_end)] = slot
        return jnp.where(live, live_end + 1, live_end), jnp.where(live, dead_end, dead_end + 1)

    lax.fori_loop(0, listed, place_slot, (jnp.int32(0), count))

    def fetch(k, _):
        block = list_ref[slots[k]]
        owner = block // per_owner
        if hop_bits is None:
            near = owner
        else:
            apart = me ^ owner
            near = sum((((apart >> bit) & 1) << t) for t, bit in enumerate(hop_bits))
        source = near * per_owner + block % per_owner
        raw[pl.ds(pl.multiple_of(k * ROWS, ROWS), blocks_ref.shape[1]), :] = blocks_ref[source]
        return 0

    lax.fori_loop(0, listed, fetch, 0)

    def row(p):
        return raw[pl.ds(p, listed, stride=ROWS), :]

    geo = geometry(row, cam)
    screen_x = cam[12] * geo["u"] + cam[14]
    screen_y = cam[13] * geo["v"] + cam[15]
    basis = harmonic_basis(*geo["toward"])
    tint = [sum(basis[k] * row(11 + 3 * k + c) for k in range(16)) + 0.5 for c in range(3)]
    log_opacity = -jnp.log(1.0 + jnp.exp(-row(10))) * log2e
    natural = [screen_x - 64.0, screen_y - (top + 4.0), *geo["conic"], log_opacity, *tint]
    for m, value in enumerate(natural):
        feat[m * listed : (m + 1) * listed, :] = value
    feat[...] = jnp.dot(feat[...], order_ref[...], precision=highest)
    sx, sy, ca, cb, cc, lo, *tint = [feat[m * listed : (m + 1) * listed, :] for m in range(9)]
    kxx = (-0.5 * log2e) * ca
    kxy = -log2e * cb
    kyy = (-0.5 * log2e) * cc
    kx = -2.0 * kxx * sx - kxy * sy
    ky = -2.0 * kyy * sy - kxy * sx
    k1 = kxx * sx * sx + kxy * sx * sy + kyy * sy * sy + lo
    for c, value in enumerate([kxx, kxx, kxy, kyy, kx, ky, k1, *tint]):
        for part, piece in enumerate(three_parts(value)):
            coef[pl.ds(part * 10 + c, listed, stride=KDIM), :] = piece
    zero = jnp.zeros((listed, LANES), jnp.float32)
    for c in range(30, KDIM):
        coef[pl.ds(c, listed, stride=KDIM), :] = zero

    sub = lax.broadcasted_iota(jnp.int32, (SUB, LANES), 0)
    one = jnp.ones((SUB, LANES), jnp.float32)
    none = jnp.zeros((SUB, LANES), jnp.float32)
    for y in range(yrows):
        carry[y] = one
    for c in range(3):
        for y in range(yrows):
            resid[c, y] = none

    def spread_row(value, index):
        return jnp.broadcast_to(value[index : index + 1, :], (SUB, LANES))

    def forward(k, _):
        mine = coef[pl.ds(pl.multiple_of(k * KDIM, KDIM), KDIM), :].astype(jnp.bfloat16)
        expo[...] = lax.dot_general(
            mine, basis_ref[...], (((0,), (0,)), ((), ())), preferred_element_type=jnp.float32
        )
        base = pl.multiple_of(k * LANES, LANES)
        shade[pl.ds(base, LANES), :] = expo[:, pixels:]
        kept = [one] * yrows
        total = [[none] * yrows for _ in range(3)]
        for i in range(groups):
            here = pl.ds(pl.multiple_of(base + i * SUB, SUB), SUB)
            tints = [
                expo[i * SUB : (i + 1) * SUB, pixels + c * LANES : pixels + (c + 1) * LANES]
                for c in range(3)
            ]
            for y in range(yrows):
                lanes = slice(y * LANES, (y + 1) * LANES)
                alpha = jnp.minimum(
                    alpha_ceiling, jnp.exp2(expo[i * SUB : (i + 1) * SUB, lanes])
                )
                weight = alpha * kept[y]
                alphas[here, lanes] = alpha
                weights[here, lanes] = weight
                kept[y] = kept[y] - weight
                for c in range(3):
                    total[c][y] = total[c][y] + weight * tints[c]
        for y in range(yrows):
            passed[k, y] = kept[y]
            through = kept[y]
            for step in (1, 2, 4):
                through = through * jnp.where(sub >= step, sub_roll(through, step), 1.0)
            entering = carry[y]
            ahead = entering * jnp.where(sub >= 1, sub_roll(through, 1), 1.0)
            before[k, y] = ahead
            carry[y] = entering * spread_row(through, SUB - 1)
            for c in range(3):
                colours[k, c, y] = total[c][y]
                resid[c, y] = resid[c, y] + ahead * total[c][y]
        return 0

    lax.fori_loop(0, count, forward, 0)

    for y in range(yrows):
        for c in range(3):
            value = jnp.sum(resid[c, y], axis=0, keepdims=True)
            value = value - target_ref[c : c + 1, y * LANES : (y + 1) * LANES]
            resid[c, y] = jnp.broadcast_to(value, (SUB, LANES))
        behind[y] = none

    def backward(back, _):
        k = count - 1 - back
        base = pl.multiple_of(k * LANES, LANES)
        pull = [[None] * yrows for _ in range(3)]
        rear = [None] * yrows
        for y in range(yrows):
            res = [resid[c, y] for c in range(3)]
            gain = passed[k, y]
            value = sum(colours[k, c, y] * res[c] for c in range(3))
            for step in (1, 2, 4):
                inside = sub < SUB - step
                value = value + gain * jnp.where(inside, sub_roll(value, -step), 0.0)
                gain = gain * jnp.where(inside, sub_roll(gain, -step), 1.0)
            last = behind[y]
            ahead = before[k, y]
            at_end = jnp.where(
                sub < SUB - 1, sub_roll(value, -1) + sub_roll(gain, -1) * last, last
            )
            behind[y] = spread_row(value + gain * last, 0)
            rear[y] = ahead * at_end
            for c in range(3):
                pull[c][y] = ahead * res[c]
        for i in reversed(range(groups)):
            here = pl.ds(pl.multiple_of(base + i * SUB, SUB), SUB)
            tints = [shade[here, c * LANES : (c + 1) * LANES] for c in range(3)]
            run = [none, none, none]
            drawn = [none, none, none]
            for y in range(yrows):
                lanes = slice(y * LANES, (y + 1) * LANES)
                alpha = alphas[here, lanes]
                weight = weights[here, lanes]
                gap = (
                    tints[0] * pull[0][y] + tints[1] * pull[1][y] + tints[2] * pull[2][y] - rear[y]
                )
                slope = jnp.where(alpha < alpha_ceiling, weight * gap, 0.0)
                rear[y] = rear[y] + alpha * gap
                run[0] = run[0] + slope
                run[1] = run[1] + run[0]
                run[2] = run[2] + run[1]
                for c in range(3):
                    drawn[c] = drawn[c] + weight * pull[c][y]
            for m, value in enumerate(run + drawn):
                sums[m * LANES + i * SUB : m * LANES + (i + 1) * SUB, :] = value
        value = sums[...]
        high = value.astype(jnp.bfloat16)
        low = (value - high.astype(jnp.float32)).astype(jnp.bfloat16)
        contract = (((1,), (1,)), ((), ()))
        xmom = xmom_ref[...]
        found[k] = lax.dot_general(
            xmom, high, contract, preferred_element_type=jnp.float32
        ) + lax.dot_general(xmom, low, contract, preferred_element_type=jnp.float32)
        return 0

    lax.fori_loop(0, count, backward, 0)

    lane = lax.broadcasted_iota(jnp.int32, (1, LANES), 1)
    middle = (
        lax.broadcasted_iota(jnp.int32, (SUB, LANES), 0) * (LANES // SEGS) + (LANES // SEGS // 2 - 64)
    ).astype(jnp.float32)
    meta = jnp.zeros((1, LANES), jnp.float32)
    for c in range(16):
        meta = jnp.where(lane == c, cam[c], meta)

    rows[...] = jnp.zeros(rows.shape, jnp.float32)

    def gather_moments(k, _):
        part = lambda order, m: found[k, order * SEGS : (order + 1) * SEGS, m * LANES : (m + 1) * LANES]
        add = lambda value: jnp.sum(value, axis=0, keepdims=True)
        off = middle - feat[pl.ds(k, 1), :]
        rise = (yrows - 4.0) - feat[pl.ds(listed + k, 1), :]
        h0, h1, h2 = part(0, 0), part(1, 0), part(2, 0)
        n0, n1 = part(0, 1), part(1, 1)
        s0 = add(h0)
        sx1 = add(h1 + off * h0)
        sxx = add(h2 + off * (2.0 * h1 + off * h0))
        t1 = add(n0)
        tx = add(n1 + off * n0)
        t2 = 2.0 * add(part(0, 2)) - t1
        sy1 = rise * s0 - t1
        sxy = rise * sx1 - tx
        syy = rise * (rise * s0 - 2.0 * t1) + t2
        answer = [s0, sx1, sy1, sxx, sxy, syy] + [add(part(0, 3 + c)) for c in range(3)]
        for m, value in enumerate(answer):
            rows[pl.ds(k * MSG + m, 1), :] = value
        return 0

    lax.fori_loop(0, count, gather_moments, 0)
    rows[...] = jnp.dot(rows[...], back_ref[...], precision=highest)

    if peers > listed:
        absent = jnp.where(lane == 16, -1.0, 0.0)
        for peer in range(peers):
            out_ref[peer] = jnp.broadcast_to(absent, (MSG, LANES))

    def send(k, _):
        block = list_ref[slots[k]]
        owner = block // per_owner
        place = (block % per_owner).astype(jnp.float32)
        rows[pl.ds(k * MSG + 9, 1), :] = jnp.where(lane == 16, place, meta)
        out_ref[owner] = rows[pl.ds(pl.multiple_of(k * MSG, MSG), MSG), :]
        return 0

    lax.fori_loop(0, listed, send, 0)


def owner_kernel(inbox_ref, own_ref, cons_ref, dual_ref, step_ref, share_ref, new_ref, vals_ref, grad):
    blocks = own_ref.shape[0]
    params = own_ref.shape[1]
    strips = inbox_ref.shape[0] // MSG

    def message(m):
        return inbox_ref[pl.ds(m, strips, stride=MSG), :]

    meta = message(9)
    cam = [jnp.broadcast_to(meta[:, k : k + 1], (strips, LANES)) for k in range(17)]
    place = cam[16]

    def row(p):
        value = jnp.broadcast_to(own_ref[0, p : p + 1, :], (strips, LANES))
        for b in range(1, blocks):
            value = jnp.where(place == b, own_ref[b, p : p + 1, :], value)
        return value

    geo = geometry(row, cam)
    s0, sx, sy, sxx, sxy, syy, *drawn = [message(m) for m in range(9)]
    ca, cb, cc = geo["conic"]
    u, v, inverse = geo["u"], geo["v"], geo["inverse"]
    axes, rot = geo["axes"], geo["rot"]
    focal_x, focal_y = cam[12], cam[13]
    grads = {}
    opacity = 1.0 / (1.0 + jnp.exp(-row(10)))
    grads[10] = s0 * (1.0 - opacity)
    t00, t01 = sxx * ca + sxy * cb, sxx * cb + sxy * cc
    t10, t11 = sxy * ca + syy * cb, sxy * cb + syy * cc
    g_xx = 0.5 * (ca * t00 + cb * t10)
    g_xy = ca * t01 + cb * t11
    g_yy = 0.5 * (cb * t01 + cc * t11)
    one, two = geo["row_one"], geo["row_two"]
    g_one = [2.0 * g_xx * one[k] + g_xy * two[k] for k in range(3)]
    g_two = [2.0 * g_yy * two[k] + g_xy * one[k] for k in range(3)]
    px, py = geo["scale_x"], geo["scale_y"]
    g_axes = [
        [px * g_one[k] for k in range(3)],
        [py * g_two[k] for k in range(3)],
        [-(px * u * g_one[k] + py * v * g_two[k]) for k in range(3)],
    ]
    g_px = sum(g_one[k] * geo["lean_x"][k] for k in range(3))
    g_py = sum(g_two[k] * geo["lean_y"][k] for k in range(3))
    g_u = focal_x * (ca * sx + cb * sy) - px * sum(g_one[k] * axes[2][k] for k in range(3))
    g_v = focal_y * (cc * sy + cb * sx) - py * sum(g_two[k] * axes[2][k] for k in range(3))
    view = geo["view"]
    g_inverse = focal_x * g_px + focal_y * g_py + view[0] * g_u + view[1] * g_v
    g_view = [inverse * g_u, inverse * g_v, -inverse * inverse * g_inverse]
    g_spread = [
        [sum(rot[i][j] * g_axes[i][k] for i in range(3)) for k in range(3)] for j in range(3)
    ]
    for k in range(3):
        grads[3 + k] = sum(g_spread[j][k] * geo["spread"][j][k] for j in range(3))
    g = [[g_spread[j][k] * geo["scales"][k] for k in range(3)] for j in range(3)]
    w, x, y, z = geo["unit"]
    g_w = 2.0 * (z * (g[1][0] - g[0][1]) + y * (g[0][2] - g[2][0]) + x * (g[2][1] - g[1][2]))
    g_x = 2.0 * (
        y * (g[0][1] + g[1][0])
        + z * (g[0][2] + g[2][0])
        + w * (g[2][1] - g[1][2])
        - 2.0 * x * (g[1][1] + g[2][2])
    )
    g_y = 2.0 * (
        x * (g[0][1] + g[1][0])
        + z * (g[1][2] + g[2][1])
        + w * (g[0][2] - g[2][0])
        - 2.0 * y * (g[0][0] + g[2][2])
    )
    g_z = 2.0 * (
        x * (g[0][2] + g[2][0])
        + y * (g[1][2] + g[2][1])
        + w * (g[1][0] - g[0][1])
        - 2.0 * z * (g[0][0] + g[1][1])
    )
    along = w * g_w + x * g_x + y * g_y + z * g_z
    for p, (g_q, q) in enumerate(((g_w, w), (g_x, x), (g_y, y), (g_z, z))):
        grads[6 + p] = (g_q - q * along) * geo["norm"]
    x, y, z = geo["toward"]
    basis = harmonic_basis(x, y, z)
    h = [None]
    for k in range(16):
        if k:
            h.append(sum(drawn[c] * row(11 + 3 * k + c) for c in range(3)))
        for c in range(3):
            grads[11 + 3 * k + c] = basis[k] * drawn[c]
    a, d = sh_two, sh_three
    xx, yy, zz, xy, yz, xz = x * x, y * y, z * z, x * y, y * z, x * z
    g_dx = (
        -sh_one * h[3] + a[0] * y * h[4] - 2.0 * a[2] * x * h[6] + a[3] * z * h[7]
        + 2.0 * a[4] * x * h[8] + 6.0 * d[0] * xy * h[9] + d[1] * yz * h[10]
        - 2.0 * d[2] * xy * h[11] - 6.0 * d[3] * xz * h[12]
        + d[4] * (4.0 * zz - 3.0 * xx - yy) * h[13] + 2.0 * d[5] * xz * h[14]
        + 3.0 * d[6] * (xx - yy) * h[15]
    )
    g_dy = (
        -sh_one * h[1] + a[0] * x * h[4] + a[1] * z * h[5] - 2.0 * a[2] * y * h[6]
        - 2.0 * a[4] * y * h[8] + 3.0 * d[0] * (xx - yy) * h[9] + d[1] * xz * h[10]
        + d[2] * (4.0 * zz - xx - 3.0 * yy) * h[11] - 6.0 * d[3] * yz * h[12]
        - 2.0 * d[4] * xy * h[13] - 2.0 * d[5] * yz * h[14] - 6.0 * d[6] * xy * h[15]
    )
    g_dz = (
        sh_one * h[2] + a[1] * y * h[5] + 4.0 * a[2] * z * h[6] + a[3] * x * h[7]
        + d[1] * xy * h[10] + 8.0 * d[2] * yz * h[11]
        + 3.0 * d[3] * (2.0 * zz - xx - yy) * h[12] + 8.0 * d[4] * xz * h[13]
        + d[5] * (xx - yy) * h[14]
    )
    along = x * g_dx + y * g_dy + z * g_dz
    turned = [(gd - t * along) * geo["shrink"] for gd, t in ((g_dx, x), (g_dy, y), (g_dz, z))]
    for j in range(3):
        grads[j] = sum(rot[i][j] * g_view[i] for i in range(3)) + turned[j]
    for b in range(blocks):
        mine = place == b
        for p in range(params):
            grad[b, p : p + 1, :] = jnp.sum(
                jnp.where(mine, grads[p], 0.0), axis=0, keepdims=True
            )

    shape = (params, params)
    diagonal = lax.broadcasted_iota(jnp.int32, shape, 0) == lax.broadcasted_iota(jnp.int32, shape, 1)
    steps = jnp.sum(
        jnp.where(diagonal, jnp.broadcast_to(step_ref[...], shape), 0.0), axis=1, keepdims=True
    )
    half = share_ref.shape[1]
    local = lax.broadcasted_iota(jnp.int32, (LANES, half), 0)
    vals = [jnp.zeros((params, half), jnp.float32) for _ in range(2)]
    for b in range(blocks):
        here = own_ref[b]
        dual = dual_ref[b]
        new = here - steps * (
            grad[b, :params, :] + penalty_weight * (here - cons_ref[b] + dual)
        )
        new_ref[b] = new
        shifted = new + dual
        for side in range(2):
            pick = (share_ref[side : side + 1, :] == local + b * LANES).astype(jnp.float32)
            vals[side] = vals[side] + jnp.dot(shifted, pick, precision=highest)
    for side in range(2):
        vals_ref[side] = vals[side]


def agree_kernel(last_group, group_ref, vals_ref, above_ref, below_ref, share_ref, out_ref):
    group = group_ref[0]
    half = share_ref.shape[1]
    blocks, params = out_ref.shape[0], out_ref.shape[1]
    changes = []
    for side, other, shared in ((0, above_ref, group < last_group), (1, below_ref, group > 0)):
        mine = vals_ref[side]
        change = mine - 0.5 * (mine + other[1 - side])
        changes.append(jnp.where(shared, change, 0.0))
    local = lax.broadcasted_iota(jnp.int32, (LANES, half), 0)
    for b in range(blocks):
        total = jnp.zeros((params, LANES), jnp.float32)
        for side in range(2):
            pick = (share_ref[side : side + 1, :] == local + b * LANES).astype(jnp.float32)
            total = total + lax.dot_general(
                changes[side], pick, (((1,), (1,)), ((), ())), precision=highest,
                preferred_element_type=jnp.float32,
            )
        out_ref[b] = total


def constants(pixels):
    place = np.arange(pixels)
    x = (place % LANES - 64).astype(np.float32)
    y = (place // LANES - 4).astype(np.float32)
    square = (x * x).astype(jnp.bfloat16).astype(np.float32)
    some = np.ones_like(x)
    part = np.zeros((10, pixels + 3 * LANES), np.float32)
    for c, value in enumerate([square, x * x - square, x * y, y * y, x, y, some]):
        part[c, :pixels] = value
    for c in range(3):
        part[7 + c, pixels + c * LANES : pixels + (c + 1) * LANES] = 1.0
    basis = np.zeros((KDIM, pixels + 3 * LANES), np.float32)
    basis[:30] = np.concatenate([part] * 3)
    lane = np.arange(LANES)
    wide = LANES // SEGS
    xmom = np.zeros((3 * SEGS + SEGS, LANES), np.float32)
    for s in range(SEGS):
        near = (lane // wide == s).astype(np.float32)
        offset = lane - s * wide - wide // 2
        for power in range(3):
            xmom[power * SEGS + s] = near * offset**power
    order = np.zeros((LANES, LANES), np.float32)
    groups = LANES // SUB
    for r in range(LANES):
        order[(r % SUB) * groups + r // SUB, r] = 1.0
    return (
        jnp.asarray(basis, jnp.bfloat16),
        jnp.asarray(xmom, jnp.bfloat16),
        jnp.asarray(order),
        jnp.asarray(order.T.copy()),
    )


def vmem():
    return pl.BlockSpec(memory_space=pltpu.VMEM)


def smem():
    return pl.BlockSpec(memory_space=pltpu.SMEM)


def on_device(
    gaussians, consensus, duals, step_sizes, cameras, camera_ids, block_lists, depth_order,
    block_counts, targets, intersection,
):
    own = gaussians[0]
    blocks, params = own.shape[0], own.shape[1]
    peers = lax.axis_size("tile")
    me = lax.axis_index("tile")
    listed = block_lists.shape[2]
    pixels = targets.shape[3]
    yrows = pixels // LANES
    f32 = jnp.float32

    everything = own
    hop_bits = None
    if peers & (peers - 1) == 0:
        hop_bits = list(reversed(range(peers.bit_length() - 1)))
        for bit in hop_bits:
            arrived = lax.ppermute(
                everything, "tile", [(i, i ^ (1 << bit)) for i in range(peers)]
            )
            everything = jnp.concatenate([everything, arrived], 0)
    else:
        everything = lax.all_gather(own, "tile", axis=0, tiled=True)

    basis, xmom, order, back = constants(pixels)
    outbox = pl.pallas_call(
        functools.partial(render_kernel, pixels, hop_bits),
        out_shape=jax.ShapeDtypeStruct((peers, MSG, LANES), f32),
        in_specs=[smem()] * 6 + [vmem()] * 6,
        out_specs=vmem(),
        scratch_shapes=[
            pltpu.VMEM((listed * ROWS, LANES), f32),
            pltpu.VMEM((9 * listed, LANES), f32),
            pltpu.VMEM((listed * KDIM, LANES), f32),
            pltpu.VMEM((LANES, pixels + 3 * LANES), f32),
            pltpu.VMEM((listed * LANES, 3 * LANES), f32),
            pltpu.VMEM((listed * LANES, pixels), f32),
            pltpu.VMEM((listed * LANES, pixels), f32),
            pltpu.VMEM((yrows, SUB, LANES), f32),
            pltpu.VMEM((listed, yrows, SUB, LANES), f32),
            pltpu.VMEM((listed, yrows, SUB, LANES), f32),
            pltpu.VMEM((listed, 3, yrows, SUB, LANES), f32),
            pltpu.VMEM((3, yrows, SUB, LANES), f32),
            pltpu.VMEM((yrows, SUB, LANES), f32),
            pltpu.VMEM((MOMENTS * LANES, LANES), f32),
            pltpu.VMEM((listed, 4 * SEGS, MOMENTS * LANES), f32),
            pltpu.VMEM((listed * MSG, LANES), f32),
            pltpu.SMEM((listed,), jnp.int32),
        ],
        compiler_params=pltpu.CompilerParams(vmem_limit_bytes=48 * 2**20),
        name="render",
    )(
        me[None], camera_ids[0], block_counts[0], block_lists[0, 0], depth_order[0, 0], cameras,
        everything, targets[0, 0], basis, xmom, order, back,
    )
    inbox = lax.all_to_all(outbox, "tile", split_axis=0, concat_axis=0, tiled=True)
    share = intersection[0, 0]
    half = share.shape[1]
    updated, vals = pl.pallas_call(
        owner_kernel,
        out_shape=(
            jax.ShapeDtypeStruct(own.shape, f32),
            jax.ShapeDtypeStruct((2, params, half), f32),
        ),
        in_specs=[vmem()] * 6,
        out_specs=(vmem(), vmem()),
        scratch_shapes=[pltpu.VMEM((blocks, ROWS, LANES), f32)],
        compiler_params=pltpu.CompilerParams(vmem_limit_bytes=32 * 2**20),
        name="owner",
    )(inbox.reshape(peers * MSG, LANES), own, consensus[0], duals[0], step_sizes[None, :], share)
    group_total = lax.axis_size("scene")
    group = lax.axis_index("scene")
    if group_total == 2:
        above = below = lax.ppermute(vals, "scene", [(0, 1), (1, 0)])
    else:
        above = lax.ppermute(vals, "scene", [(g + 1, g) for g in range(group_total - 1)])
        below = lax.ppermute(vals, "scene", [(g, g + 1) for g in range(group_total - 1)])
    new_duals = pl.pallas_call(
        functools.partial(agree_kernel, group_total - 1),
        out_shape=jax.ShapeDtypeStruct(own.shape, f32),
        in_specs=[smem()] + [vmem()] * 4,
        out_specs=vmem(),
        name="agree",
    )(group[None], vals, above, below, share)
    return updated[None], new_duals[None]


def solution(mesh):
    placed = (
        P("scene", "tile", None, None),
        P("scene", "tile", None, None),
        P("scene", "tile", None, None),
        P(),
        P(),
        P("scene", "tile"),
        P("scene", "tile", None),
        P("scene", "tile", None),
        P("scene", "tile"),
        P("scene", "tile", None, None),
        P("scene", "tile", None, None),
    )
    return jax.shard_map(
        on_device,
        mesh=mesh,
        in_specs=placed,
        out_specs=(P("scene", "tile", None, None), P("scene", "tile", None, None)),
        check_vma=False,
    )
```

time: 541 us -> 76.2 us (0.14)
  other arithmetic: 159 us -> 0.06 us
  matrix products: 133 us -> 0 us
  local copies, waits for them, and re-layouts: 100 us -> 5.11 us
  loops' own time: 70.3 us -> 0 us
  blocking collectives: 46.8 us -> 0 us
  waiting for transfers between devices: 10.5 us -> 27.7 us
  Pallas kernels: 0 us -> 12.4 us
  starting transfers between devices: 16.3 us -> 28.3 us
    dot_general x227 -> x0, matrix products: 133 us -> none  [the longest x48 75.2 us: blend_block(): before = jnp.dot(logs_kept, strict, precision=highest)]
    sub x97 -> x0, other arithmetic: 98.7 us -> none  [the longest x32 59.6 us: blend_block(): delta_y = pixel_y[:, None] - screen_y[None, :]]
    another operation x34 -> x0, loops' own time: 70.3 us -> none  [the longest x2 53 us: strip_loss(): final_pair, unused = lax.scan(advance, initial, depth_steps)]
    all_gather x1 -> x0, blocking collectives: 46.8 us -> none  [on_device(): everything = lax.all_gather(own_blocks, 'tile', axis=0, tiled=True)]
    dynamic_slice x96 -> x0, local copies, waits for them, and re-layouts: 29 us -> none  [the longest x80 28.8 us: strip_loss(): final_pair, unused = lax.scan(advance, initial, depth_steps)]
    slice x128 -> x0, local copies, waits for them, and re-layouts: 26.1 us -> none  [the longest x32 23 us: gauss_features(): camera[15]]
    reduce_sum x208 -> x0, other arithmetic: 25.6 us -> none  [the longest x32 18.9 us: blend_block(): transmit = transmit * jnp.exp(jnp.sum(logs_kept, 1))]
    mul x320 -> x0, other arithmetic: 24 us -> none  [the longest x32 20.1 us: gauss_features(): focal_y * viewed[1] * inverse * inverse * world_axes[2]]
  transfers between devices with their start and end apart: 4 -> 6, of which waited for: 1 -> 6; matrix products, arithmetic and copies ran while one was open for 72% -> 1% of each run, Pallas kernels for 0% -> 0%
where the time goes in v1:
time: 76.2 us; the launch traced here: 75.8 us
  starting transfers between devices  28.3 us (37%)
  waiting for transfers between devices  27.7 us (36%)
  Pallas kernels  12.4 us (16%)
  local copies, waits for them, and re-layouts  5.11 us (7%)
  between operations  2.14 us (3%)
    all_to_all x1, starting transfers between devices, on_device(): lax.all_to_all(outbox, 'tile', split_axis=0, concat_axis=0, tiled=True)  20 us
    ppermute x4, waiting for transfers between devices, on_device(): lax.ppermute(everything, 'tile', [(i, i ^ 1 << bit) for i in range(peers)])  19.4 us
    pallas_call x1, Pallas kernels, on_device(): pl.pallas_call(functools.partial(render_kernel, pixels, hop_bits), out_sh...  9.49 us
    ppermute x4, starting transfers between devices, on_device(): lax.ppermute(everything, 'tile', [(i, i ^ 1 << bit) for i in range(peers)])  8.23 us
    all_to_all x1, waiting for transfers between devices, on_device(): lax.all_to_all(outbox, 'tile', split_axis=0, concat_axis=0, tiled=True)  7.76 us
    unnamed x38, local copies, waits for them, and re-layouts  5.06 us
    pallas_call x1, Pallas kernels, on_device(): pl.pallas_call(functools.partial(agree_kernel, group_total - 1), out_shap...  2.13 us
  transfers between devices with their start and end apart: 6, of which 6 were waited for; matrix products, arithmetic and copies ran while one was open for 1% of the time, Pallas kernels for 0%

profile of v1, /device:TPU:0, one launch (start us, length us, event | category | flops | bytes accessed | tf_op | source)
XLA Modules:
  0.0 75.8 jit_solution(3798569430014799278)
XLA Ops:
  0.6 0.8 %copy.29 = f32[1,2,59,128]{3,2,1,0:T(8,128)S(1)} copy(f32[1,2,59,128]{3,1,2,0:T(2,128)} %param.15) | data formatting | bytes 120832 | tf_op args[0]
  1.5 4.0 %collective-permute-start = (f32[2,59,128]{2,1,0:T(8,128)S(1)}, f32[2,59,128]{2,1,0:T(8,128)S(1)}, u32[]{:S(2)}, u32[]{:S(2)}) collective-permute-start(f32[2,59,128]{2,1,0:T(8,128)S(1)} %bitcast.25), channel_id=1, source_target_pairs={{0,8},{1,9},{2,10},{3,11},{4,12},{5,13},{6,14},{7,15},{8,0},{9,1},... | collective-permute-start | bytes 181256 | tf_op jit(solution)/shard_map/ppermute | solution.py:592
  5.5 3.6 %collective-permute-done = f32[2,59,128]{2,1,0:T(8,128)S(1)} collective-permute-done((f32[2,59,128]{2,1,0:T(8,128)S(1)}, f32[2,59,128]{2,1,0:T(8,128)S(1)}, u32[]{:S(2)}, u32[]{:S(2)}) %collective-permute-start) | collective-permute-done | bytes 60448 | tf_op jit(solution)/shard_map/ppermute | solution.py:592
  9.2 0.6 collective-permute-start.1
  9.8 4.4 %collective-permute-done.1 = f32[4,59,128]{2,1,0:T(8,128)S(1)} collective-permute-done((f32[4,59,128]{2,1,0:T(8,128)S(1)}, f32[4,59,128]{2,1,0:T(8,128)S(1)}, u32[]{:S(2)}, u32[]{:S(2)}) %collective-permute-start.1) | collective-permute-done | bytes 120864 | tf_op jit(solution)/shard_map/ppermute | solution.py:592
  14.2 0.0 copy-start.14
  14.2 1.8 %collective-permute-start.2 = (f32[8,59,128]{2,1,0:T(8,128)S(1)}, f32[8,59,128]{2,1,0:T(8,128)S(1)}, u32[]{:S(2)}, u32[]{:S(2)}) collective-permute-start(f32[8,59,128]{2,1,0:T(8,128)S(1)} %pad_maximum_fusion.1), channel_id=1, source_target_pairs={{0,2},{1,3},{2,0},{3,1},{4,6},{5,7},{6,4},{7,5},{8,10},{9,11},{10,... | collective-permute-start | bytes 725000 | tf_op jit(solution)/shard_map/ppermute | solution.py:592
  17.3 0.0 copy-done.14
  17.3 0.0 copy-start.11
  17.4 3.3 %collective-permute-done.2 = f32[8,59,128]{2,1,0:T(8,128)S(1)} collective-permute-done((f32[8,59,128]{2,1,0:T(8,128)S(1)}, f32[8,59,128]{2,1,0:T(8,128)S(1)}, u32[]{:S(2)}, u32[]{:S(2)}) %collective-permute-start.2) | collective-permute-done | bytes 241696 | tf_op jit(solution)/shard_map/ppermute | solution.py:592
  20.7 1.8 %collective-permute-start.3 = (f32[16,59,128]{2,1,0:T(8,128)S(1)}, f32[16,59,128]{2,1,0:T(8,128)S(1)}, u32[]{:S(2)}, u32[]{:S(2)}) collective-permute-start(f32[16,59,128]{2,1,0:T(8,128)S(1)} %pad_maximum_fusion), channel_id=1, source_target_pairs={{0,1},{1,0},{2,3},{3,2},{4,5},{5,4},{6,7},{7,6},{8,9},{9,8},{10,11... | collective-permute-start | bytes 1449992 | tf_op jit(solution)/shard_map/ppermute | solution.py:592
  22.5 0.0 copy-done.11
  22.5 0.0 copy-start
  22.6 0.0 copy-start.2
  22.6 0.0 copy-start.3
  22.6 8.1 %collective-permute-done.3 = f32[16,59,128]{2,1,0:T(8,128)S(1)} collective-permute-done((f32[16,59,128]{2,1,0:T(8,128)S(1)}, f32[16,59,128]{2,1,0:T(8,128)S(1)}, u32[]{:S(2)}, u32[]{:S(2)}) %collective-permute-start.3) | collective-permute-done | bytes 483360 | tf_op jit(solution)/shard_map/ppermute | solution.py:592
  30.6 0.0 copy-start.5
  30.7 0.0 copy-start.4
  30.7 0.0 copy-start.7
  30.7 0.0 copy-start.8
  30.7 0.0 copy-done
  30.7 0.0 copy-done.2
  30.8 0.0 copy-done.3
  30.8 0.6 copy-done.5
  31.3 0.1 copy-done.4
  31.4 0.0 copy-done.7
  31.4 0.0 copy-done.8
  31.4 9.5 %render.1 = f32[16,16,128]{2,1,0:T(8,128)} custom-call(s32[1]{0:T(128)} %bitcast.me_ref, s32[1]{0:T(128)} %bitcast.23.cam_id_ref, s32[1]{0:T(128)} %bitcast.24.count_ref, s32[16]{0:T(128)S(1)} %bitcast.35, s32[16]{0:T(128)S(1)} %bitcast.36, f32[16,16]{1,0:T(8,128)S(1)} %copy-done.4, f32[32,59,128]{2,1,0:T(8,128)S(1)} %constant_dynamic-update-slice_fusion.blocks_ref, ...), custom_call_target="tpu_custom_call" | custom-call | tf_op jit(solution)/shard_map/render/pallas_call | solution.py:600
  40.9 0.0 copy-start.12
  40.9 0.0 copy-start.13
  40.9 20.0 %all-to-all-start = ((f32[16,16,128]{2,1,0:T(8,128)}), f32[16,16,128]{2,1,0:T(8,128)S(1)}, u32[]{:S(2)}, u32[]{:S(2)}) async-start(f32[16,16,128]{2,1,0:T(8,128)} %render.1), calls=%async_computation | async-start | bytes 262144 | tf_op jit(solution)/shard_map/all_to_all | solution.py:630
  60.9 0.0 copy-done.12
  60.9 0.0 copy-done.13
  60.9 7.8 %all-to-all-done = f32[16,16,128]{2,1,0:T(8,128)S(1)} async-done(((f32[16,16,128]{2,1,0:T(8,128)}), f32[16,16,128]{2,1,0:T(8,128)S(1)}, u32[]{:S(2)}, u32[]{:S(2)}) %all-to-all-start) | async-done | bytes 131104 | tf_op jit(solution)/shard_map/all_to_all | solution.py:630
  68.7 0.0 copy-start.6
  68.7 0.0 copy-start.9
  68.7 0.7 copy-done.6
  69.3 0.0 copy-done.9
  69.4 0.8 %owner.1 = (f32[2,59,128]{2,1,0:T(8,128)S(1)}, f32[2,59,64]{2,1,0:T(8,128)S(1)}) custom-call(f32[256,128]{1,0:T(8,128)S(1)} %bitcast.30, f32[2,59,128]{2,1,0:T(8,128)S(1)} %bitcast.29, f32[2,59,128]{2,1,0:T(8,128)S(1)} %get-tuple-element.9.cons_ref, f32[2,59,128]{2,1,0:T(8,128)S(1)} %get-tuple-element.8.dual_ref, f32[1,59]{1,0:T(1,128)S(1)} %bitcast.37, ...), custom_call_target="tpu_custom_call" | custom-call | tf_op jit(solution)/shard_map/owner/pallas_call | solution.py:633
  70.2 0.0 copy-start.1
  70.2 0.1 collective-permute-start.4
  70.3 0.7 copy.20
  70.9 0.0 copy-done.1
  70.9 0.6 collective-permute-done.4.above_ref.below_ref
  71.5 0.0 copy-start.10
  71.5 0.6 copy-done.10
  72.1 2.1 %agree.1 = f32[2,59,128]{2,1,0:T(8,128)} custom-call(s32[1]{0:T(128)} %bitcast.12.group_ref, f32[2,59,64]{2,1,0:T(8,128)} %copy-done.1, f32[2,59,64]{2,1,0:T(8,128)} %copy-done.10, f32[2,59,64]{2,1,0:T(8,128)} %copy-done.10, s32[2,64]{1,0:T(2,128)} %bitcast.33), custom_call_target="tpu_custom_call" | custom-call | tf_op jit(solution)/shard_map/agree/pallas_call | solution.py:652
  74.3 1.5 %copy.21 = f32[1,2,59,128]{3,1,2,0:T(2,128)} copy(f32[1,2,59,128]{3,2,1,0:T(8,128)} %bitcast.38) | data formatting | bytes 120832
  (10 shorter events, 0.2 us)
Async XLA Ops:
  1.5 7.7 %collective-permute-start = (f32[2,59,128]{2,1,0:T(8,128)S(1)}, f32[2,59,128]{2,1,0:T(8,128)S(1)}, u32[]{:S(2)}, u32[]{:S(2)}) collective-permute-start(f32[2,59,128]{2,1,0:T(8,128)S(1)} %bitcast.25), channel_id=1, source_target_pairs={{0,8},{1,9},{2,10},{3,11},{4,12},{5,13},{6,14},{7,15},{8,0},{9,1},... | collective-permute-start | bytes 181256 | tf_op jit(solution)/shard_map/ppermute | solution.py:592
  9.2 5.0 %collective-permute-start.1 = (f32[4,59,128]{2,1,0:T(8,128)S(1)}, f32[4,59,128]{2,1,0:T(8,128)S(1)}, u32[]{:S(2)}, u32[]{:S(2)}) collective-permute-start(f32[4,59,128]{2,1,0:T(8,128)S(1)} %pad_maximum_fusion.2), channel_id=1, source_target_pairs={{0,4},{1,5},{2,6},{3,7},{4,0},{5,1},{6,2},{7,3},{8,12},{9,13},{10,... | collective-permute-start | bytes 362504 | tf_op jit(solution)/shard_map/ppermute | solution.py:592
  14.2 3.1 %copy-start.14 = (f32[1,1,3,1024]{3,1,2,0:T(1,128)S(1)}, f32[1,1,3,1024]{3,1,2,0:T(1,128)}, u32[]{:S(2)}) copy-start(f32[1,1,3,1024]{3,1,2,0:T(1,128)} %param.24) | copy-start | bytes 36868
  14.2 6.4 %collective-permute-start.2 = (f32[8,59,128]{2,1,0:T(8,128)S(1)}, f32[8,59,128]{2,1,0:T(8,128)S(1)}, u32[]{:S(2)}, u32[]{:S(2)}) collective-permute-start(f32[8,59,128]{2,1,0:T(8,128)S(1)} %pad_maximum_fusion.1), channel_id=1, source_target_pairs={{0,2},{1,3},{2,0},{3,1},{4,6},{5,7},{6,4},{7,5},{8,10},{9,11},{10,... | collective-permute-start | bytes 725000 | tf_op jit(solution)/shard_map/ppermute | solution.py:592
  17.3 5.1 %copy-start.11 = (f32[1,2,59,128]{3,1,2,0:T(2,128)S(1)}, f32[1,2,59,128]{3,1,2,0:T(2,128)}, u32[]{:S(2)}) copy-start(f32[1,2,59,128]{3,1,2,0:T(2,128)} %param.15) | copy-start | bytes 181252
  20.7 9.9 %collective-permute-start.3 = (f32[16,59,128]{2,1,0:T(8,128)S(1)}, f32[16,59,128]{2,1,0:T(8,128)S(1)}, u32[]{:S(2)}, u32[]{:S(2)}) collective-permute-start(f32[16,59,128]{2,1,0:T(8,128)S(1)} %pad_maximum_fusion), channel_id=1, source_target_pairs={{0,1},{1,0},{2,3},{3,2},{4,5},{5,4},{6,7},{7,6},{8,9},{9,8},{10,11... | collective-permute-start | bytes 1449992 | tf_op jit(solution)/shard_map/ppermute | solution.py:592
  22.5 8.2 %copy-start = (bf16[32,1408]{1,0:T(8,128)(2,1)S(1)}, bf16[32,1408]{1,0:T(8,128)(2,1)}, u32[]{:S(2)}) copy-start(bf16[32,1408]{1,0:T(8,128)(2,1)} %constant.17.clone.basis_ref) | copy-start | bytes 270340
  22.6 8.2 %copy-start.2 = (f32[128,128]{1,0:T(8,128)S(1)}, f32[128,128]{1,0:T(8,128)}, u32[]{:S(2)}) copy-start(f32[128,128]{1,0:T(8,128)} %constant.19.clone.order_ref) | copy-start | bytes 196612
  22.6 8.2 %copy-start.3 = (f32[128,128]{1,0:T(8,128)S(1)}, f32[128,128]{1,0:T(8,128)}, u32[]{:S(2)}) copy-start(f32[128,128]{1,0:T(8,128)} %constant.20.clone.back_ref) | copy-start | bytes 196612
  30.6 0.7 copy-start.5
  30.7 0.7 copy-start.4
  30.7 0.7 copy-start.7
  30.7 0.7 copy-start.8
  40.9 20.0 %copy-start.12 = (f32[1,2,59,128]{3,1,2,0:T(2,128)S(1)}, f32[1,2,59,128]{3,1,2,0:T(2,128)}, u32[]{:S(2)}) copy-start(f32[1,2,59,128]{3,1,2,0:T(2,128)} %param.17) | copy-start | bytes 181252
  40.9 20.0 %copy-start.13 = (f32[1,2,59,128]{3,1,2,0:T(2,128)S(1)}, f32[1,2,59,128]{3,1,2,0:T(2,128)}, u32[]{:S(2)}) copy-start(f32[1,2,59,128]{3,1,2,0:T(2,128)} %param.16) | copy-start | bytes 181252
  40.9 27.8 %all-to-all-start = ((f32[16,16,128]{2,1,0:T(8,128)}), f32[16,16,128]{2,1,0:T(8,128)S(1)}, u32[]{:S(2)}, u32[]{:S(2)}) async-start(f32[16,16,128]{2,1,0:T(8,128)} %render.1), calls=%async_computation | async-start | bytes 262144 | tf_op jit(solution)/shard_map/all_to_all | solution.py:630
  68.7 0.7 copy-start.6
  68.7 0.7 copy-start.9
  70.2 0.8 %copy-start.1 = (f32[2,59,64]{2,1,0:T(8,128)}, f32[2,59,64]{2,1,0:T(8,128)S(1)}, u32[]{:S(2)}) copy-start(f32[2,59,64]{2,1,0:T(8,128)S(1)} %get-tuple-element.5.vals_ref) | copy-start | bytes 90628
  70.2 1.3 %collective-permute-start.4 = (f32[2,59,64]{2,1,0:T(8,128)S(1)}, f32[2,59,64]{2,1,0:T(8,128)S(1)}, u32[]{:S(2)}, u32[]{:S(2)}) collective-permute-start(f32[2,59,64]{2,1,0:T(8,128)S(1)} %get-tuple-element.5.vals_ref), channel_id=1, source_target_pairs={{0,16},{16,0},{1,17},{17,1},{2,18},{18,2},{3,19},{19,3},{4,20},{20... | collective-permute-start | bytes 90632 | tf_op jit(solution)/shard_map/ppermute | solution.py:648
  71.5 0.6 copy-start.10

commit v2 on v1

--- a/solution.py
+++ b/solution.py
@@ -33,8 +33,10 @@
 
 LANES = 128
 SUB = 8
-ROWS = 64
-KDIM = 32
+PART = 16
+KDIM = 3 * PART
+COEFS = 9
+INNER = 4
 SEGS = 8
 MOMENTS = 6
 MSG = 16
@@ -132,25 +134,122 @@
     return high, mid, rest - mid
 
 
+def exact_pick(value, pick):
+    high, mid, low = [part.astype(jnp.bfloat16) for part in three_parts(value)]
+    dot = functools.partial(jnp.dot, preferred_element_type=jnp.float32)
+    return (dot(high, pick) + dot(mid, pick)) + dot(low, pick)
+
+
 def sub_roll(value, shift):
     return pltpu.roll(value, shift % SUB, 0)
 
 
+def prepare_kernel(
+    links, group_ref, own_ref, cons_ref, dual_ref, step_ref, share_ref, *refs
+):
+    others, (base_ref, steps_ref, pick_ref, mask_ref) = refs[: len(links)], refs[len(links) :]
+    blocks, params = own_ref.shape[0], own_ref.shape[1]
+    group = group_ref[0]
+    shape = (params, params)
+    diagonal = lax.broadcasted_iota(jnp.int32, shape, 0) == lax.broadcasted_iota(jnp.int32, shape, 1)
+    steps = jnp.sum(
+        jnp.where(diagonal, jnp.broadcast_to(step_ref[...], shape), 0.0), axis=1, keepdims=True
+    )
+    steps = jnp.broadcast_to(steps, (params, LANES))
+    steps_ref[...] = steps
+    for b in range(blocks):
+        here = own_ref[b]
+        base_ref[b] = here - steps * (penalty_weight * (here - cons_ref[b] + dual_ref[b]))
+    half = share_ref.shape[1]
+    local = lax.broadcasted_iota(jnp.int32, (blocks * LANES, half), 0)
+    contract = (((1,), (1,)), ((), ()))
+    for n, (side_of, exists_of) in enumerate(links):
+        other = others[n]
+        up = side_of(group)
+        mine = jnp.where(up, share_ref[0:1, :], share_ref[1:2, :])
+        theirs = jnp.where(up, other[1:2, :], other[0:1, :])
+        source = (local == mine).astype(jnp.bfloat16)
+        target = (local == theirs).astype(jnp.bfloat16)
+        pick_ref[n] = lax.dot_general(
+            source, target, contract, preferred_element_type=jnp.float32
+        ).astype(jnp.bfloat16)
+        there = jnp.full((SUB, half), jnp.where(exists_of(group), 1.0, 0.0)).astype(jnp.bfloat16)
+        mask = lax.dot_general(there, source, contract, preferred_element_type=jnp.float32)
+        for b in range(blocks):
+            mask_ref[n, b] = mask[:, b * LANES : (b + 1) * LANES]
+
+
+def project_kernel(masks, yrows, me_ref, raw_ref, ids_ref, cameras_ref, order_ref, *refs):
+    outs, feat = refs[:INNER], refs[INNER]
+    outer = len(masks)
+    blocks = raw_ref.shape[0] // outer
+    me = me_ref[0]
+    ids = jnp.concatenate([ids_ref[...]] * (SUB // INNER), axis=0)
+    lane = lax.broadcasted_iota(jnp.int32, (SUB, LANES), 1)
+    sub = lax.broadcasted_iota(jnp.int32, (SUB, LANES), 0)
+    ncam = cameras_ref.shape[0]
+    chosen = lax.broadcasted_iota(jnp.int32, (SUB, ncam), 1) == ids[:, 0:1]
+    shots = jnp.dot(chosen.astype(jnp.float32), cameras_ref[...], precision=highest)
+    cam = [jnp.broadcast_to(shots[:, k : k + 1], (SUB, LANES)) for k in range(16)]
+    top = (((me & 3) ^ (sub & 3)) * yrows).astype(jnp.float32)
+    lists = ids[:, LANES:]
+    rows = outer * INNER
+    for v in range(rows // SUB):
+        owners = [2 * v, 2 * v + 1]
+        first = jnp.where(sub < INNER, (me ^ masks[owners[0]]) * blocks, (me ^ masks[owners[1]]) * blocks)
+        found = []
+        for b in range(1, blocks):
+            same = (lists == first[:, : lists.shape[1]] + b).astype(jnp.float32)
+            found.append(jnp.broadcast_to(jnp.max(same, axis=1, keepdims=True), (SUB, LANES)) > 0.5)
+
+        def row(p):
+            def of(b):
+                return jnp.where(
+                    sub < INNER,
+                    jnp.broadcast_to(raw_ref[owners[0] * blocks + b, p : p + 1, :], (SUB, LANES)),
+                    jnp.broadcast_to(raw_ref[owners[1] * blocks + b, p : p + 1, :], (SUB, LANES)),
+                )
+
+            value = of(0)
+            for b in range(1, blocks):
+                value = jnp.where(found[b - 1], of(b), value)
+            return value
+
+        geo = geometry(row, cam)
+        sx = cam[12] * geo["u"] + (cam[14] - 64.0)
+        sy = cam[13] * geo["v"] + (cam[15] - top - 4.0)
+        basis = harmonic_basis(*geo["toward"])
+        tint = [sum(basis[k] * row(11 + 3 * k + c) for k in range(16)) + 0.5 for c in range(3)]
+        lo = -jnp.log(1.0 + jnp.exp(-row(10))) * log2e
+        ca, cb, cc = geo["conic"]
+        kxx = (-0.5 * log2e) * ca
+        kxy = -log2e * cb
+        kyy = (-0.5 * log2e) * cc
+        kx = -2.0 * kxx * sx - kxy * sy
+        ky = -2.0 * kyy * sy - kxy * sx
+        k1 = kxx * sx * sx + kxy * sx * sy + kyy * sy * sy + lo
+        for m, value in enumerate([kxx, kxy, kyy, kx, ky, k1, *tint]):
+            feat[m * rows + v * SUB : m * rows + (v + 1) * SUB, :] = value
+    feat[...] = exact_pick(feat[...], order_ref[...])
+    for j in range(INNER):
+        outs[j][...] = feat[pl.ds(j, COEFS * outer, stride=INNER), :]
+
+
 def render_kernel(
-    pixels, hop_bits, me_ref, cam_id_ref, count_ref, list_ref, depth_ref, cameras_ref,
-    blocks_ref, target_ref, basis_ref, xmom_ref, order_ref, back_ref, out_ref,
-    raw, feat, coef, expo, shade, alphas, weights, carry, before, passed, colours,
+    pixels, blocks, hop_bits, me_ref, cam_id_ref, count_ref, list_ref, depth_ref, cameras_ref,
+    src0, src1, src2, src3, target_ref, basis_ref, xmom_ref, back_ref, out_ref,
+    raw, coef, expo, shade, alphas, weights, carry, before, passed, colours,
     resid, behind, sums, found, rows, slots,
 ):
     listed = list_ref.shape[0]
     peers = out_ref.shape[0]
-    per_owner = blocks_ref.shape[0] // peers
+    outer = peers // INNER
+    per_owner = blocks
     yrows = pixels // LANES
     groups = LANES // SUB
     me = me_ref[0]
     count = count_ref[0]
     cam_id = cam_id_ref[0]
-    cam = [cameras_ref[cam_id, k] for k in range(16)]
     top = ((me % 4) * yrows).astype(jnp.float32)
 
     def place_slot(j, ends):
@@ -162,46 +261,22 @@
 
     lax.fori_loop(0, listed, place_slot, (jnp.int32(0), count))
 
+    for j, src in enumerate((src0, src1, src2, src3)):
+        raw[j * COEFS * outer : (j + 1) * COEFS * outer, :] = src[...]
+    coef[...] = jnp.zeros(coef.shape, jnp.float32)
+
     def fetch(k, _):
-        block = list_ref[slots[k]]
-        owner = block // per_owner
-        if hop_bits is None:
-            near = owner
-        else:
-            apart = me ^ owner
-            near = sum((((apart >> bit) & 1) << t) for t, bit in enumerate(hop_bits))
-        source = near * per_owner + block % per_owner
-        raw[pl.ds(pl.multiple_of(k * ROWS, ROWS), blocks_ref.shape[1]), :] = blocks_ref[source]
+        apart = me ^ (list_ref[slots[k]] // per_owner)
+        near = sum((((apart >> bit) & 1) << t) for t, bit in enumerate(hop_bits))
+        start = (apart & (INNER - 1)) * (COEFS * outer) + near
+        value = raw[pl.ds(start, COEFS, stride=outer), :]
+        for part, piece in enumerate(three_parts(value)):
+            base = pl.multiple_of(k * KDIM + part * PART, PART)
+            coef[pl.ds(base, COEFS), :] = piece
+            coef[pl.ds(base + COEFS, 1), :] = piece[0:1, :]
         return 0
 
-    lax.fori_loop(0, listed, fetch, 0)
-
-    def row(p):
-        return raw[pl.ds(p, listed, stride=ROWS), :]
-
-    geo = geometry(row, cam)
-    screen_x = cam[12] * geo["u"] + cam[14]
-    screen_y = cam[13] * geo["v"] + cam[15]
-    basis = harmonic_basis(*geo["toward"])
-    tint = [sum(basis[k] * row(11 + 3 * k + c) for k in range(16)) + 0.5 for c in range(3)]
-    log_opacity = -jnp.log(1.0 + jnp.exp(-row(10))) * log2e
-    natural = [screen_x - 64.0, screen_y - (top + 4.0), *geo["conic"], log_opacity, *tint]
-    for m, value in enumerate(natural):
-        feat[m * listed : (m + 1) * listed, :] = value
-    feat[...] = jnp.dot(feat[...], order_ref[...], precision=highest)
-    sx, sy, ca, cb, cc, lo, *tint = [feat[m * listed : (m + 1) * listed, :] for m in range(9)]
-    kxx = (-0.5 * log2e) * ca
-    kxy = -log2e * cb
-    kyy = (-0.5 * log2e) * cc
-    kx = -2.0 * kxx * sx - kxy * sy
-    ky = -2.0 * kyy * sy - kxy * sx
-    k1 = kxx * sx * sx + kxy * sx * sy + kyy * sy * sy + lo
-    for c, value in enumerate([kxx, kxx, kxy, kyy, kx, ky, k1, *tint]):
-        for part, piece in enumerate(three_parts(value)):
-            coef[pl.ds(part * 10 + c, listed, stride=KDIM), :] = piece
-    zero = jnp.zeros((listed, LANES), jnp.float32)
-    for c in range(30, KDIM):
-        coef[pl.ds(c, listed, stride=KDIM), :] = zero
+    lax.fori_loop(0, count, fetch, 0)
 
     sub = lax.broadcasted_iota(jnp.int32, (SUB, LANES), 0)
     one = jnp.ones((SUB, LANES), jnp.float32)
@@ -216,7 +291,7 @@
         return jnp.broadcast_to(value[index : index + 1, :], (SUB, LANES))
 
     def forward(k, _):
-        mine = coef[pl.ds(pl.multiple_of(k * KDIM, KDIM), KDIM), :].astype(jnp.bfloat16)
+        mine = coef[pl.ds(pl.multiple_of(k * KDIM, PART), KDIM), :].astype(jnp.bfloat16)
         expo[...] = lax.dot_general(
             mine, basis_ref[...], (((0,), (0,)), ((), ())), preferred_element_type=jnp.float32
         )
@@ -321,37 +396,35 @@
 
     lane = lax.broadcasted_iota(jnp.int32, (1, LANES), 1)
     middle = (
-        lax.broadcasted_iota(jnp.int32, (SUB, LANES), 0) * (LANES // SEGS) + (LANES // SEGS // 2 - 64)
+        lax.broadcasted_iota(jnp.int32, (SUB, LANES), 0) * (LANES // SEGS)
+        + (LANES // SEGS // 2 - 64)
     ).astype(jnp.float32)
-    meta = jnp.zeros((1, LANES), jnp.float32)
+    meta = jnp.where(lane == 17, top, 0.0)
     for c in range(16):
-        meta = jnp.where(lane == c, cam[c], meta)
+        meta = jnp.where(lane == c, cameras_ref[cam_id, c], meta)
 
     rows[...] = jnp.zeros(rows.shape, jnp.float32)
 
     def gather_moments(k, _):
         part = lambda order, m: found[k, order * SEGS : (order + 1) * SEGS, m * LANES : (m + 1) * LANES]
         add = lambda value: jnp.sum(value, axis=0, keepdims=True)
-        off = middle - feat[pl.ds(k, 1), :]
-        rise = (yrows - 4.0) - feat[pl.ds(listed + k, 1), :]
+        rise = yrows - 4.0
         h0, h1, h2 = part(0, 0), part(1, 0), part(2, 0)
         n0, n1 = part(0, 1), part(1, 1)
         s0 = add(h0)
-        sx1 = add(h1 + off * h0)
-        sxx = add(h2 + off * (2.0 * h1 + off * h0))
+        x1 = add(h1 + middle * h0)
+        x2 = add(h2 + middle * (2.0 * h1 + middle * h0))
         t1 = add(n0)
-        tx = add(n1 + off * n0)
+        tx = add(n1 + middle * n0)
         t2 = 2.0 * add(part(0, 2)) - t1
-        sy1 = rise * s0 - t1
-        sxy = rise * sx1 - tx
-        syy = rise * (rise * s0 - 2.0 * t1) + t2
-        answer = [s0, sx1, sy1, sxx, sxy, syy] + [add(part(0, 3 + c)) for c in range(3)]
+        answer = [s0, x1, rise * s0 - t1, x2, rise * x1 - tx, rise * (rise * s0 - 2.0 * t1) + t2]
+        answer += [add(part(0, 3 + c)) for c in range(3)]
         for m, value in enumerate(answer):
             rows[pl.ds(k * MSG + m, 1), :] = value
         return 0
 
     lax.fori_loop(0, count, gather_moments, 0)
-    rows[...] = jnp.dot(rows[...], back_ref[...], precision=highest)
+    rows[...] = exact_pick(rows[...], back_ref[...])
 
     if peers > listed:
         absent = jnp.where(lane == 16, -1.0, 0.0)
@@ -369,7 +442,9 @@
     lax.fori_loop(0, listed, send, 0)
 
 
-def owner_kernel(inbox_ref, own_ref, cons_ref, dual_ref, step_ref, share_ref, new_ref, vals_ref, grad):
+def owner_kernel(
+    inbox_ref, own_ref, base_ref, dual_ref, steps_ref, pick_ref, new_ref, shifted_ref, sent_ref, grad
+):
     blocks = own_ref.shape[0]
     params = own_ref.shape[1]
     strips = inbox_ref.shape[0] // MSG
@@ -378,8 +453,8 @@
         return inbox_ref[pl.ds(m, strips, stride=MSG), :]
 
     meta = message(9)
-    cam = [jnp.broadcast_to(meta[:, k : k + 1], (strips, LANES)) for k in range(17)]
-    place = cam[16]
+    cam = [jnp.broadcast_to(meta[:, k : k + 1], (strips, LANES)) for k in range(18)]
+    place, top = cam[16], cam[17]
 
     def row(p):
         value = jnp.broadcast_to(own_ref[0, p : p + 1, :], (strips, LANES))
@@ -388,11 +463,18 @@
         return value
 
     geo = geometry(row, cam)
-    s0, sx, sy, sxx, sxy, syy, *drawn = [message(m) for m in range(9)]
+    u, v, inverse = geo["u"], geo["v"], geo["inverse"]
+    focal_x, focal_y = cam[12], cam[13]
+    at_x = focal_x * u + (cam[14] - 64.0)
+    at_y = focal_y * v + (cam[15] - top - 4.0)
+    s0, x1, y1, x2, xy, y2, *drawn = [message(m) for m in range(9)]
+    sx = x1 - at_x * s0
+    sy = y1 - at_y * s0
+    sxx = x2 - at_x * (x1 + sx)
+    sxy = xy - at_x * y1 - at_y * sx
+    syy = y2 - at_y * (y1 + sy)
     ca, cb, cc = geo["conic"]
-    u, v, inverse = geo["u"], geo["v"], geo["inverse"]
     axes, rot = geo["axes"], geo["rot"]
-    focal_x, focal_y = cam[12], cam[13]
     grads = {}
     opacity = 1.0 / (1.0 + jnp.exp(-row(10)))
     grads[10] = s0 * (1.0 - opacity)
@@ -486,48 +568,18 @@
                 jnp.where(mine, grads[p], 0.0), axis=0, keepdims=True
             )
 
-    shape = (params, params)
-    diagonal = lax.broadcasted_iota(jnp.int32, shape, 0) == lax.broadcasted_iota(jnp.int32, shape, 1)
-    steps = jnp.sum(
-        jnp.where(diagonal, jnp.broadcast_to(step_ref[...], shape), 0.0), axis=1, keepdims=True
-    )
-    half = share_ref.shape[1]
-    local = lax.broadcasted_iota(jnp.int32, (LANES, half), 0)
-    vals = [jnp.zeros((params, half), jnp.float32) for _ in range(2)]
+    parts = []
     for b in range(blocks):
-        here = own_ref[b]
-        dual = dual_ref[b]
-        new = here - steps * (
-            grad[b, :params, :] + penalty_weight * (here - cons_ref[b] + dual)
-        )
+        new = base_ref[b] - steps_ref[...] * grad[b, :params, :]
+        shifted = new + dual_ref[b]
         new_ref[b] = new
-        shifted = new + dual
-        for side in range(2):
-            pick = (share_ref[side : side + 1, :] == local + b * LANES).astype(jnp.float32)
-            vals[side] = vals[side] + jnp.dot(shifted, pick, precision=highest)
-    for side in range(2):
-        vals_ref[side] = vals[side]
-
-
-def agree_kernel(last_group, group_ref, vals_ref, above_ref, below_ref, share_ref, out_ref):
-    group = group_ref[0]
-    half = share_ref.shape[1]
-    blocks, params = out_ref.shape[0], out_ref.shape[1]
-    changes = []
-    for side, other, shared in ((0, above_ref, group < last_group), (1, below_ref, group > 0)):
-        mine = vals_ref[side]
-        change = mine - 0.5 * (mine + other[1 - side])
-        changes.append(jnp.where(shared, change, 0.0))
-    local = lax.broadcasted_iota(jnp.int32, (LANES, half), 0)
-    for b in range(blocks):
-        total = jnp.zeros((params, LANES), jnp.float32)
-        for side in range(2):
-            pick = (share_ref[side : side + 1, :] == local + b * LANES).astype(jnp.float32)
-            total = total + lax.dot_general(
-                changes[side], pick, (((1,), (1,)), ((), ())), precision=highest,
-                preferred_element_type=jnp.float32,
-            )
-        out_ref[b] = total
+        shifted_ref[b] = shifted
+        parts.append(shifted)
+    shifted = jnp.concatenate(parts, axis=1)
+    for n in range(pick_ref.shape[0]):
+        value = exact_pick(shifted, pick_ref[n])
+        for b in range(blocks):
+            sent_ref[n, b] = value[:, b * LANES : (b + 1) * LANES]
 
 
 def constants(pixels):
@@ -535,14 +587,13 @@
     x = (place % LANES - 64).astype(np.float32)
     y = (place // LANES - 4).astype(np.float32)
     square = (x * x).astype(jnp.bfloat16).astype(np.float32)
-    some = np.ones_like(x)
-    part = np.zeros((10, pixels + 3 * LANES), np.float32)
-    for c, value in enumerate([square, x * x - square, x * y, y * y, x, y, some]):
+    part = np.zeros((PART, pixels + 3 * LANES), np.float32)
+    for c, value in enumerate([square, x * y, y * y, x, y, np.ones_like(x)]):
         part[c, :pixels] = value
     for c in range(3):
-        part[7 + c, pixels + c * LANES : pixels + (c + 1) * LANES] = 1.0
-    basis = np.zeros((KDIM, pixels + 3 * LANES), np.float32)
-    basis[:30] = np.concatenate([part] * 3)
+        part[6 + c, pixels + c * LANES : pixels + (c + 1) * LANES] = 1.0
+    part[COEFS, :pixels] = x * x - square
+    basis = np.concatenate([part] * 3)
     lane = np.arange(LANES)
     wide = LANES // SEGS
     xmom = np.zeros((3 * SEGS + SEGS, LANES), np.float32)
@@ -555,20 +606,19 @@
     groups = LANES // SUB
     for r in range(LANES):
         order[(r % SUB) * groups + r // SUB, r] = 1.0
-    return (
-        jnp.asarray(basis, jnp.bfloat16),
-        jnp.asarray(xmom, jnp.bfloat16),
-        jnp.asarray(order),
-        jnp.asarray(order.T.copy()),
-    )
-
-
-def vmem():
-    return pl.BlockSpec(memory_space=pltpu.VMEM)
-
-
-def smem():
-    return pl.BlockSpec(memory_space=pltpu.SMEM)
+    return [jnp.asarray(value, jnp.bfloat16) for value in (basis, xmom, order, order.T)]
+
+
+def vmem(number=1):
+    return [pl.BlockSpec(memory_space=pltpu.VMEM)] * number
+
+
+def smem(number=1):
+    return [pl.BlockSpec(memory_space=pltpu.SMEM)] * number
+
+
+def params_with(mib):
+    return pltpu.CompilerParams(vmem_limit_bytes=mib * 2**20)
 
 
 def on_device(
@@ -578,33 +628,78 @@
     own = gaussians[0]
     blocks, params = own.shape[0], own.shape[1]
     peers = lax.axis_size("tile")
-    me = lax.axis_index("tile")
+    me = lax.axis_index("tile")[None]
     listed = block_lists.shape[2]
     pixels = targets.shape[3]
     yrows = pixels // LANES
+    outer = peers // INNER
     f32 = jnp.float32
-
+    shape_of = jax.ShapeDtypeStruct
+    basis, xmom, order, back = constants(pixels)
+
+    def swap(value, mask):
+        return lax.ppermute(value, "tile", [(i, i ^ mask) for i in range(peers)])
+
+    hop_bits = list(reversed(range(2, peers.bit_length() - 1)))
+    ids = jnp.concatenate(
+        [jnp.broadcast_to(camera_ids, (1, LANES)), block_lists[0]], axis=1
+    )
     everything = own
-    hop_bits = None
-    if peers & (peers - 1) == 0:
-        hop_bits = list(reversed(range(peers.bit_length() - 1)))
-        for bit in hop_bits:
-            arrived = lax.ppermute(
-                everything, "tile", [(i, i ^ (1 << bit)) for i in range(peers)]
-            )
-            everything = jnp.concatenate([everything, arrived], 0)
+    masks = [0]
+    for step, bit in enumerate(hop_bits):
+        arrived = swap(everything, 1 << bit)
+        if step < 2:
+            ids = jnp.concatenate([ids, swap(ids, 1 << step)], 0)
+        everything = jnp.concatenate([everything, arrived], 0)
+        masks += [mask | (1 << bit) for mask in masks]
+
+    group_total = lax.axis_size("scene")
+    group = lax.axis_index("scene")[None]
+    share = intersection[0, 0]
+    if group_total == 2:
+        routes = [[(0, 1), (1, 0)]]
+        links = [(lambda g: g == 0, lambda g: g >= 0)]
     else:
-        everything = lax.all_gather(own, "tile", axis=0, tiled=True)
-
-    basis, xmom, order, back = constants(pixels)
+        routes = [
+            [(g + 1, g) for g in range(group_total - 1)],
+            [(g, g + 1) for g in range(group_total - 1)],
+        ]
+        links = [
+            (lambda g: g >= 0, lambda g: g < group_total - 1),
+            (lambda g: g < 0, lambda g: g > 0),
+        ]
+    lists = [lax.ppermute(share, "scene", route) for route in routes]
+
+    base, steps, pick, mask = pl.pallas_call(
+        functools.partial(prepare_kernel, links),
+        out_shape=(
+            shape_of(own.shape, f32),
+            shape_of((params, LANES), f32),
+            shape_of((len(links), blocks * LANES, blocks * LANES), jnp.bfloat16),
+            shape_of((len(links), blocks, SUB, LANES), f32),
+        ),
+        in_specs=smem() + vmem(5 + len(links)),
+        out_specs=tuple(vmem(4)),
+        name="prepare",
+    )(group, own, consensus[0], duals[0], step_sizes[None, :], share, *lists)
+
+    messages = pl.pallas_call(
+        functools.partial(project_kernel, masks, yrows),
+        out_shape=tuple([shape_of((COEFS * outer, LANES), f32)] * INNER),
+        in_specs=smem() + vmem(4),
+        out_specs=tuple(vmem(INNER)),
+        scratch_shapes=[pltpu.VMEM((COEFS * outer * INNER, LANES), f32)],
+        name="project",
+    )(me, everything, ids, cameras, order)
+    sources = [messages[0]] + [swap(messages[j], j) for j in range(1, INNER)]
+
     outbox = pl.pallas_call(
-        functools.partial(render_kernel, pixels, hop_bits),
-        out_shape=jax.ShapeDtypeStruct((peers, MSG, LANES), f32),
-        in_specs=[smem()] * 6 + [vmem()] * 6,
-        out_specs=vmem(),
+        functools.partial(render_kernel, pixels, blocks, hop_bits),
+        out_shape=shape_of((peers, MSG, LANES), f32),
+        in_specs=smem(6) + vmem(INNER + 4),
+        out_specs=vmem()[0],
         scratch_shapes=[
-            pltpu.VMEM((listed * ROWS, LANES), f32),
-            pltpu.VMEM((9 * listed, LANES), f32),
+            pltpu.VMEM((COEFS * peers, LANES), f32),
             pltpu.VMEM((listed * KDIM, LANES), f32),
             pltpu.VMEM((LANES, pixels + 3 * LANES), f32),
             pltpu.VMEM((listed * LANES, 3 * LANES), f32),
@@ -621,41 +716,30 @@
             pltpu.VMEM((listed * MSG, LANES), f32),
             pltpu.SMEM((listed,), jnp.int32),
         ],
-        compiler_params=pltpu.CompilerParams(vmem_limit_bytes=48 * 2**20),
+        compiler_params=params_with(48),
         name="render",
     )(
-        me[None], camera_ids[0], block_counts[0], block_lists[0, 0], depth_order[0, 0], cameras,
-        everything, targets[0, 0], basis, xmom, order, back,
+        me, camera_ids[0], block_counts[0], block_lists[0, 0], depth_order[0, 0], cameras,
+        *sources, targets[0, 0], basis, xmom, back,
     )
     inbox = lax.all_to_all(outbox, "tile", split_axis=0, concat_axis=0, tiled=True)
-    share = intersection[0, 0]
-    half = share.shape[1]
-    updated, vals = pl.pallas_call(
+    updated, shifted, sent = pl.pallas_call(
         owner_kernel,
         out_shape=(
-            jax.ShapeDtypeStruct(own.shape, f32),
-            jax.ShapeDtypeStruct((2, params, half), f32),
+            shape_of(own.shape, f32),
+            shape_of(own.shape, f32),
+            shape_of((len(links),) + own.shape, f32),
         ),
-        in_specs=[vmem()] * 6,
-        out_specs=(vmem(), vmem()),
-        scratch_shapes=[pltpu.VMEM((blocks, ROWS, LANES), f32)],
-        compiler_params=pltpu.CompilerParams(vmem_limit_bytes=32 * 2**20),
+        in_specs=vmem(6),
+        out_specs=tuple(vmem(3)),
+        scratch_shapes=[pltpu.VMEM((blocks, params + 5, LANES), f32)],
         name="owner",
-    )(inbox.reshape(peers * MSG, LANES), own, consensus[0], duals[0], step_sizes[None, :], share)
-    group_total = lax.axis_size("scene")
-    group = lax.axis_index("scene")
-    if group_total == 2:
-        above = below = lax.ppermute(vals, "scene", [(0, 1), (1, 0)])
-    else:
-        above = lax.ppermute(vals, "scene", [(g + 1, g) for g in range(group_total - 1)])
-        below = lax.ppermute(vals, "scene", [(g, g + 1) for g in range(group_total - 1)])
-    new_duals = pl.pallas_call(
-        functools.partial(agree_kernel, group_total - 1),
-        out_shape=jax.ShapeDtypeStruct(own.shape, f32),
-        in_specs=[smem()] + [vmem()] * 4,
-        out_specs=vmem(),
-        name="agree",
-    )(group[None], vals, above, below, share)
+    )(inbox.reshape(peers * MSG, LANES), own, base, duals[0], steps, pick)
+    new_duals = jnp.zeros_like(shifted)
+    for n, route in enumerate(routes):
+        theirs = lax.ppermute(sent[n], "scene", route)
+        change = shifted - 0.5 * (shifted + theirs)
+        new_duals = jnp.where(mask[n, :, :1, :] > 0.5, change, new_duals)
     return updated[None], new_duals[None]
 
 

time: 76.2 us -> 64.7 us (0.85)
  waiting for transfers between devices: 27.7 us -> 10.3 us
  Pallas kernels: 12.4 us -> 25.8 us
  starting transfers between devices: 28.3 us -> 15.1 us
  local copies, waits for them, and re-layouts: 5.11 us -> 8.5 us
  other arithmetic: 0.06 us -> 2.07 us
    all_to_all x1, starting transfers between devices: 20 us -> 3.64 us  [on_device(): lax.all_to_all(outbox, 'tile', split_axis=0, concat_axis=0, tiled=True)]
    pallas_call x3 -> x4, Pallas kernels: 12.4 us -> 25.8 us  [the longest x1 19.4 us: on_device(): pl.pallas_call(functools.partial(render_kernel, pixels, blocks, hop_bits)...]
    ppermute x5 -> x9, waiting for transfers between devices: 20 us -> 7.05 us  [the longest x7 7.04 us: swap(): return lax.ppermute(value, 'tile', [(i, i ^ mask) for i in range(peers)])]
    all_to_all x1, waiting for transfers between devices: 7.76 us -> 3.22 us  [on_device(): lax.all_to_all(outbox, 'tile', split_axis=0, concat_axis=0, tiled=True)]
    unnamed x38 -> x37, local copies, waits for them, and re-layouts: 5.06 us -> 8.49 us
    ppermute x5 -> x9, starting transfers between devices: 8.31 us -> 11.4 us  [the longest x7 11.4 us: swap(): return lax.ppermute(value, 'tile', [(i, i ^ mask) for i in range(peers)])]
  transfers between devices with their start and end apart: 6 -> 10, of which waited for: 6 -> 6; matrix products, arithmetic and copies ran while one was open for 1% -> 7% of each run, Pallas kernels for 0% -> 3%
where the time goes in v2:
time: 64.7 us; the launch traced here: 63.7 us
  Pallas kernels  25.8 us (40%)
  starting transfers between devices  15.1 us (23%)
  waiting for transfers between devices  10.3 us (16%)
  local copies, waits for them, and re-layouts  8.5 us (13%)
  other arithmetic  2.07 us (3%)
  between operations  2.04 us (3%)
    pallas_call x1, Pallas kernels, on_device(): pl.pallas_call(functools.partial(render_kernel, pixels, blocks, hop_bits)...  19.4 us
    ppermute x7, starting transfers between devices, swap(): return lax.ppermute(value, 'tile', [(i, i ^ mask) for i in range(peers)])  11.4 us
    unnamed x37, local copies, waits for them, and re-layouts  8.49 us
    ppermute x7, waiting for transfers between devices, swap(): return lax.ppermute(value, 'tile', [(i, i ^ mask) for i in range(peers)])  7.04 us
    all_to_all x1, starting transfers between devices, on_device(): lax.all_to_all(outbox, 'tile', split_axis=0, concat_axis=0, tiled=True)  3.64 us
    all_to_all x1, waiting for transfers between devices, on_device(): lax.all_to_all(outbox, 'tile', split_axis=0, concat_axis=0, tiled=True)  3.22 us
    pallas_call x1, Pallas kernels, on_device(): pl.pallas_call(owner_kernel, out_shape=(shape_of(own.shape, f32), shape_o...  2.34 us
    pallas_call x1, Pallas kernels, on_device(): pl.pallas_call(functools.partial(project_kernel, masks, yrows), out_shape...  2.23 us
  transfers between devices with their start and end apart: 10, of which 6 were waited for; matrix products, arithmetic and copies ran while one was open for 7% of the time, Pallas kernels for 3%

profile of v2, /device:TPU:0, one launch (start us, length us, event | category | flops | bytes accessed | tf_op | source)
XLA Modules:
  0.0 63.7 jit_solution(8689003589270270756)
XLA Ops:
  0.6 0.8 %copy.36 = f32[1,2,59,128]{3,2,1,0:T(8,128)S(1)} copy(f32[1,2,59,128]{3,1,2,0:T(2,128)} %param.15) | data formatting | bytes 120832 | tf_op args[0]
  1.5 0.0 copy-start.7
  1.5 4.0 %collective-permute-start = (f32[2,59,128]{2,1,0:T(8,128)S(1)}, f32[2,59,128]{2,1,0:T(8,128)S(1)}, u32[]{:S(2)}, u32[]{:S(2)}) collective-permute-start(f32[2,59,128]{2,1,0:T(8,128)S(1)} %bitcast.37), channel_id=1, source_target_pairs={{0,8},{1,9},{2,10},{3,11},{4,12},{5,13},{6,14},{7,15},{8,0},{9,1},... | collective-permute-start | bytes 181256 | tf_op jit(solution)/shard_map/ppermute | solution.py:641
  6.2 0.0 copy-start.5
  6.2 0.6 %copy-done.5 = s32[1,1,16]{2,1,0:T(1,128)S(1)} copy-done((s32[1,1,16]{2,1,0:T(1,128)S(1)}, s32[1,1,16]{2,1,0:T(1,128)}, u32[]{:S(2)}) %copy-start.5) | copy-done | bytes 88
  6.8 1.5 %collective-permute-start.2 = (s32[1,144]{1,0:T(1,128)S(1)}, s32[1,144]{1,0:T(1,128)S(1)}, u32[]{:S(2)}, u32[]{:S(2)}) collective-permute-start(s32[1,144]{1,0:T(1,128)S(1)} %concatenate.19), channel_id=1, source_target_pairs={{0,1},{1,0},{2,3},{3,2},{4,5},{5,4},{6,7},{7,6},{8,9},{9,8},{10,11... | collective-permute-start | bytes 1736 | tf_op jit(solution)/shard_map/ppermute | solution.py:641
  8.3 0.8 %collective-permute-done = f32[2,59,128]{2,1,0:T(8,128)S(1)} collective-permute-done((f32[2,59,128]{2,1,0:T(8,128)S(1)}, f32[2,59,128]{2,1,0:T(8,128)S(1)}, u32[]{:S(2)}, u32[]{:S(2)}) %collective-permute-start) | collective-permute-done | bytes 60448 | tf_op jit(solution)/shard_map/ppermute | solution.py:641
  9.2 0.8 %collective-permute-start.1 = (f32[4,59,128]{2,1,0:T(8,128)S(1)}, f32[4,59,128]{2,1,0:T(8,128)S(1)}, u32[]{:S(2)}, u32[]{:S(2)}) collective-permute-start(f32[4,59,128]{2,1,0:T(8,128)S(1)} %pad_maximum_fusion.1), channel_id=1, source_target_pairs={{0,4},{1,5},{2,6},{3,7},{4,0},{5,1},{6,2},{7,3},{8,12},{9,13},{10,... | collective-permute-start | bytes 362504 | tf_op jit(solution)/shard_map/ppermute | solution.py:641
  10.0 0.4 collective-permute-done.2
  10.4 1.6 %collective-permute-start.3 = (s32[2,144]{1,0:T(2,128)S(1)}, s32[2,144]{1,0:T(2,128)S(1)}, u32[]{:S(2)}, u32[]{:S(2)}) collective-permute-start(s32[2,144]{1,0:T(2,128)S(1)} %pad_add_fusion.1), channel_id=1, source_target_pairs={{0,2},{1,3},{2,0},{3,1},{4,6},{5,7},{6,4},{7,5},{8,10},{9,11},{10,... | collective-permute-start | bytes 3464 | tf_op jit(solution)/shard_map/ppermute | solution.py:641
  12.0 2.1 %collective-permute-done.3 = s32[2,144]{1,0:T(2,128)S(1)} collective-permute-done((s32[2,144]{1,0:T(2,128)S(1)}, s32[2,144]{1,0:T(2,128)S(1)}, u32[]{:S(2)}, u32[]{:S(2)}) %collective-permute-start.3) | collective-permute-done | bytes 1184 | tf_op jit(solution)/shard_map/ppermute | solution.py:641
  14.0 0.6 pad_add_fusion.ids_ref
  14.7 0.0 collective-permute-done.1
  14.7 0.0 copy-done.7
  14.7 0.7 %pad_maximum_fusion.raw_ref = f32[8,59,128]{2,1,0:T(8,128)} fusion(f32[4,59,128]{2,1,0:T(8,128)S(1)} %collective-permute-done.1, f32[2,59,128]{2,1,0:T(8,128)S(1)} %collective-permute-done, f32[2,59,128]{2,1,0:T(8,128)S(1)} %bitcast.39), kind=kLoop, calls=%fused_computation | loop fusion | flops 120832 | bytes 483328 | tf_op jit(solution)/shard_map/concatenate | solution.py:653
  15.4 0.0 copy-start.12
  15.4 0.0 copy-start
  15.4 0.0 copy-start.4
  15.4 2.2 %project.1 = (f32[36,128]{1,0:T(8,128)}, f32[36,128]{1,0:T(8,128)}, f32[36,128]{1,0:T(8,128)}, f32[36,128]{1,0:T(8,128)}) custom-call(s32[1]{0:T(128)} %bitcast.me_ref, f32[8,59,128]{2,1,0:T(8,128)} %pad_maximum_fusion.raw_ref, s32[4,144]{1,0:T(4,128)} %pad_add_fusion.ids_ref, f32[16,16]{1,0:T(8,128)} %cameras_ref.3, bf16[128,128]{1,0:T(8,128)(2,1)} %constant.24.clone.order_ref), custom_call_target="tpu_custom_call" | custom-call | tf_op jit(solution)/shard_map/project/pallas_call | solution.py:686
  17.6 0.0 copy-start.1
  17.6 1.5 %collective-permute-start.4 = (f32[36,128]{1,0:T(8,128)}, f32[36,128]{1,0:T(8,128)S(1)}, u32[]{:S(2)}, u32[]{:S(2)}) collective-permute-start(f32[36,128]{1,0:T(8,128)} %get-tuple-element.14), channel_id=1, source_target_pairs={{0,1},{1,0},{2,3},{3,2},{4,5},{5,4},{6,7},{7,6},{8,9},{9,8},{10,11... | collective-permute-start | bytes 55304 | tf_op jit(solution)/shard_map/ppermute | solution.py:641
  19.1 1.5 %collective-permute-start.5 = (f32[36,128]{1,0:T(8,128)}, f32[36,128]{1,0:T(8,128)S(1)}, u32[]{:S(2)}, u32[]{:S(2)}) collective-permute-start(f32[36,128]{1,0:T(8,128)} %get-tuple-element.15), channel_id=1, source_target_pairs={{0,2},{1,3},{2,0},{3,1},{4,6},{5,7},{6,4},{7,5},{8,10},{9,11},{10,... | collective-permute-start | bytes 55304 | tf_op jit(solution)/shard_map/ppermute | solution.py:641
  20.6 0.5 collective-permute-start.6
  21.8 0.0 copy-done.12
  21.8 0.0 copy-start.2
  21.8 0.0 collective-permute-done.4.src1
  21.8 1.3 %collective-permute-done.5.src2 = f32[36,128]{1,0:T(8,128)S(1)} collective-permute-done((f32[36,128]{1,0:T(8,128)}, f32[36,128]{1,0:T(8,128)S(1)}, u32[]{:S(2)}, u32[]{:S(2)}) %collective-permute-start.5) | collective-permute-done | bytes 18464 | tf_op jit(solution)/shard_map/ppermute | solution.py:641
  23.1 2.4 %collective-permute-done.6.src3 = f32[36,128]{1,0:T(8,128)S(1)} collective-permute-done((f32[36,128]{1,0:T(8,128)}, f32[36,128]{1,0:T(8,128)S(1)}, u32[]{:S(2)}, u32[]{:S(2)}) %collective-permute-start.6) | collective-permute-done | bytes 18464 | tf_op jit(solution)/shard_map/ppermute | solution.py:641
  25.5 0.0 copy-start.6
  25.5 0.0 copy-done
  25.5 0.0 copy-done.4
  25.5 0.0 copy-done.1
  25.5 0.0 copy-done.2
  25.6 0.6 copy-done.6
  26.2 0.0 copy-start.3
  26.2 0.7 %copy-done.3 = f32[36,128]{1,0:T(8,128)S(1)} copy-done((f32[36,128]{1,0:T(8,128)S(1)}, f32[36,128]{1,0:T(8,128)}, u32[]{:S(2)}) %copy-start.3) | copy-done | bytes 18456
  26.9 19.4 %render.1 = f32[16,16,128]{2,1,0:T(8,128)} custom-call(s32[1]{0:T(128)} %bitcast.me_ref, s32[1]{0:T(128)} %bitcast.30.cam_id_ref, s32[1]{0:T(128)} %bitcast.32.count_ref, s32[16]{0:T(128)S(1)} %bitcast.35, s32[16]{0:T(128)S(1)} %bitcast.36, f32[16,16]{1,0:T(8,128)S(1)} %copy-done.2, f32[36,128]{1,0:T(8,128)S(1)} %copy-done.3, ...), custom_call_target="tpu_custom_call" | custom-call | tf_op jit(solution)/shard_map/render/pallas_call | solution.py:696
  46.3 0.0 copy-start.10
  46.3 3.6 %all-to-all-start = ((f32[16,16,128]{2,1,0:T(8,128)}), f32[16,16,128]{2,1,0:T(8,128)S(1)}, u32[]{:S(2)}, u32[]{:S(2)}) async-start(f32[16,16,128]{2,1,0:T(8,128)} %render.1), calls=%async_computation | async-start | bytes 262144 | tf_op jit(solution)/shard_map/all_to_all | solution.py:725
  50.0 0.0 copy-start.13
  50.0 0.7 %copy-done.13 = s32[1,1,2,64]{3,2,1,0:T(2,128)S(1)} copy-done((s32[1,1,2,64]{3,2,1,0:T(2,128)S(1)}, s32[1,1,2,64]{3,2,1,0:T(2,128)}, u32[]{:S(2)}) %copy-start.13) | copy-done | bytes 536
  50.6 0.0 collective-permute-start.7
  50.6 0.0 copy-done.10
  50.6 0.0 copy-start.11
  50.6 0.6 %copy.35 = f32[1,2,59,128]{3,2,1,0:T(8,128)} copy(f32[1,2,59,128]{3,1,2,0:T(2,128)S(1)} %copy-done.10) | data formatting | bytes 120832 | tf_op args[1]
  51.3 0.2 copy-done.11
  51.5 0.6 copy.34
  52.1 0.0 collective-permute-done.7.refs_0_
  52.1 0.0 copy-start.14
  52.1 0.6 copy-done.14
  52.7 1.8 %prepare.1 = (f32[2,59,128]{2,1,0:T(8,128)}, f32[59,128]{1,0:T(8,128)}, bf16[1,256,256]{2,1,0:T(8,128)(2,1)}, f32[1,2,8,128]{3,2,1,0:T(8,128)}) custom-call(s32[1]{0:T(128)} %bitcast.9.group_ref, f32[2,59,128]{2,1,0:T(8,128)} %bitcast.40, f32[2,59,128]{2,1,0:T(8,128)} %bitcast.45, f32[2,59,128]{2,1,0:T(8,128)} %bitcast.42, f32[1,59]{1,0:T(1,128)} %bitcast.49, ...), custom_call_target="tpu_custom_call" | custom-call | tf_op jit(solution)/shard_map/prepare/pallas_call | solution.py:673
  54.5 3.2 %all-to-all-done = f32[16,16,128]{2,1,0:T(8,128)S(1)} async-done(((f32[16,16,128]{2,1,0:T(8,128)}), f32[16,16,128]{2,1,0:T(8,128)S(1)}, u32[]{:S(2)}, u32[]{:S(2)}) %all-to-all-start) | async-done | bytes 131104 | tf_op jit(solution)/shard_map/all_to_all | solution.py:725
  57.7 0.0 copy-start.8
  57.7 0.7 %copy-done.8 = f32[16,16,128]{2,1,0:T(8,128)} copy-done((f32[16,16,128]{2,1,0:T(8,128)}, f32[16,16,128]{2,1,0:T(8,128)S(1)}, u32[]{:S(2)}) %copy-start.8) | copy-done | bytes 131096
  58.4 2.3 %owner.1 = (f32[2,59,128]{2,1,0:T(8,128)}, f32[2,59,128]{2,1,0:T(8,128)}, f32[1,2,59,128]{3,2,1,0:T(8,128)}) custom-call(f32[256,128]{1,0:T(8,128)} %bitcast.44, f32[2,59,128]{2,1,0:T(8,128)} %bitcast.41, f32[2,59,128]{2,1,0:T(8,128)} %get-tuple-element.17.base_ref, f32[2,59,128]{2,1,0:T(8,128)} %bitcast.43, f32[59,128]{1,0:T(8,128)} %get-tuple-element.18.steps_ref, ...), custom_call_target="tpu_custom_call" | custom-call | tf_op jit(solution)/shard_map/owner/pallas_call | solution.py:726
  60.7 0.0 collective-permute-start.8
  60.7 0.7 %slice_compare_fusion = pred[1,2,1,128]{3,2,1,0:T(4,128)(4,1)S(1)} fusion(f32[1,2,8,128]{3,2,1,0:T(8,128)} %get-tuple-element.21), kind=kLoop, calls=%fused_computation.10 | loop fusion | flops 256 | bytes 1280 | tf_op jit(solution)/shard_map/gt | solution.py:742
  61.4 0.0 copy-start.9
  61.4 1.5 %copy.25 = f32[1,2,59,128]{3,1,2,0:T(2,128)} copy(f32[1,2,59,128]{3,2,1,0:T(8,128)} %bitcast.46) | data formatting | bytes 120832
  63.0 0.0 collective-permute-done.8
  63.0 0.0 copy-done.9
  63.0 0.7 %copy.26 = f32[1,2,59,128]{3,1,2,0:T(2,128)} copy(f32[1,2,59,128]{3,2,1,0:T(8,128)S(1)} %select_bitcast_fusion) | data formatting | bytes 120832
  (6 shorter events, 0.1 us)
Async XLA Ops:
  1.5 13.2 %copy-start.7 = (f32[1,2,59,128]{3,2,1,0:T(8,128)}, f32[1,2,59,128]{3,2,1,0:T(8,128)S(1)}, u32[]{:S(2)}) copy-start(f32[1,2,59,128]{3,2,1,0:T(8,128)S(1)} %copy.36) | copy-start | bytes 181252
  1.5 7.7 %collective-permute-start = (f32[2,59,128]{2,1,0:T(8,128)S(1)}, f32[2,59,128]{2,1,0:T(8,128)S(1)}, u32[]{:S(2)}, u32[]{:S(2)}) collective-permute-start(f32[2,59,128]{2,1,0:T(8,128)S(1)} %bitcast.37), channel_id=1, source_target_pairs={{0,8},{1,9},{2,10},{3,11},{4,12},{5,13},{6,14},{7,15},{8,0},{9,1},... | collective-permute-start | bytes 181256 | tf_op jit(solution)/shard_map/ppermute | solution.py:641
  6.2 0.7 %copy-start.5 = (s32[1,1,16]{2,1,0:T(1,128)S(1)}, s32[1,1,16]{2,1,0:T(1,128)}, u32[]{:S(2)}) copy-start(s32[1,1,16]{2,1,0:T(1,128)} %param.21) | copy-start | bytes 196
  6.8 3.6 %collective-permute-start.2 = (s32[1,144]{1,0:T(1,128)S(1)}, s32[1,144]{1,0:T(1,128)S(1)}, u32[]{:S(2)}, u32[]{:S(2)}) collective-permute-start(s32[1,144]{1,0:T(1,128)S(1)} %concatenate.19), channel_id=1, source_target_pairs={{0,1},{1,0},{2,3},{3,2},{4,5},{5,4},{6,7},{7,6},{8,9},{9,8},{10,11... | collective-permute-start | bytes 1736 | tf_op jit(solution)/shard_map/ppermute | solution.py:641
  9.2 5.5 %collective-permute-start.1 = (f32[4,59,128]{2,1,0:T(8,128)S(1)}, f32[4,59,128]{2,1,0:T(8,128)S(1)}, u32[]{:S(2)}, u32[]{:S(2)}) collective-permute-start(f32[4,59,128]{2,1,0:T(8,128)S(1)} %pad_maximum_fusion.1), channel_id=1, source_target_pairs={{0,4},{1,5},{2,6},{3,7},{4,0},{5,1},{6,2},{7,3},{8,12},{9,13},{10,... | collective-permute-start | bytes 362504 | tf_op jit(solution)/shard_map/ppermute | solution.py:641
  10.4 3.7 %collective-permute-start.3 = (s32[2,144]{1,0:T(2,128)S(1)}, s32[2,144]{1,0:T(2,128)S(1)}, u32[]{:S(2)}, u32[]{:S(2)}) collective-permute-start(s32[2,144]{1,0:T(2,128)S(1)} %pad_add_fusion.1), channel_id=1, source_target_pairs={{0,2},{1,3},{2,0},{3,1},{4,6},{5,7},{6,4},{7,5},{8,10},{9,11},{10,... | collective-permute-start | bytes 3464 | tf_op jit(solution)/shard_map/ppermute | solution.py:641
  15.4 6.4 %copy-start.12 = (f32[1,1,3,1024]{3,1,2,0:T(1,128)S(1)}, f32[1,1,3,1024]{3,1,2,0:T(1,128)}, u32[]{:S(2)}) copy-start(f32[1,1,3,1024]{3,1,2,0:T(1,128)} %param.24) | copy-start | bytes 36868
  15.4 10.1 %copy-start = (bf16[48,1408]{1,0:T(8,128)(2,1)S(1)}, bf16[48,1408]{1,0:T(8,128)(2,1)}, u32[]{:S(2)}) copy-start(bf16[48,1408]{1,0:T(8,128)(2,1)} %constant.22.clone.basis_ref) | copy-start | bytes 405508
  15.4 10.1 %copy-start.4 = (bf16[32,128]{1,0:T(8,128)(2,1)S(1)}, bf16[32,128]{1,0:T(8,128)(2,1)}, u32[]{:S(2)}) copy-start(bf16[32,128]{1,0:T(8,128)(2,1)} %constant.23.clone.xmom_ref) | copy-start | bytes 24580
  17.6 7.9 %copy-start.1 = (bf16[128,128]{1,0:T(8,128)(2,1)S(1)}, bf16[128,128]{1,0:T(8,128)(2,1)}, u32[]{:S(2)}) copy-start(bf16[128,128]{1,0:T(8,128)(2,1)} %constant.25.clone.back_ref) | copy-start | bytes 98308
  17.6 4.2 %collective-permute-start.4 = (f32[36,128]{1,0:T(8,128)}, f32[36,128]{1,0:T(8,128)S(1)}, u32[]{:S(2)}, u32[]{:S(2)}) collective-permute-start(f32[36,128]{1,0:T(8,128)} %get-tuple-element.14), channel_id=1, source_target_pairs={{0,1},{1,0},{2,3},{3,2},{4,5},{5,4},{6,7},{7,6},{8,9},{9,8},{10,11... | collective-permute-start | bytes 55304 | tf_op jit(solution)/shard_map/ppermute | solution.py:641
  19.1 4.0 %collective-permute-start.5 = (f32[36,128]{1,0:T(8,128)}, f32[36,128]{1,0:T(8,128)S(1)}, u32[]{:S(2)}, u32[]{:S(2)}) collective-permute-start(f32[36,128]{1,0:T(8,128)} %get-tuple-element.15), channel_id=1, source_target_pairs={{0,2},{1,3},{2,0},{3,1},{4,6},{5,7},{6,4},{7,5},{8,10},{9,11},{10,... | collective-permute-start | bytes 55304 | tf_op jit(solution)/shard_map/ppermute | solution.py:641
  20.6 4.9 %collective-permute-start.6 = (f32[36,128]{1,0:T(8,128)}, f32[36,128]{1,0:T(8,128)S(1)}, u32[]{:S(2)}, u32[]{:S(2)}) collective-permute-start(f32[36,128]{1,0:T(8,128)} %get-tuple-element.16), channel_id=1, source_target_pairs={{0,3},{1,2},{2,1},{3,0},{4,7},{5,6},{6,5},{7,4},{8,11},{9,10},{10,... | collective-permute-start | bytes 55304 | tf_op jit(solution)/shard_map/ppermute | solution.py:641
  21.8 3.8 %copy-start.2 = (f32[16,16]{1,0:T(8,128)S(1)}, f32[16,16]{1,0:T(8,128)}, u32[]{:S(2)}) copy-start(f32[16,16]{1,0:T(8,128)} %cameras_ref.3) | copy-start | bytes 3076
  25.5 0.7 %copy-start.6 = (s32[1,1,16]{2,1,0:T(1,128)S(1)}, s32[1,1,16]{2,1,0:T(1,128)}, u32[]{:S(2)}) copy-start(s32[1,1,16]{2,1,0:T(1,128)} %param.22) | copy-start | bytes 196
  26.2 0.7 %copy-start.3 = (f32[36,128]{1,0:T(8,128)S(1)}, f32[36,128]{1,0:T(8,128)}, u32[]{:S(2)}) copy-start(f32[36,128]{1,0:T(8,128)} %get-tuple-element.13.src0) | copy-start | bytes 55300
  46.3 4.3 %copy-start.10 = (f32[1,2,59,128]{3,1,2,0:T(2,128)S(1)}, f32[1,2,59,128]{3,1,2,0:T(2,128)}, u32[]{:S(2)}) copy-start(f32[1,2,59,128]{3,1,2,0:T(2,128)} %param.16) | copy-start | bytes 181252
  46.3 11.4 %all-to-all-start = ((f32[16,16,128]{2,1,0:T(8,128)}), f32[16,16,128]{2,1,0:T(8,128)S(1)}, u32[]{:S(2)}, u32[]{:S(2)}) async-start(f32[16,16,128]{2,1,0:T(8,128)} %render.1), calls=%async_computation | async-start | bytes 262144 | tf_op jit(solution)/shard_map/all_to_all | solution.py:725
  50.0 0.7 %copy-start.13 = (s32[1,1,2,64]{3,2,1,0:T(2,128)S(1)}, s32[1,1,2,64]{3,2,1,0:T(2,128)}, u32[]{:S(2)}) copy-start(s32[1,1,2,64]{3,2,1,0:T(2,128)} %param.25) | copy-start | bytes 1540
  50.6 1.5 %collective-permute-start.7 = (s32[2,64]{1,0:T(2,128)S(1)}, s32[2,64]{1,0:T(2,128)S(1)}, u32[]{:S(2)}, u32[]{:S(2)}) collective-permute-start(s32[2,64]{1,0:T(2,128)S(1)} %bitcast.48), channel_id=1, source_target_pairs={{0,16},{16,0},{1,17},{17,1},{2,18},{18,2},{3,19},{19,3},{4,20},{20... | collective-permute-start | bytes 1544 | tf_op jit(solution)/shard_map/ppermute | solution.py:671
  50.6 0.8 %copy-start.11 = (f32[1,2,59,128]{3,1,2,0:T(2,128)S(1)}, f32[1,2,59,128]{3,1,2,0:T(2,128)}, u32[]{:S(2)}) copy-start(f32[1,2,59,128]{3,1,2,0:T(2,128)} %param.17) | copy-start | bytes 181252
  52.1 0.6 copy-start.14
  57.7 0.7 %copy-start.8 = (f32[16,16,128]{2,1,0:T(8,128)}, f32[16,16,128]{2,1,0:T(8,128)S(1)}, u32[]{:S(2)}) copy-start(f32[16,16,128]{2,1,0:T(8,128)S(1)} %all-to-all-done) | copy-start | bytes 393220
  60.7 2.3 %collective-permute-start.8 = (f32[2,59,128]{2,1,0:T(8,128)}, f32[2,59,128]{2,1,0:T(8,128)S(1)}, u32[]{:S(2)}, u32[]{:S(2)}) collective-permute-start(f32[2,59,128]{2,1,0:T(8,128)} %bitcast.51), channel_id=1, source_target_pairs={{0,16},{16,0},{1,17},{17,1},{2,18},{18,2},{3,19},{19,3},{4,20},{20... | collective-permute-start | bytes 181256 | tf_op jit(solution)/shard_map/ppermute | solution.py:740
  61.4 1.6 %copy-start.9 = (f32[2,59,128]{2,1,0:T(8,128)S(1)}, f32[2,59,128]{2,1,0:T(8,128)}, u32[]{:S(2)}) copy-start(f32[2,59,128]{2,1,0:T(8,128)} %get-tuple-element.22) | copy-start | bytes 181252

commit v3 on v2

--- a/solution.py
+++ b/solution.py
@@ -148,18 +148,13 @@
     links, group_ref, own_ref, cons_ref, dual_ref, step_ref, share_ref, *refs
 ):
     others, (base_ref, steps_ref, pick_ref, mask_ref) = refs[: len(links)], refs[len(links) :]
-    blocks, params = own_ref.shape[0], own_ref.shape[1]
+    params, blocks = own_ref.shape[0], own_ref.shape[1]
     group = group_ref[0]
-    shape = (params, params)
-    diagonal = lax.broadcasted_iota(jnp.int32, shape, 0) == lax.broadcasted_iota(jnp.int32, shape, 1)
-    steps = jnp.sum(
-        jnp.where(diagonal, jnp.broadcast_to(step_ref[...], shape), 0.0), axis=1, keepdims=True
-    )
-    steps = jnp.broadcast_to(steps, (params, LANES))
-    steps_ref[...] = steps
-    for b in range(blocks):
-        here = own_ref[b]
-        base_ref[b] = here - steps * (penalty_weight * (here - cons_ref[b] + dual_ref[b]))
+    for p in range(params):
+        step = step_ref[p]
+        here = own_ref[p]
+        steps_ref[p] = jnp.full((blocks, LANES), step)
+        base_ref[p] = here - step * (penalty_weight * (here - cons_ref[p] + dual_ref[p]))
     half = share_ref.shape[1]
     local = lax.broadcasted_iota(jnp.int32, (blocks * LANES, half), 0)
     contract = (((1,), (1,)), ((), ()))
@@ -176,13 +171,13 @@
         there = jnp.full((SUB, half), jnp.where(exists_of(group), 1.0, 0.0)).astype(jnp.bfloat16)
         mask = lax.dot_general(there, source, contract, preferred_element_type=jnp.float32)
         for b in range(blocks):
-            mask_ref[n, b] = mask[:, b * LANES : (b + 1) * LANES]
+            mask_ref[n, b : b + 1, :] = mask[0:1, b * LANES : (b + 1) * LANES]
 
 
 def project_kernel(masks, yrows, me_ref, raw_ref, ids_ref, cameras_ref, order_ref, *refs):
     outs, feat = refs[:INNER], refs[INNER]
     outer = len(masks)
-    blocks = raw_ref.shape[0] // outer
+    blocks = raw_ref.shape[2]
     me = me_ref[0]
     ids = jnp.concatenate([ids_ref[...]] * (SUB // INNER), axis=0)
     lane = lax.broadcasted_iota(jnp.int32, (SUB, LANES), 1)
@@ -206,8 +201,8 @@
             def of(b):
                 return jnp.where(
                     sub < INNER,
-                    jnp.broadcast_to(raw_ref[owners[0] * blocks + b, p : p + 1, :], (SUB, LANES)),
-                    jnp.broadcast_to(raw_ref[owners[1] * blocks + b, p : p + 1, :], (SUB, LANES)),
+                    jnp.broadcast_to(raw_ref[owners[0], p, b : b + 1, :], (SUB, LANES)),
+                    jnp.broadcast_to(raw_ref[owners[1], p, b : b + 1, :], (SUB, LANES)),
                 )
 
             value = of(0)
@@ -443,10 +438,10 @@
 
 
 def owner_kernel(
-    inbox_ref, own_ref, base_ref, dual_ref, steps_ref, pick_ref, new_ref, shifted_ref, sent_ref, grad
+    inbox_ref, own_ref, base_ref, dual_ref, steps_ref, pick_ref, new_ref, shifted_ref, sent_ref,
+    grad, moved
 ):
-    blocks = own_ref.shape[0]
-    params = own_ref.shape[1]
+    params, blocks = own_ref.shape[0], own_ref.shape[1]
     strips = inbox_ref.shape[0] // MSG
 
     def message(m):
@@ -457,9 +452,9 @@
     place, top = cam[16], cam[17]
 
     def row(p):
-        value = jnp.broadcast_to(own_ref[0, p : p + 1, :], (strips, LANES))
+        value = jnp.broadcast_to(own_ref[p, 0:1, :], (strips, LANES))
         for b in range(1, blocks):
-            value = jnp.where(place == b, own_ref[b, p : p + 1, :], value)
+            value = jnp.where(place == b, own_ref[p, b : b + 1, :], value)
         return value
 
     geo = geometry(row, cam)
@@ -564,22 +559,26 @@
     for b in range(blocks):
         mine = place == b
         for p in range(params):
-            grad[b, p : p + 1, :] = jnp.sum(
+            grad[p * blocks + b : p * blocks + b + 1, :] = jnp.sum(
                 jnp.where(mine, grads[p], 0.0), axis=0, keepdims=True
             )
 
-    parts = []
-    for b in range(blocks):
-        new = base_ref[b] - steps_ref[...] * grad[b, :params, :]
-        shifted = new + dual_ref[b]
-        new_ref[b] = new
-        shifted_ref[b] = shifted
-        parts.append(shifted)
-    shifted = jnp.concatenate(parts, axis=1)
+    for p in range(params):
+        here = slice(p * blocks, (p + 1) * blocks)
+        new = base_ref[p] - steps_ref[p] * grad[here, :]
+        shifted = new + dual_ref[p]
+        new_ref[p] = new
+        shifted_ref[p] = shifted
+        moved[here, :] = shifted
+    shifted = jnp.concatenate(
+        [moved[pl.ds(b, params, stride=blocks), :] for b in range(blocks)], axis=1
+    )
     for n in range(pick_ref.shape[0]):
         value = exact_pick(shifted, pick_ref[n])
         for b in range(blocks):
-            sent_ref[n, b] = value[:, b * LANES : (b + 1) * LANES]
+            moved[pl.ds(b, params, stride=blocks), :] = value[:, b * LANES : (b + 1) * LANES]
+        for p in range(params):
+            sent_ref[n, p] = moved[p * blocks : (p + 1) * blocks, :]
 
 
 def constants(pixels):
@@ -625,8 +624,8 @@
     gaussians, consensus, duals, step_sizes, cameras, camera_ids, block_lists, depth_order,
     block_counts, targets, intersection,
 ):
-    own = gaussians[0]
-    blocks, params = own.shape[0], own.shape[1]
+    own, prior, dual = [value[0].swapaxes(0, 1) for value in (gaussians, consensus, duals)]
+    params, blocks = own.shape[0], own.shape[1]
     peers = lax.axis_size("tile")
     me = lax.axis_index("tile")[None]
     listed = block_lists.shape[2]
@@ -644,7 +643,7 @@
     ids = jnp.concatenate(
         [jnp.broadcast_to(camera_ids, (1, LANES)), block_lists[0]], axis=1
     )
-    everything = own
+    everything = own[None]
     masks = [0]
     for step, bit in enumerate(hop_bits):
         arrived = swap(everything, 1 << bit)
@@ -674,14 +673,15 @@
         functools.partial(prepare_kernel, links),
         out_shape=(
             shape_of(own.shape, f32),
-            shape_of((params, LANES), f32),
+            shape_of(own.shape, f32),
             shape_of((len(links), blocks * LANES, blocks * LANES), jnp.bfloat16),
-            shape_of((len(links), blocks, SUB, LANES), f32),
+            shape_of((len(links), blocks, LANES), f32),
         ),
-        in_specs=smem() + vmem(5 + len(links)),
+        in_specs=smem() + vmem(3) + smem() + vmem(1 + len(links)),
         out_specs=tuple(vmem(4)),
+        compiler_params=params_with(8),
         name="prepare",
-    )(group, own, consensus[0], duals[0], step_sizes[None, :], share, *lists)
+    )(group, own, prior, dual, step_sizes, share, *lists)
 
     messages = pl.pallas_call(
         functools.partial(project_kernel, masks, yrows),
@@ -689,6 +689,7 @@
         in_specs=smem() + vmem(4),
         out_specs=tuple(vmem(INNER)),
         scratch_shapes=[pltpu.VMEM((COEFS * outer * INNER, LANES), f32)],
+        compiler_params=params_with(8),
         name="project",
     )(me, everything, ids, cameras, order)
     sources = [messages[0]] + [swap(messages[j], j) for j in range(1, INNER)]
@@ -732,15 +733,16 @@
         ),
         in_specs=vmem(6),
         out_specs=tuple(vmem(3)),
-        scratch_shapes=[pltpu.VMEM((blocks, params + 5, LANES), f32)],
+        scratch_shapes=[pltpu.VMEM((params * blocks, LANES), f32)] * 2,
+        compiler_params=params_with(16),
         name="owner",
-    )(inbox.reshape(peers * MSG, LANES), own, base, duals[0], steps, pick)
+    )(inbox.reshape(peers * MSG, LANES), own, base, dual, steps, pick)
     new_duals = jnp.zeros_like(shifted)
     for n, route in enumerate(routes):
         theirs = lax.ppermute(sent[n], "scene", route)
         change = shifted - 0.5 * (shifted + theirs)
-        new_duals = jnp.where(mask[n, :, :1, :] > 0.5, change, new_duals)
-    return updated[None], new_duals[None]
+        new_duals = jnp.where(mask[n] > 0.5, change, new_duals)
+    return updated.swapaxes(0, 1)[None], new_duals.swapaxes(0, 1)[None]
 
 
 def solution(mesh):

time: 64.7 us -> 58.9 us (0.910); the launches traced: 63.7 us -> 58.5 us
  Pallas kernels: 25.8 us -> 10 us
  starting transfers between devices: 15.1 us -> 28.7 us
  local copies, waits for them, and re-layouts: 8.5 us -> 3.27 us
  waiting for transfers between devices: 10.3 us -> 12.8 us
    all_to_all x1, starting transfers between devices: 3.64 us -> 16.5 us  [on_device(): lax.all_to_all(outbox, 'tile', split_axis=0, concat_axis=0, tiled=True)]
    pallas_call x1, Pallas kernels: 19.4 us -> 7.44 us  [on_device(): pl.pallas_call(functools.partial(render_kernel, pixels, blocks, hop_bits)...]
    unnamed x37 -> x27, local copies, waits for them, and re-layouts: 8.49 us -> 3.26 us
    pallas_call x1, Pallas kernels: 2.23 us -> 0.63 us  [on_device(): pl.pallas_call(functools.partial(project_kernel, masks, yrows), out_shape...]
    all_to_all x1, waiting for transfers between devices: 3.22 us -> 4.49 us  [on_device(): lax.all_to_all(outbox, 'tile', split_axis=0, concat_axis=0, tiled=True)]
    ppermute x1, waiting for transfers between devices: 0.01 us -> 1.24 us  [on_device(): theirs = lax.ppermute(sent[n], 'scene', route)]
    pallas_call x1, Pallas kernels: 2.34 us -> 1.16 us  [on_device(): pl.pallas_call(owner_kernel, out_shape=(shape_of(own.shape, f32), shape_o...]
    ppermute x1, waiting for transfers between devices: 0.01 us -> 1.14 us  [on_device(): lists = [lax.ppermute(share, 'scene', route) for route in routes]]
  transfers between devices with their start and end apart: 10 -> 10, of which waited for: 6 -> 7; matrix products, arithmetic and copies ran while one was open for 7% -> 2% of each run, Pallas kernels for 3% -> 1%
where the time goes in v3:
time: 58.9 us; the launch traced here: 58.5 us
  starting transfers between devices  28.7 us (49%)
  waiting for transfers between devices  12.8 us (22%)
  Pallas kernels  10 us (17%)
  local copies, waits for them, and re-layouts  3.27 us (6%)
  between operations  2.08 us (4%)
  other arithmetic  1.69 us (3%)
    all_to_all x1, starting transfers between devices, on_device(): lax.all_to_all(outbox, 'tile', split_axis=0, concat_axis=0, tiled=True)  16.5 us
    ppermute x7, starting transfers between devices, swap(): return lax.ppermute(value, 'tile', [(i, i ^ mask) for i in range(peers)])  12.1 us
    pallas_call x1, Pallas kernels, on_device(): pl.pallas_call(functools.partial(render_kernel, pixels, blocks, hop_bits)...  7.44 us
    ppermute x7, waiting for transfers between devices, swap(): return lax.ppermute(value, 'tile', [(i, i ^ mask) for i in range(peers)])  5.91 us
    all_to_all x1, waiting for transfers between devices, on_device(): lax.all_to_all(outbox, 'tile', split_axis=0, concat_axis=0, tiled=True)  4.49 us
    unnamed x27, local copies, waits for them, and re-layouts  3.26 us
    ppermute x1, waiting for transfers between devices, on_device(): theirs = lax.ppermute(sent[n], 'scene', route)  1.24 us
  transfers between devices with their start and end apart: 10, of which 7 were waited for; matrix products, arithmetic and copies ran while one was open for 2% of the time, Pallas kernels for 1%

profile of v3, /device:TPU:0, one launch (start us, length us, event | category | flops | bytes accessed | tf_op | source)
XLA Modules:
  0.0 58.5 jit_solution(7303271360639690991)
XLA Ops:
  0.6 4.1 %collective-permute-start = (f32[1,59,2,128]{3,2,1,0:T(2,128)}, f32[1,59,2,128]{3,2,1,0:T(2,128)S(1)}, u32[]{:S(2)}, u32[]{:S(2)}) collective-permute-start(f32[1,59,2,128]{3,2,1,0:T(2,128)} %bitcast.37), channel_id=1, source_target_pairs={{0,8},{1,9},{2,10},{3,11},{4,12},{5,13},{6,14},{7,15},{8,0},{9,1},... | collective-permute-start | bytes 181256 | tf_op jit(solution)/shard_map/ppermute | solution.py:640
  5.4 0.0 copy-start.8
  5.4 0.6 %copy-done.8 = s32[1,1,16]{2,1,0:T(1,128)S(1)} copy-done((s32[1,1,16]{2,1,0:T(1,128)S(1)}, s32[1,1,16]{2,1,0:T(1,128)}, u32[]{:S(2)}) %copy-start.8) | copy-done | bytes 88
  6.0 0.0 copy-start
  6.0 1.5 %collective-permute-start.2 = (s32[1,144]{1,0:T(1,128)S(1)}, s32[1,144]{1,0:T(1,128)S(1)}, u32[]{:S(2)}, u32[]{:S(2)}) collective-permute-start(s32[1,144]{1,0:T(1,128)S(1)} %concatenate.19), channel_id=1, source_target_pairs={{0,1},{1,0},{2,3},{3,2},{4,5},{5,4},{6,7},{7,6},{8,9},{9,8},{10,11... | collective-permute-start | bytes 1736 | tf_op jit(solution)/shard_map/ppermute | solution.py:640
  7.5 0.2 collective-permute-done
  7.8 0.9 %pad_maximum_fusion.1 = f32[2,59,2,128]{3,2,1,0:T(2,128)S(1)} fusion(f32[1,59,2,128]{3,2,1,0:T(2,128)S(1)} %collective-permute-done, f32[1,59,2,128]{3,2,1,0:T(2,128)} %bitcast.38), kind=kLoop, calls=%fused_computation.1 | loop fusion | flops 30208 | bytes 241664 | tf_op jit(solution)/shard_map/concatenate | solution.py:652
  8.7 1.4 %collective-permute-start.1 = (f32[2,59,2,128]{3,2,1,0:T(2,128)S(1)}, f32[2,59,2,128]{3,2,1,0:T(2,128)S(1)}, u32[]{:S(2)}, u32[]{:S(2)}) collective-permute-start(f32[2,59,2,128]{3,2,1,0:T(2,128)S(1)} %pad_maximum_fusion.1), channel_id=1, source_target_pairs={{0,4},{1,5},{2,6},{3,7},{4,0},{5,1},{6,2},{7,3},{8,12},{9,13},{10,... | collective-permute-start | bytes 362504 | tf_op jit(solution)/shard_map/ppermute | solution.py:640
  10.1 0.0 collective-permute-done.2
  10.1 1.6 %collective-permute-start.3 = (s32[2,144]{1,0:T(2,128)S(1)}, s32[2,144]{1,0:T(2,128)S(1)}, u32[]{:S(2)}, u32[]{:S(2)}) collective-permute-start(s32[2,144]{1,0:T(2,128)S(1)} %pad_add_fusion.1), channel_id=1, source_target_pairs={{0,2},{1,3},{2,0},{3,1},{4,6},{5,7},{6,4},{7,5},{8,10},{9,11},{10,... | collective-permute-start | bytes 3464 | tf_op jit(solution)/shard_map/ppermute | solution.py:640
  11.7 2.1 %collective-permute-done.3 = s32[2,144]{1,0:T(2,128)S(1)} collective-permute-done((s32[2,144]{1,0:T(2,128)S(1)}, s32[2,144]{1,0:T(2,128)S(1)}, u32[]{:S(2)}, u32[]{:S(2)}) %collective-permute-start.3) | collective-permute-done | bytes 1184 | tf_op jit(solution)/shard_map/ppermute | solution.py:640
  13.7 0.0 copy-start.5
  13.8 0.0 copy-start.6
  13.8 0.0 collective-permute-done.1
  13.8 0.0 copy-done
  13.8 0.1 pad_maximum_fusion.raw_ref
  13.9 0.6 %copy-done.5 = bf16[128,128]{1,0:T(8,128)(2,1)S(1)} copy-done((bf16[128,128]{1,0:T(8,128)(2,1)S(1)}, bf16[128,128]{1,0:T(8,128)(2,1)}, u32[]{:S(2)}) %copy-start.5) | copy-done | bytes 32792
  14.5 0.0 copy-done.6
  14.5 0.0 copy-start.12
  14.5 0.0 copy-start.2
  14.5 0.6 %project.1 = (f32[36,128]{1,0:T(8,128)S(1)}, f32[36,128]{1,0:T(8,128)S(1)}, f32[36,128]{1,0:T(8,128)S(1)}, f32[36,128]{1,0:T(8,128)S(1)}) custom-call(s32[1]{0:T(128)} %bitcast.me_ref, f32[4,59,2,128]{3,2,1,0:T(2,128)S(1)} %pad_maximum_fusion.raw_ref, s32[4,144]{1,0:T(4,128)S(1)} %pad_add_fusion.ids_ref, f32[16,16]{1,0:T(8,128)S(1)} %copy-done.6, ...), custom_call_target="tpu_custom_call" | custom-call | tf_op jit(solution)/shard_map/project/pallas_call | solution.py:686
  15.1 0.0 copy-start.4
  15.2 1.7 %collective-permute-start.4 = (f32[36,128]{1,0:T(8,128)S(1)}, f32[36,128]{1,0:T(8,128)S(1)}, u32[]{:S(2)}, u32[]{:S(2)}) collective-permute-start(f32[36,128]{1,0:T(8,128)S(1)} %get-tuple-element.14), channel_id=1, source_target_pairs={{0,1},{1,0},{2,3},{3,2},{4,5},{5,4},{6,7},{7,6},{8,9},{9,8},{10,11... | collective-permute-start | bytes 55304 | tf_op jit(solution)/shard_map/ppermute | solution.py:640
  16.8 1.5 %collective-permute-start.5 = (f32[36,128]{1,0:T(8,128)S(1)}, f32[36,128]{1,0:T(8,128)S(1)}, u32[]{:S(2)}, u32[]{:S(2)}) collective-permute-start(f32[36,128]{1,0:T(8,128)S(1)} %get-tuple-element.15), channel_id=1, source_target_pairs={{0,2},{1,3},{2,0},{3,1},{4,6},{5,7},{6,4},{7,5},{8,10},{9,11},{10,... | collective-permute-start | bytes 55304 | tf_op jit(solution)/shard_map/ppermute | solution.py:640
  18.3 0.4 collective-permute-start.6
  19.4 0.0 copy-done.12
  19.4 0.0 copy-start.7
  19.4 0.0 collective-permute-done.4.src1
  19.4 1.2 %collective-permute-done.5.src2 = f32[36,128]{1,0:T(8,128)S(1)} collective-permute-done((f32[36,128]{1,0:T(8,128)S(1)}, f32[36,128]{1,0:T(8,128)S(1)}, u32[]{:S(2)}, u32[]{:S(2)}) %collective-permute-start.5) | collective-permute-done | bytes 18464 | tf_op jit(solution)/shard_map/ppermute | solution.py:640
  20.6 2.4 %collective-permute-done.6.src3 = f32[36,128]{1,0:T(8,128)S(1)} collective-permute-done((f32[36,128]{1,0:T(8,128)S(1)}, f32[36,128]{1,0:T(8,128)S(1)}, u32[]{:S(2)}, u32[]{:S(2)}) %collective-permute-start.6) | collective-permute-done | bytes 18464 | tf_op jit(solution)/shard_map/ppermute | solution.py:640
  23.0 0.0 copy-start.10
  23.0 0.0 copy-done.2
  23.0 0.0 copy-done.4
  23.0 0.0 copy-done.7
  23.0 0.6 %copy-done.10 = s32[1,1,16]{2,1,0:T(1,128)S(1)} copy-done((s32[1,1,16]{2,1,0:T(1,128)S(1)}, s32[1,1,16]{2,1,0:T(1,128)}, u32[]{:S(2)}) %copy-start.10) | copy-done | bytes 88
  23.7 7.4 %render.1 = f32[16,16,128]{2,1,0:T(8,128)} custom-call(s32[1]{0:T(128)} %bitcast.me_ref, s32[1]{0:T(128)} %bitcast.34.cam_id_ref, s32[1]{0:T(128)} %bitcast.36.count_ref, s32[16]{0:T(128)S(1)} %bitcast.48, s32[16]{0:T(128)S(1)} %bitcast.51, f32[16,16]{1,0:T(8,128)S(1)} %copy-done.6, f32[36,128]{1,0:T(8,128)S(1)} %get-tuple-element.13.src0, ...), custom_call_target="tpu_custom_call" | custom-call | tf_op jit(solution)/shard_map/render/pallas_call | solution.py:697
  31.1 0.0 copy-start.1
  31.1 0.0 copy-start.3
  31.1 16.5 %all-to-all-start = ((f32[16,16,128]{2,1,0:T(8,128)}), f32[16,16,128]{2,1,0:T(8,128)S(1)}, u32[]{:S(2)}, u32[]{:S(2)}) async-start(f32[16,16,128]{2,1,0:T(8,128)} %render.1), calls=%async_computation | async-start | bytes 262144 | tf_op jit(solution)/shard_map/all_to_all | solution.py:726
  47.7 0.0 copy-start.9
  47.7 0.7 %copy-done.9 = s32[1,1,2,64]{3,2,1,0:T(2,128)S(1)} copy-done((s32[1,1,2,64]{3,2,1,0:T(2,128)S(1)}, s32[1,1,2,64]{3,2,1,0:T(2,128)}, u32[]{:S(2)}) %copy-start.9) | copy-done | bytes 536
  48.4 0.0 collective-permute-start.7
  48.4 1.1 %collective-permute-done.7.refs_0_ = s32[2,64]{1,0:T(2,128)S(1)} collective-permute-done((s32[2,64]{1,0:T(2,128)S(1)}, s32[2,64]{1,0:T(2,128)S(1)}, u32[]{:S(2)}, u32[]{:S(2)}) %collective-permute-start.7) | collective-permute-done | bytes 544 | tf_op jit(solution)/shard_map/ppermute | solution.py:670
  49.5 0.0 copy-start.11
  49.5 0.0 copy-done.1
  49.5 0.0 copy-done.3
  49.5 0.6 %copy-done.11 = f32[59]{0:T(128)S(1)} copy-done((f32[59]{0:T(128)S(1)}, f32[59]{0:T(128)}, u32[]{:S(2)}) %copy-start.11) | copy-done | bytes 260
  50.2 0.8 %prepare.1 = (f32[59,2,128]{2,1,0:T(2,128)S(1)}, f32[59,2,128]{2,1,0:T(2,128)S(1)}, bf16[1,256,256]{2,1,0:T(8,128)(2,1)S(1)}, f32[1,2,128]{2,1,0:T(2,128)S(1)}) custom-call(s32[1]{0:T(128)} %bitcast.13.group_ref, f32[59,2,128]{2,1,0:T(2,128)S(1)} %bitcast.40, f32[59,2,128]{2,1,0:T(2,128)S(1)} %bitcast.46, f32[59,2,128]{2,1,0:T(2,128)S(1)} %bitcast.43, ...), custom_call_target="tpu_custom_call" | custom-call | tf_op jit(solution)/shard_map/prepare/pallas_call | solution.py:672
  51.0 4.5 %all-to-all-done = f32[16,16,128]{2,1,0:T(8,128)S(1)} async-done(((f32[16,16,128]{2,1,0:T(8,128)}), f32[16,16,128]{2,1,0:T(8,128)S(1)}, u32[]{:S(2)}, u32[]{:S(2)}) %all-to-all-start) | async-done | bytes 131104 | tf_op jit(solution)/shard_map/all_to_all | solution.py:726
  55.5 1.2 %owner.1 = (f32[59,2,128]{2,1,0:T(2,128)}, f32[59,2,128]{2,1,0:T(2,128)S(1)}, f32[1,59,2,128]{3,2,1,0:T(2,128)S(1)}) custom-call(f32[256,128]{1,0:T(8,128)S(1)} %bitcast.42, f32[59,2,128]{2,1,0:T(2,128)S(1)} %bitcast.41, f32[59,2,128]{2,1,0:T(2,128)S(1)} %get-tuple-element.17.base_ref, f32[59,2,128]{2,1,0:T(2,128)S(1)} %bitcast.44, ...), custom_call_target="tpu_custom_call" | custom-call | tf_op jit(solution)/shard_map/owner/pallas_call | solution.py:727
  56.6 0.0 collective-permute-start.8
  56.6 1.2 %collective-permute-done.8 = f32[59,2,128]{2,1,0:T(2,128)S(1)} collective-permute-done((f32[59,2,128]{2,1,0:T(2,128)S(1)}, f32[59,2,128]{2,1,0:T(2,128)S(1)}, u32[]{:S(2)}, u32[]{:S(2)}) %collective-permute-start.8) | collective-permute-done | bytes 60448 | tf_op jit(solution)/shard_map/ppermute | solution.py:742
  57.9 0.7 %select_bitcast_fusion = f32[1,2,59,128]{3,1,2,0:T(2,128)} fusion(f32[59,2,128]{2,1,0:T(2,128)S(1)} %get-tuple-element.22, f32[59,2,128]{2,1,0:T(2,128)S(1)} %collective-permute-done.8, pred[2,128]{1,0:T(4,128)(4,1)S(1)} %compare_bitcast_fusion), kind=kLoop, calls=%fused_computation.2 | loop fusion | flops 60416 | bytes 181504 | tf_op jit(solution)/shard_map/broadcast_in_dim | solution.py:745
  (5 shorter events, 0.0 us)
Async XLA Ops:
  0.6 7.2 %collective-permute-start = (f32[1,59,2,128]{3,2,1,0:T(2,128)}, f32[1,59,2,128]{3,2,1,0:T(2,128)S(1)}, u32[]{:S(2)}, u32[]{:S(2)}) collective-permute-start(f32[1,59,2,128]{3,2,1,0:T(2,128)} %bitcast.37), channel_id=1, source_target_pairs={{0,8},{1,9},{2,10},{3,11},{4,12},{5,13},{6,14},{7,15},{8,0},{9,1},... | collective-permute-start | bytes 181256 | tf_op jit(solution)/shard_map/ppermute | solution.py:640
  5.4 0.7 %copy-start.8 = (s32[1,1,16]{2,1,0:T(1,128)S(1)}, s32[1,1,16]{2,1,0:T(1,128)}, u32[]{:S(2)}) copy-start(s32[1,1,16]{2,1,0:T(1,128)} %param.21) | copy-start | bytes 196
  6.0 7.7 %copy-start = (f32[1,2,59,128]{3,1,2,0:T(2,128)S(1)}, f32[1,2,59,128]{3,1,2,0:T(2,128)}, u32[]{:S(2)}) copy-start(f32[1,2,59,128]{3,1,2,0:T(2,128)} %param.15) | copy-start | bytes 181252
  6.0 4.0 %collective-permute-start.2 = (s32[1,144]{1,0:T(1,128)S(1)}, s32[1,144]{1,0:T(1,128)S(1)}, u32[]{:S(2)}, u32[]{:S(2)}) collective-permute-start(s32[1,144]{1,0:T(1,128)S(1)} %concatenate.19), channel_id=1, source_target_pairs={{0,1},{1,0},{2,3},{3,2},{4,5},{5,4},{6,7},{7,6},{8,9},{9,8},{10,11... | collective-permute-start | bytes 1736 | tf_op jit(solution)/shard_map/ppermute | solution.py:640
  8.7 5.1 %collective-permute-start.1 = (f32[2,59,2,128]{3,2,1,0:T(2,128)S(1)}, f32[2,59,2,128]{3,2,1,0:T(2,128)S(1)}, u32[]{:S(2)}, u32[]{:S(2)}) collective-permute-start(f32[2,59,2,128]{3,2,1,0:T(2,128)S(1)} %pad_maximum_fusion.1), channel_id=1, source_target_pairs={{0,4},{1,5},{2,6},{3,7},{4,0},{5,1},{6,2},{7,3},{8,12},{9,13},{10,... | collective-permute-start | bytes 362504 | tf_op jit(solution)/shard_map/ppermute | solution.py:640
  10.1 3.7 %collective-permute-start.3 = (s32[2,144]{1,0:T(2,128)S(1)}, s32[2,144]{1,0:T(2,128)S(1)}, u32[]{:S(2)}, u32[]{:S(2)}) collective-permute-start(s32[2,144]{1,0:T(2,128)S(1)} %pad_add_fusion.1), channel_id=1, source_target_pairs={{0,2},{1,3},{2,0},{3,1},{4,6},{5,7},{6,4},{7,5},{8,10},{9,11},{10,... | collective-permute-start | bytes 3464 | tf_op jit(solution)/shard_map/ppermute | solution.py:640
  13.7 0.8 %copy-start.5 = (bf16[128,128]{1,0:T(8,128)(2,1)S(1)}, bf16[128,128]{1,0:T(8,128)(2,1)}, u32[]{:S(2)}) copy-start(bf16[128,128]{1,0:T(8,128)(2,1)} %constant.24.clone.order_ref) | copy-start | bytes 98308
  13.8 0.8 %copy-start.6 = (f32[16,16]{1,0:T(8,128)S(1)}, f32[16,16]{1,0:T(8,128)}, u32[]{:S(2)}) copy-start(f32[16,16]{1,0:T(8,128)} %cameras_ref.3) | copy-start | bytes 3076
  14.5 4.9 %copy-start.12 = (f32[1,1,3,1024]{3,1,2,0:T(1,128)S(1)}, f32[1,1,3,1024]{3,1,2,0:T(1,128)}, u32[]{:S(2)}) copy-start(f32[1,1,3,1024]{3,1,2,0:T(1,128)} %param.24) | copy-start | bytes 36868
  14.5 8.5 %copy-start.2 = (bf16[48,1408]{1,0:T(8,128)(2,1)S(1)}, bf16[48,1408]{1,0:T(8,128)(2,1)}, u32[]{:S(2)}) copy-start(bf16[48,1408]{1,0:T(8,128)(2,1)} %constant.22.clone.basis_ref) | copy-start | bytes 405508
  15.1 7.9 %copy-start.4 = (bf16[128,128]{1,0:T(8,128)(2,1)S(1)}, bf16[128,128]{1,0:T(8,128)(2,1)}, u32[]{:S(2)}) copy-start(bf16[128,128]{1,0:T(8,128)(2,1)} %constant.25.clone.back_ref) | copy-start | bytes 98308
  15.2 4.2 %collective-permute-start.4 = (f32[36,128]{1,0:T(8,128)S(1)}, f32[36,128]{1,0:T(8,128)S(1)}, u32[]{:S(2)}, u32[]{:S(2)}) collective-permute-start(f32[36,128]{1,0:T(8,128)S(1)} %get-tuple-element.14), channel_id=1, source_target_pairs={{0,1},{1,0},{2,3},{3,2},{4,5},{5,4},{6,7},{7,6},{8,9},{9,8},{10,11... | collective-permute-start | bytes 55304 | tf_op jit(solution)/shard_map/ppermute | solution.py:640
  16.8 3.8 %collective-permute-start.5 = (f32[36,128]{1,0:T(8,128)S(1)}, f32[36,128]{1,0:T(8,128)S(1)}, u32[]{:S(2)}, u32[]{:S(2)}) collective-permute-start(f32[36,128]{1,0:T(8,128)S(1)} %get-tuple-element.15), channel_id=1, source_target_pairs={{0,2},{1,3},{2,0},{3,1},{4,6},{5,7},{6,4},{7,5},{8,10},{9,11},{10,... | collective-permute-start | bytes 55304 | tf_op jit(solution)/shard_map/ppermute | solution.py:640
  18.3 4.7 %collective-permute-start.6 = (f32[36,128]{1,0:T(8,128)S(1)}, f32[36,128]{1,0:T(8,128)S(1)}, u32[]{:S(2)}, u32[]{:S(2)}) collective-permute-start(f32[36,128]{1,0:T(8,128)S(1)} %get-tuple-element.16), channel_id=1, source_target_pairs={{0,3},{1,2},{2,1},{3,0},{4,7},{5,6},{6,5},{7,4},{8,11},{9,10},{10,... | collective-permute-start | bytes 55304 | tf_op jit(solution)/shard_map/ppermute | solution.py:640
  19.4 3.6 %copy-start.7 = (bf16[32,128]{1,0:T(8,128)(2,1)S(1)}, bf16[32,128]{1,0:T(8,128)(2,1)}, u32[]{:S(2)}) copy-start(bf16[32,128]{1,0:T(8,128)(2,1)} %constant.23.clone.xmom_ref) | copy-start | bytes 24580
  23.0 0.7 %copy-start.10 = (s32[1,1,16]{2,1,0:T(1,128)S(1)}, s32[1,1,16]{2,1,0:T(1,128)}, u32[]{:S(2)}) copy-start(s32[1,1,16]{2,1,0:T(1,128)} %param.22) | copy-start | bytes 196
  31.1 18.4 %copy-start.1 = (f32[1,2,59,128]{3,1,2,0:T(2,128)S(1)}, f32[1,2,59,128]{3,1,2,0:T(2,128)}, u32[]{:S(2)}) copy-start(f32[1,2,59,128]{3,1,2,0:T(2,128)} %param.17) | copy-start | bytes 181252
  31.1 18.4 %copy-start.3 = (f32[1,2,59,128]{3,1,2,0:T(2,128)S(1)}, f32[1,2,59,128]{3,1,2,0:T(2,128)}, u32[]{:S(2)}) copy-start(f32[1,2,59,128]{3,1,2,0:T(2,128)} %param.16) | copy-start | bytes 181252
  31.1 24.4 %all-to-all-start = ((f32[16,16,128]{2,1,0:T(8,128)}), f32[16,16,128]{2,1,0:T(8,128)S(1)}, u32[]{:S(2)}, u32[]{:S(2)}) async-start(f32[16,16,128]{2,1,0:T(8,128)} %render.1), calls=%async_computation | async-start | bytes 262144 | tf_op jit(solution)/shard_map/all_to_all | solution.py:726
  47.7 0.7 %copy-start.9 = (s32[1,1,2,64]{3,2,1,0:T(2,128)S(1)}, s32[1,1,2,64]{3,2,1,0:T(2,128)}, u32[]{:S(2)}) copy-start(s32[1,1,2,64]{3,2,1,0:T(2,128)} %param.25) | copy-start | bytes 1540
  48.4 1.1 %collective-permute-start.7 = (s32[2,64]{1,0:T(2,128)S(1)}, s32[2,64]{1,0:T(2,128)S(1)}, u32[]{:S(2)}, u32[]{:S(2)}) collective-permute-start(s32[2,64]{1,0:T(2,128)S(1)} %bitcast.49), channel_id=1, source_target_pairs={{0,16},{16,0},{1,17},{17,1},{2,18},{18,2},{3,19},{19,3},{4,20},{20... | collective-permute-start | bytes 1544 | tf_op jit(solution)/shard_map/ppermute | solution.py:670
  49.5 0.7 %copy-start.11 = (f32[59]{0:T(128)S(1)}, f32[59]{0:T(128)}, u32[]{:S(2)}) copy-start(f32[59]{0:T(128)} %step_ref.1) | copy-start | bytes 712
  56.6 1.2 %collective-permute-start.8 = (f32[59,2,128]{2,1,0:T(2,128)S(1)}, f32[59,2,128]{2,1,0:T(2,128)S(1)}, u32[]{:S(2)}, u32[]{:S(2)}) collective-permute-start(f32[59,2,128]{2,1,0:T(2,128)S(1)} %bitcast.52), channel_id=1, source_target_pairs={{0,16},{16,0},{1,17},{17,1},{2,18},{18,2},{3,19},{19,3},{4,20},{20... | collective-permute-start | bytes 181256 | tf_op jit(solution)/shard_map/ppermute | solution.py:742

commit v4 on v3

--- a/solution.py
+++ b/solution.py
@@ -37,8 +37,8 @@
 KDIM = 3 * PART
 COEFS = 9
 INNER = 4
-SEGS = 8
 MOMENTS = 6
+WIDE = 256
 MSG = 16
 highest = lax.Precision.HIGHEST
 
@@ -233,8 +233,8 @@
 def render_kernel(
     pixels, blocks, hop_bits, me_ref, cam_id_ref, count_ref, list_ref, depth_ref, cameras_ref,
     src0, src1, src2, src3, target_ref, basis_ref, xmom_ref, back_ref, out_ref,
-    raw, coef, expo, shade, alphas, weights, carry, before, passed, colours,
-    resid, behind, sums, found, rows, slots,
+    raw, coef, shade, stage_a, stage_b, gaps_a, gaps_b, alphas, weights, carry, before, passed,
+    colours, resid, mirror, pulls, behind, sums_a, sums_b, found, rows, slots,
 ):
     listed = list_ref.shape[0]
     peers = out_ref.shape[0]
@@ -259,6 +259,8 @@
     for j, src in enumerate((src0, src1, src2, src3)):
         raw[j * COEFS * outer : (j + 1) * COEFS * outer, :] = src[...]
     coef[...] = jnp.zeros(coef.shape, jnp.float32)
+    for k in range(coef.shape[0] // KDIM):
+        coef[k * KDIM + 5 : k * KDIM + 6, :] = jnp.full((1, LANES), -4096.0)
 
     def fetch(k, _):
         apart = me ^ (list_ref[slots[k]] // per_owner)
@@ -269,6 +271,7 @@
             base = pl.multiple_of(k * KDIM + part * PART, PART)
             coef[pl.ds(base, COEFS), :] = piece
             coef[pl.ds(base + COEFS, 1), :] = piece[0:1, :]
+            coef[pl.ds(base + COEFS + 1, 3), :] = piece[COEFS - 3 : COEFS, :]
         return 0
 
     lax.fori_loop(0, count, fetch, 0)
@@ -276,107 +279,155 @@
     sub = lax.broadcasted_iota(jnp.int32, (SUB, LANES), 0)
     one = jnp.ones((SUB, LANES), jnp.float32)
     none = jnp.zeros((SUB, LANES), jnp.float32)
+    row_sets = [range(yrows // 2), range(yrows // 2, yrows)]
     for y in range(yrows):
         carry[y] = one
-    for c in range(3):
-        for y in range(yrows):
+        behind[y] = none
+        for c in range(3):
             resid[c, y] = none
 
     def spread_row(value, index):
         return jnp.broadcast_to(value[index : index + 1, :], (SUB, LANES))
 
-    def forward(k, _):
-        mine = coef[pl.ds(pl.multiple_of(k * KDIM, PART), KDIM), :].astype(jnp.bfloat16)
-        expo[...] = lax.dot_general(
-            mine, basis_ref[...], (((0,), (0,)), ((), ())), preferred_element_type=jnp.float32
-        )
+    def rows_at(start, size, step):
+        return pl.ds(pl.multiple_of(start, step), size)
+
+    def product(k, right, out, finish):
+        mine = coef[rows_at(k * KDIM, KDIM, PART), :].T.astype(jnp.bfloat16)
+        for start in range(0, pixels, WIDE):
+            here = slice(start, start + WIDE)
+            out[:, here] = finish(
+                jnp.dot(mine, right[:, here], preferred_element_type=jnp.float32)
+            )
+        if right.shape[1] > pixels:
+            shade[rows_at(k * LANES, LANES, LANES), :] = jnp.dot(
+                mine, right[:, pixels:], preferred_element_type=jnp.float32
+            )
+
+    def to_alpha(value):
+        return jnp.minimum(alpha_ceiling, jnp.exp2(value))
+
+    def as_it_is(value):
+        return value
+
+    def chain(k, stage):
         base = pl.multiple_of(k * LANES, LANES)
-        shade[pl.ds(base, LANES), :] = expo[:, pixels:]
         kept = [one] * yrows
-        total = [[none] * yrows for _ in range(3)]
         for i in range(groups):
-            here = pl.ds(pl.multiple_of(base + i * SUB, SUB), SUB)
-            tints = [
-                expo[i * SUB : (i + 1) * SUB, pixels + c * LANES : pixels + (c + 1) * LANES]
-                for c in range(3)
-            ]
+            here = rows_at(base + i * SUB, SUB, SUB)
             for y in range(yrows):
                 lanes = slice(y * LANES, (y + 1) * LANES)
-                alpha = jnp.minimum(
-                    alpha_ceiling, jnp.exp2(expo[i * SUB : (i + 1) * SUB, lanes])
-                )
+                alpha = stage[i * SUB : (i + 1) * SUB, lanes]
                 weight = alpha * kept[y]
                 alphas[here, lanes] = alpha
                 weights[here, lanes] = weight
                 kept[y] = kept[y] - weight
-                for c in range(3):
-                    total[c][y] = total[c][y] + weight * tints[c]
         for y in range(yrows):
             passed[k, y] = kept[y]
-            through = kept[y]
-            for step in (1, 2, 4):
-                through = through * jnp.where(sub >= step, sub_roll(through, step), 1.0)
-            entering = carry[y]
-            ahead = entering * jnp.where(sub >= 1, sub_roll(through, 1), 1.0)
-            before[k, y] = ahead
-            carry[y] = entering * spread_row(through, SUB - 1)
-            for c in range(3):
-                colours[k, c, y] = total[c][y]
-                resid[c, y] = resid[c, y] + ahead * total[c][y]
+
+    def tally(k, ended):
+        base = pl.multiple_of(k * LANES, LANES)
+        for some in row_sets:
+            total = [[last - last for last in ends] for ends in ended]
+            for i in range(groups):
+                here = rows_at(base + i * SUB, SUB, SUB)
+                tints = [shade[here, c * LANES : (c + 1) * LANES] for c in range(3)]
+                for j, y in enumerate(some):
+                    weight = weights[here, y * LANES : (y + 1) * LANES]
+                    for c in range(3):
+                        total[c][j] = total[c][j] + weight * tints[c]
+            for j, y in enumerate(some):
+                through = passed[k, y]
+                for step in (1, 2, 4):
+                    through = through * jnp.where(sub >= step, sub_roll(through, step), 1.0)
+                entering = carry[y]
+                ahead = entering * jnp.where(sub >= 1, sub_roll(through, 1), 1.0)
+                before[k, y] = ahead
+                carry[y] = entering * spread_row(through, SUB - 1)
+                for c in range(3):
+                    colours[k, c, y] = total[c][j]
+                    resid[c, y] = resid[c, y] + ahead * total[c][j]
+            ended = total
+        return ended
+
+    pairs = (count + 1) // 2
+    fresh = [[none] * (yrows // 2)] * 3
+    product(0, basis_ref, stage_a, to_alpha)
+    product(1, basis_ref, stage_b, to_alpha)
+
+    def advance(pair):
+        chain(2 * pair, stage_a)
+        product(2 * pair + 2, basis_ref, stage_a, to_alpha)
+        chain(2 * pair + 1, stage_b)
+        product(2 * pair + 3, basis_ref, stage_b, to_alpha)
+
+    def forward(pair, _):
+        tally(2 * pair - 1, tally(2 * pair - 2, fresh))
+        advance(pair)
         return 0
 
-    lax.fori_loop(0, count, forward, 0)
-
+    advance(0)
+    lax.fori_loop(1, pairs, forward, 0)
+    tally(2 * pairs - 1, tally(2 * pairs - 2, fresh))
+
+    mirror[...] = jnp.zeros(mirror.shape, jnp.float32)
     for y in range(yrows):
         for c in range(3):
             value = jnp.sum(resid[c, y], axis=0, keepdims=True)
             value = value - target_ref[c : c + 1, y * LANES : (y + 1) * LANES]
             resid[c, y] = jnp.broadcast_to(value, (SUB, LANES))
-        behind[y] = none
-
-    def backward(back, _):
-        k = count - 1 - back
+            high, low, _ = three_parts(value)
+            for piece in range(3):
+                lanes = slice(y * LANES, (y + 1) * LANES)
+                at = piece * PART + COEFS - 3 + c
+                mirror[at : at + 1, lanes] = high
+                if piece < 2:
+                    mirror[at + 4 : at + 5, lanes] = low
+    pulls[...] = mirror[...].astype(jnp.bfloat16)
+
+    def follow(k, stage, gaps):
         base = pl.multiple_of(k * LANES, LANES)
-        pull = [[None] * yrows for _ in range(3)]
         rear = [None] * yrows
         for y in range(yrows):
-            res = [resid[c, y] for c in range(3)]
             gain = passed[k, y]
-            value = sum(colours[k, c, y] * res[c] for c in range(3))
+            value = sum(colours[k, c, y] * resid[c, y] for c in range(3))
             for step in (1, 2, 4):
                 inside = sub < SUB - step
                 value = value + gain * jnp.where(inside, sub_roll(value, -step), 0.0)
                 gain = gain * jnp.where(inside, sub_roll(gain, -step), 1.0)
             last = behind[y]
-            ahead = before[k, y]
-            at_end = jnp.where(
+            rear[y] = jnp.where(
                 sub < SUB - 1, sub_roll(value, -1) + sub_roll(gain, -1) * last, last
             )
             behind[y] = spread_row(value + gain * last, 0)
-            rear[y] = ahead * at_end
-            for c in range(3):
-                pull[c][y] = ahead * res[c]
         for i in reversed(range(groups)):
-            here = pl.ds(pl.multiple_of(base + i * SUB, SUB), SUB)
-            tints = [shade[here, c * LANES : (c + 1) * LANES] for c in range(3)]
-            run = [none, none, none]
-            drawn = [none, none, none]
+            here = slice(i * SUB, (i + 1) * SUB)
             for y in range(yrows):
                 lanes = slice(y * LANES, (y + 1) * LANES)
-                alpha = alphas[here, lanes]
-                weight = weights[here, lanes]
-                gap = (
-                    tints[0] * pull[0][y] + tints[1] * pull[1][y] + tints[2] * pull[2][y] - rear[y]
-                )
-                slope = jnp.where(alpha < alpha_ceiling, weight * gap, 0.0)
-                rear[y] = rear[y] + alpha * gap
+                gap = stage[here, lanes] - rear[y]
+                gaps[here, lanes] = gap
+                rear[y] = rear[y] + alphas[rows_at(base + i * SUB, SUB, SUB), lanes] * gap
+
+    def weigh(k, gaps, sums):
+        base = pl.multiple_of(k * LANES, LANES)
+        front = [before[k, y] for y in range(yrows)]
+        for i in range(groups):
+            at = slice(i * SUB, (i + 1) * SUB)
+            here = rows_at(base + i * SUB, SUB, SUB)
+            run = [none] * MOMENTS
+            for y in range(yrows):
+                lanes = slice(y * LANES, (y + 1) * LANES)
+                weight = weights[here, lanes] * front[y]
+                slope = jnp.where(alphas[here, lanes] < alpha_ceiling, weight * gaps[at, lanes], 0.0)
                 run[0] = run[0] + slope
                 run[1] = run[1] + run[0]
                 run[2] = run[2] + run[1]
                 for c in range(3):
-                    drawn[c] = drawn[c] + weight * pull[c][y]
-            for m, value in enumerate(run + drawn):
+                    run[3 + c] = run[3 + c] + weight * resid[c, y]
+            for m, value in enumerate(run):
                 sums[m * LANES + i * SUB : m * LANES + (i + 1) * SUB, :] = value
+
+    def moments(k, sums):
         value = sums[...]
         high = value.astype(jnp.bfloat16)
         low = (value - high.astype(jnp.float32)).astype(jnp.bfloat16)
@@ -385,15 +436,36 @@
         found[k] = lax.dot_general(
             xmom, high, contract, preferred_element_type=jnp.float32
         ) + lax.dot_general(xmom, low, contract, preferred_element_type=jnp.float32)
+
+    rearmost = 2 * pairs - 1
+    product(rearmost, pulls, stage_a, as_it_is)
+    product(rearmost - 1, pulls, stage_b, as_it_is)
+
+    def retreat(k):
+        follow(k, stage_a, gaps_a)
+        product(jnp.maximum(k - 2, 0), pulls, stage_a, as_it_is)
+        follow(k - 1, stage_b, gaps_b)
+        product(jnp.maximum(k - 3, 0), pulls, stage_b, as_it_is)
+
+    def collect(k):
+        moments(k + 2, sums_a)
+        weigh(k, gaps_a, sums_a)
+        moments(k + 1, sums_b)
+        weigh(k - 1, gaps_b, sums_b)
+
+    def backward(pair, _):
+        k = rearmost - 2 * pair
+        collect(k + 2)
+        retreat(k)
         return 0
 
-    lax.fori_loop(0, count, backward, 0)
+    retreat(rearmost)
+    lax.fori_loop(1, pairs, backward, 0)
+    collect(jnp.int32(1))
+    moments(1, sums_a)
+    moments(0, sums_b)
 
     lane = lax.broadcasted_iota(jnp.int32, (1, LANES), 1)
-    middle = (
-        lax.broadcasted_iota(jnp.int32, (SUB, LANES), 0) * (LANES // SEGS)
-        + (LANES // SEGS // 2 - 64)
-    ).astype(jnp.float32)
     meta = jnp.where(lane == 17, top, 0.0)
     for c in range(16):
         meta = jnp.where(lane == c, cameras_ref[cam_id, c], meta)
@@ -401,19 +473,12 @@
     rows[...] = jnp.zeros(rows.shape, jnp.float32)
 
     def gather_moments(k, _):
-        part = lambda order, m: found[k, order * SEGS : (order + 1) * SEGS, m * LANES : (m + 1) * LANES]
-        add = lambda value: jnp.sum(value, axis=0, keepdims=True)
+        part = lambda order, m: found[k, order : order + 1, m * LANES : (m + 1) * LANES]
         rise = yrows - 4.0
-        h0, h1, h2 = part(0, 0), part(1, 0), part(2, 0)
-        n0, n1 = part(0, 1), part(1, 1)
-        s0 = add(h0)
-        x1 = add(h1 + middle * h0)
-        x2 = add(h2 + middle * (2.0 * h1 + middle * h0))
-        t1 = add(n0)
-        tx = add(n1 + middle * n0)
-        t2 = 2.0 * add(part(0, 2)) - t1
+        s0, x1, x2 = part(0, 0), part(1, 0), part(2, 0) + part(3, 0)
+        t1, tx, t2 = part(0, 1), part(1, 1), 2.0 * part(0, 2) - part(0, 1)
         answer = [s0, x1, rise * s0 - t1, x2, rise * x1 - tx, rise * (rise * s0 - 2.0 * t1) + t2]
-        answer += [add(part(0, 3 + c)) for c in range(3)]
+        answer += [part(0, 3 + c) for c in range(3)]
         for m, value in enumerate(answer):
             rows[pl.ds(k * MSG + m, 1), :] = value
         return 0
@@ -589,18 +654,12 @@
     part = np.zeros((PART, pixels + 3 * LANES), np.float32)
     for c, value in enumerate([square, x * y, y * y, x, y, np.ones_like(x)]):
         part[c, :pixels] = value
+    part[COEFS, :pixels] = x * x - square
     for c in range(3):
-        part[6 + c, pixels + c * LANES : pixels + (c + 1) * LANES] = 1.0
-    part[COEFS, :pixels] = x * x - square
+        part[COEFS - 3 + c, pixels + c * LANES : pixels + (c + 1) * LANES] = 1.0
     basis = np.concatenate([part] * 3)
-    lane = np.arange(LANES)
-    wide = LANES // SEGS
-    xmom = np.zeros((3 * SEGS + SEGS, LANES), np.float32)
-    for s in range(SEGS):
-        near = (lane // wide == s).astype(np.float32)
-        offset = lane - s * wide - wide // 2
-        for power in range(3):
-            xmom[power * SEGS + s] = near * offset**power
+    xmom = np.zeros((SUB, LANES), np.float32)
+    xmom[:4] = [np.ones(LANES), x[:LANES], square[:LANES], (x * x - square)[:LANES]]
     order = np.zeros((LANES, LANES), np.float32)
     groups = LANES // SUB
     for r in range(LANES):
@@ -701,19 +760,25 @@
         out_specs=vmem()[0],
         scratch_shapes=[
             pltpu.VMEM((COEFS * peers, LANES), f32),
-            pltpu.VMEM((listed * KDIM, LANES), f32),
-            pltpu.VMEM((LANES, pixels + 3 * LANES), f32),
-            pltpu.VMEM((listed * LANES, 3 * LANES), f32),
-            pltpu.VMEM((listed * LANES, pixels), f32),
-            pltpu.VMEM((listed * LANES, pixels), f32),
+            pltpu.VMEM(((listed + 2) * KDIM, LANES), f32),
+            pltpu.VMEM(((listed + 2) * LANES, 3 * LANES), f32),
+            pltpu.VMEM((LANES, pixels), f32),
+            pltpu.VMEM((LANES, pixels), f32),
+            pltpu.VMEM((LANES, pixels), f32),
+            pltpu.VMEM((LANES, pixels), f32),
+            pltpu.VMEM(((listed + 1) * LANES, pixels), f32),
+            pltpu.VMEM(((listed + 1) * LANES, pixels), f32),
             pltpu.VMEM((yrows, SUB, LANES), f32),
-            pltpu.VMEM((listed, yrows, SUB, LANES), f32),
-            pltpu.VMEM((listed, yrows, SUB, LANES), f32),
-            pltpu.VMEM((listed, 3, yrows, SUB, LANES), f32),
+            pltpu.VMEM((listed + 1, yrows, SUB, LANES), f32),
+            pltpu.VMEM((listed + 1, yrows, SUB, LANES), f32),
+            pltpu.VMEM((listed + 1, 3, yrows, SUB, LANES), f32),
             pltpu.VMEM((3, yrows, SUB, LANES), f32),
+            pltpu.VMEM((KDIM, pixels), f32),
+            pltpu.VMEM((KDIM, pixels), jnp.bfloat16),
             pltpu.VMEM((yrows, SUB, LANES), f32),
             pltpu.VMEM((MOMENTS * LANES, LANES), f32),
-            pltpu.VMEM((listed, 4 * SEGS, MOMENTS * LANES), f32),
+            pltpu.VMEM((MOMENTS * LANES, LANES), f32),
+            pltpu.VMEM((listed + 4, SUB, MOMENTS * LANES), f32),
             pltpu.VMEM((listed * MSG, LANES), f32),
             pltpu.SMEM((listed,), jnp.int32),
         ],

time: 58.9 us -> 55.9 us (0.949)
  starting transfers between devices: 28.7 us -> 16.8 us
  Pallas kernels: 10 us -> 18.8 us
    all_to_all x1, starting transfers between devices: 16.5 us -> 4.63 us  [on_device(): lax.all_to_all(outbox, 'tile', split_axis=0, concat_axis=0, tiled=True)]
    pallas_call x1, Pallas kernels: 7.44 us -> 16.2 us  [on_device(): pl.pallas_call(functools.partial(render_kernel, pixels, blocks, hop_bits)...]
where the time goes in v4:
time: 55.9 us; the launch traced here: 55.5 us
  Pallas kernels  18.8 us (34%)
  starting transfers between devices  16.8 us (30%)
  waiting for transfers between devices  12.8 us (23%)
  local copies, waits for them, and re-layouts  3.29 us (6%)
  between operations  2.07 us (4%)
  other arithmetic  1.69 us (3%)
    pallas_call x1, Pallas kernels, on_device(): pl.pallas_call(functools.partial(render_kernel, pixels, blocks, hop_bits)...  16.2 us
    ppermute x7, starting transfers between devices, swap(): return lax.ppermute(value, 'tile', [(i, i ^ mask) for i in range(peers)])  12.1 us
    ppermute x7, waiting for transfers between devices, swap(): return lax.ppermute(value, 'tile', [(i, i ^ mask) for i in range(peers)])  5.93 us
    all_to_all x1, starting transfers between devices, on_device(): lax.all_to_all(outbox, 'tile', split_axis=0, concat_axis=0, tiled=True)  4.63 us
    all_to_all x1, waiting for transfers between devices, on_device(): lax.all_to_all(outbox, 'tile', split_axis=0, concat_axis=0, tiled=True)  4.49 us
    unnamed x27, local copies, waits for them, and re-layouts  3.29 us
    ppermute x1, waiting for transfers between devices, on_device(): theirs = lax.ppermute(sent[n], 'scene', route)  1.24 us
    pallas_call x1, Pallas kernels, on_device(): pl.pallas_call(owner_kernel, out_shape=(shape_of(own.shape, f32), shape_o...  1.16 us
  transfers between devices with their start and end apart: 10, of which 7 were waited for; matrix products, arithmetic and copies ran while one was open for 2% of the time, Pallas kernels for 1%

profile of v4, /device:TPU:0, one launch (start us, length us, event | category | flops | bytes accessed | tf_op | source)
XLA Modules:
  0.0 55.5 jit_solution(4703687719876899421)
XLA Ops:
  0.6 4.1 %collective-permute-start = (f32[1,59,2,128]{3,2,1,0:T(2,128)}, f32[1,59,2,128]{3,2,1,0:T(2,128)S(1)}, u32[]{:S(2)}, u32[]{:S(2)}) collective-permute-start(f32[1,59,2,128]{3,2,1,0:T(2,128)} %bitcast.37), channel_id=1, source_target_pairs={{0,8},{1,9},{2,10},{3,11},{4,12},{5,13},{6,14},{7,15},{8,0},{9,1},... | collective-permute-start | bytes 181256 | tf_op jit(solution)/shard_map/ppermute | solution.py:699
  5.4 0.0 copy-start.8
  5.4 0.6 %copy-done.8 = s32[1,1,16]{2,1,0:T(1,128)S(1)} copy-done((s32[1,1,16]{2,1,0:T(1,128)S(1)}, s32[1,1,16]{2,1,0:T(1,128)}, u32[]{:S(2)}) %copy-start.8) | copy-done | bytes 88
  6.0 0.0 copy-start
  6.0 1.5 %collective-permute-start.2 = (s32[1,144]{1,0:T(1,128)S(1)}, s32[1,144]{1,0:T(1,128)S(1)}, u32[]{:S(2)}, u32[]{:S(2)}) collective-permute-start(s32[1,144]{1,0:T(1,128)S(1)} %concatenate.19), channel_id=1, source_target_pairs={{0,1},{1,0},{2,3},{3,2},{4,5},{5,4},{6,7},{7,6},{8,9},{9,8},{10,11... | collective-permute-start | bytes 1736 | tf_op jit(solution)/shard_map/ppermute | solution.py:699
  7.5 0.2 collective-permute-done
  7.8 0.9 %pad_maximum_fusion.1 = f32[2,59,2,128]{3,2,1,0:T(2,128)S(1)} fusion(f32[1,59,2,128]{3,2,1,0:T(2,128)S(1)} %collective-permute-done, f32[1,59,2,128]{3,2,1,0:T(2,128)} %bitcast.38), kind=kLoop, calls=%fused_computation.1 | loop fusion | flops 30208 | bytes 241664 | tf_op jit(solution)/shard_map/concatenate | solution.py:711
  8.7 1.4 %collective-permute-start.1 = (f32[2,59,2,128]{3,2,1,0:T(2,128)S(1)}, f32[2,59,2,128]{3,2,1,0:T(2,128)S(1)}, u32[]{:S(2)}, u32[]{:S(2)}) collective-permute-start(f32[2,59,2,128]{3,2,1,0:T(2,128)S(1)} %pad_maximum_fusion.1), channel_id=1, source_target_pairs={{0,4},{1,5},{2,6},{3,7},{4,0},{5,1},{6,2},{7,3},{8,12},{9,13},{10,... | collective-permute-start | bytes 362504 | tf_op jit(solution)/shard_map/ppermute | solution.py:699
  10.1 0.0 collective-permute-done.2
  10.1 1.6 %collective-permute-start.3 = (s32[2,144]{1,0:T(2,128)S(1)}, s32[2,144]{1,0:T(2,128)S(1)}, u32[]{:S(2)}, u32[]{:S(2)}) collective-permute-start(s32[2,144]{1,0:T(2,128)S(1)} %pad_add_fusion.1), channel_id=1, source_target_pairs={{0,2},{1,3},{2,0},{3,1},{4,6},{5,7},{6,4},{7,5},{8,10},{9,11},{10,... | collective-permute-start | bytes 3464 | tf_op jit(solution)/shard_map/ppermute | solution.py:699
  11.7 2.1 %collective-permute-done.3 = s32[2,144]{1,0:T(2,128)S(1)} collective-permute-done((s32[2,144]{1,0:T(2,128)S(1)}, s32[2,144]{1,0:T(2,128)S(1)}, u32[]{:S(2)}, u32[]{:S(2)}) %collective-permute-start.3) | collective-permute-done | bytes 1184 | tf_op jit(solution)/shard_map/ppermute | solution.py:699
  13.7 0.0 copy-start.5
  13.8 0.0 copy-start.6
  13.8 0.0 collective-permute-done.1
  13.8 0.0 copy-done
  13.8 0.1 pad_maximum_fusion.raw_ref
  13.9 0.6 %copy-done.5 = bf16[128,128]{1,0:T(8,128)(2,1)S(1)} copy-done((bf16[128,128]{1,0:T(8,128)(2,1)S(1)}, bf16[128,128]{1,0:T(8,128)(2,1)}, u32[]{:S(2)}) %copy-start.5) | copy-done | bytes 32792
  14.5 0.0 copy-done.6
  14.5 0.0 copy-start.12
  14.5 0.0 copy-start.2
  14.5 0.6 %project.1 = (f32[36,128]{1,0:T(8,128)S(1)}, f32[36,128]{1,0:T(8,128)S(1)}, f32[36,128]{1,0:T(8,128)S(1)}, f32[36,128]{1,0:T(8,128)S(1)}) custom-call(s32[1]{0:T(128)} %bitcast.me_ref, f32[4,59,2,128]{3,2,1,0:T(2,128)S(1)} %pad_maximum_fusion.raw_ref, s32[4,144]{1,0:T(4,128)S(1)} %pad_add_fusion.ids_ref, f32[16,16]{1,0:T(8,128)S(1)} %copy-done.6, ...), custom_call_target="tpu_custom_call" | custom-call | tf_op jit(solution)/shard_map/project/pallas_call | solution.py:745
  15.1 0.0 copy-start.4
  15.2 1.7 %collective-permute-start.4 = (f32[36,128]{1,0:T(8,128)S(1)}, f32[36,128]{1,0:T(8,128)S(1)}, u32[]{:S(2)}, u32[]{:S(2)}) collective-permute-start(f32[36,128]{1,0:T(8,128)S(1)} %get-tuple-element.14), channel_id=1, source_target_pairs={{0,1},{1,0},{2,3},{3,2},{4,5},{5,4},{6,7},{7,6},{8,9},{9,8},{10,11... | collective-permute-start | bytes 55304 | tf_op jit(solution)/shard_map/ppermute | solution.py:699
  16.8 1.5 %collective-permute-start.5 = (f32[36,128]{1,0:T(8,128)S(1)}, f32[36,128]{1,0:T(8,128)S(1)}, u32[]{:S(2)}, u32[]{:S(2)}) collective-permute-start(f32[36,128]{1,0:T(8,128)S(1)} %get-tuple-element.15), channel_id=1, source_target_pairs={{0,2},{1,3},{2,0},{3,1},{4,6},{5,7},{6,4},{7,5},{8,10},{9,11},{10,... | collective-permute-start | bytes 55304 | tf_op jit(solution)/shard_map/ppermute | solution.py:699
  18.3 0.4 collective-permute-start.6
  19.4 0.0 copy-done.12
  19.4 0.0 collective-permute-done.4.src1
  19.4 1.2 %collective-permute-done.5.src2 = f32[36,128]{1,0:T(8,128)S(1)} collective-permute-done((f32[36,128]{1,0:T(8,128)S(1)}, f32[36,128]{1,0:T(8,128)S(1)}, u32[]{:S(2)}, u32[]{:S(2)}) %collective-permute-start.5) | collective-permute-done | bytes 18464 | tf_op jit(solution)/shard_map/ppermute | solution.py:699
  20.6 2.4 %collective-permute-done.6.src3 = f32[36,128]{1,0:T(8,128)S(1)} collective-permute-done((f32[36,128]{1,0:T(8,128)S(1)}, f32[36,128]{1,0:T(8,128)S(1)}, u32[]{:S(2)}, u32[]{:S(2)}) %collective-permute-start.6) | collective-permute-done | bytes 18464 | tf_op jit(solution)/shard_map/ppermute | solution.py:699
  23.0 0.0 copy-start.7
  23.0 0.0 copy-start.10
  23.0 0.0 copy-done.2
  23.0 0.0 copy-done.4
  23.0 0.7 %copy-done.7 = bf16[8,128]{1,0:T(8,128)(2,1)S(1)} copy-done((bf16[8,128]{1,0:T(8,128)(2,1)S(1)}, bf16[8,128]{1,0:T(8,128)(2,1)}, u32[]{:S(2)}) %copy-start.7) | copy-done | bytes 2072
  23.7 0.0 copy-done.10
  23.7 16.2 %render.1 = f32[16,16,128]{2,1,0:T(8,128)} custom-call(s32[1]{0:T(128)} %bitcast.me_ref, s32[1]{0:T(128)} %bitcast.34.cam_id_ref, s32[1]{0:T(128)} %bitcast.36.count_ref, s32[16]{0:T(128)S(1)} %bitcast.48, s32[16]{0:T(128)S(1)} %bitcast.51, f32[16,16]{1,0:T(8,128)S(1)} %copy-done.6, f32[36,128]{1,0:T(8,128)S(1)} %get-tuple-element.13.src0, ...), custom_call_target="tpu_custom_call" | custom-call | tf_op jit(solution)/shard_map/render/pallas_call | solution.py:756
  39.9 0.0 copy-start.1
  39.9 0.0 copy-start.3
  40.0 4.6 %all-to-all-start = ((f32[16,16,128]{2,1,0:T(8,128)}), f32[16,16,128]{2,1,0:T(8,128)S(1)}, u32[]{:S(2)}, u32[]{:S(2)}) async-start(f32[16,16,128]{2,1,0:T(8,128)} %render.1), calls=%async_computation | async-start | bytes 262144 | tf_op jit(solution)/shard_map/all_to_all | solution.py:791
  44.6 0.0 copy-start.9
  44.6 0.7 %copy-done.9 = s32[1,1,2,64]{3,2,1,0:T(2,128)S(1)} copy-done((s32[1,1,2,64]{3,2,1,0:T(2,128)S(1)}, s32[1,1,2,64]{3,2,1,0:T(2,128)}, u32[]{:S(2)}) %copy-start.9) | copy-done | bytes 536
  45.3 0.0 collective-permute-start.7
  45.3 1.1 %collective-permute-done.7.refs_0_ = s32[2,64]{1,0:T(2,128)S(1)} collective-permute-done((s32[2,64]{1,0:T(2,128)S(1)}, s32[2,64]{1,0:T(2,128)S(1)}, u32[]{:S(2)}, u32[]{:S(2)}) %collective-permute-start.7) | collective-permute-done | bytes 544 | tf_op jit(solution)/shard_map/ppermute | solution.py:729
  46.4 0.0 copy-start.11
  46.4 0.0 copy-done.1
  46.4 0.0 copy-done.3
  46.4 0.6 %copy-done.11 = f32[59]{0:T(128)S(1)} copy-done((f32[59]{0:T(128)S(1)}, f32[59]{0:T(128)}, u32[]{:S(2)}) %copy-start.11) | copy-done | bytes 260
  47.1 0.8 %prepare.1 = (f32[59,2,128]{2,1,0:T(2,128)S(1)}, f32[59,2,128]{2,1,0:T(2,128)S(1)}, bf16[1,256,256]{2,1,0:T(8,128)(2,1)S(1)}, f32[1,2,128]{2,1,0:T(2,128)S(1)}) custom-call(s32[1]{0:T(128)} %bitcast.13.group_ref, f32[59,2,128]{2,1,0:T(2,128)S(1)} %bitcast.40, f32[59,2,128]{2,1,0:T(2,128)S(1)} %bitcast.46, f32[59,2,128]{2,1,0:T(2,128)S(1)} %bitcast.43, ...), custom_call_target="tpu_custom_call" | custom-call | tf_op jit(solution)/shard_map/prepare/pallas_call | solution.py:731
  47.9 4.5 %all-to-all-done = f32[16,16,128]{2,1,0:T(8,128)S(1)} async-done(((f32[16,16,128]{2,1,0:T(8,128)}), f32[16,16,128]{2,1,0:T(8,128)S(1)}, u32[]{:S(2)}, u32[]{:S(2)}) %all-to-all-start) | async-done | bytes 131104 | tf_op jit(solution)/shard_map/all_to_all | solution.py:791
  52.4 1.2 %owner.1 = (f32[59,2,128]{2,1,0:T(2,128)}, f32[59,2,128]{2,1,0:T(2,128)S(1)}, f32[1,59,2,128]{3,2,1,0:T(2,128)S(1)}) custom-call(f32[256,128]{1,0:T(8,128)S(1)} %bitcast.42, f32[59,2,128]{2,1,0:T(2,128)S(1)} %bitcast.41, f32[59,2,128]{2,1,0:T(2,128)S(1)} %get-tuple-element.17.base_ref, f32[59,2,128]{2,1,0:T(2,128)S(1)} %bitcast.44, ...), custom_call_target="tpu_custom_call" | custom-call | tf_op jit(solution)/shard_map/owner/pallas_call | solution.py:792
  53.5 0.0 collective-permute-start.8
  53.6 1.2 %collective-permute-done.8 = f32[59,2,128]{2,1,0:T(2,128)S(1)} collective-permute-done((f32[59,2,128]{2,1,0:T(2,128)S(1)}, f32[59,2,128]{2,1,0:T(2,128)S(1)}, u32[]{:S(2)}, u32[]{:S(2)}) %collective-permute-start.8) | collective-permute-done | bytes 60448 | tf_op jit(solution)/shard_map/ppermute | solution.py:807
  54.8 0.7 %select_bitcast_fusion = f32[1,2,59,128]{3,1,2,0:T(2,128)} fusion(f32[59,2,128]{2,1,0:T(2,128)S(1)} %get-tuple-element.22, f32[59,2,128]{2,1,0:T(2,128)S(1)} %collective-permute-done.8, pred[2,128]{1,0:T(4,128)(4,1)S(1)} %compare_bitcast_fusion), kind=kLoop, calls=%fused_computation.2 | loop fusion | flops 60416 | bytes 181504 | tf_op jit(solution)/shard_map/broadcast_in_dim | solution.py:810
  (5 shorter events, 0.0 us)
Async XLA Ops:
  0.6 7.2 %collective-permute-start = (f32[1,59,2,128]{3,2,1,0:T(2,128)}, f32[1,59,2,128]{3,2,1,0:T(2,128)S(1)}, u32[]{:S(2)}, u32[]{:S(2)}) collective-permute-start(f32[1,59,2,128]{3,2,1,0:T(2,128)} %bitcast.37), channel_id=1, source_target_pairs={{0,8},{1,9},{2,10},{3,11},{4,12},{5,13},{6,14},{7,15},{8,0},{9,1},... | collective-permute-start | bytes 181256 | tf_op jit(solution)/shard_map/ppermute | solution.py:699
  5.4 0.7 %copy-start.8 = (s32[1,1,16]{2,1,0:T(1,128)S(1)}, s32[1,1,16]{2,1,0:T(1,128)}, u32[]{:S(2)}) copy-start(s32[1,1,16]{2,1,0:T(1,128)} %param.21) | copy-start | bytes 196
  6.0 7.7 %copy-start = (f32[1,2,59,128]{3,1,2,0:T(2,128)S(1)}, f32[1,2,59,128]{3,1,2,0:T(2,128)}, u32[]{:S(2)}) copy-start(f32[1,2,59,128]{3,1,2,0:T(2,128)} %param.15) | copy-start | bytes 181252
  6.0 4.0 %collective-permute-start.2 = (s32[1,144]{1,0:T(1,128)S(1)}, s32[1,144]{1,0:T(1,128)S(1)}, u32[]{:S(2)}, u32[]{:S(2)}) collective-permute-start(s32[1,144]{1,0:T(1,128)S(1)} %concatenate.19), channel_id=1, source_target_pairs={{0,1},{1,0},{2,3},{3,2},{4,5},{5,4},{6,7},{7,6},{8,9},{9,8},{10,11... | collective-permute-start | bytes 1736 | tf_op jit(solution)/shard_map/ppermute | solution.py:699
  8.7 5.1 %collective-permute-start.1 = (f32[2,59,2,128]{3,2,1,0:T(2,128)S(1)}, f32[2,59,2,128]{3,2,1,0:T(2,128)S(1)}, u32[]{:S(2)}, u32[]{:S(2)}) collective-permute-start(f32[2,59,2,128]{3,2,1,0:T(2,128)S(1)} %pad_maximum_fusion.1), channel_id=1, source_target_pairs={{0,4},{1,5},{2,6},{3,7},{4,0},{5,1},{6,2},{7,3},{8,12},{9,13},{10,... | collective-permute-start | bytes 362504 | tf_op jit(solution)/shard_map/ppermute | solution.py:699
  10.1 3.7 %collective-permute-start.3 = (s32[2,144]{1,0:T(2,128)S(1)}, s32[2,144]{1,0:T(2,128)S(1)}, u32[]{:S(2)}, u32[]{:S(2)}) collective-permute-start(s32[2,144]{1,0:T(2,128)S(1)} %pad_add_fusion.1), channel_id=1, source_target_pairs={{0,2},{1,3},{2,0},{3,1},{4,6},{5,7},{6,4},{7,5},{8,10},{9,11},{10,... | collective-permute-start | bytes 3464 | tf_op jit(solution)/shard_map/ppermute | solution.py:699
  13.7 0.8 %copy-start.5 = (bf16[128,128]{1,0:T(8,128)(2,1)S(1)}, bf16[128,128]{1,0:T(8,128)(2,1)}, u32[]{:S(2)}) copy-start(bf16[128,128]{1,0:T(8,128)(2,1)} %constant.24.clone.order_ref) | copy-start | bytes 98308
  13.8 0.8 %copy-start.6 = (f32[16,16]{1,0:T(8,128)S(1)}, f32[16,16]{1,0:T(8,128)}, u32[]{:S(2)}) copy-start(f32[16,16]{1,0:T(8,128)} %cameras_ref.3) | copy-start | bytes 3076
  14.5 4.9 %copy-start.12 = (f32[1,1,3,1024]{3,1,2,0:T(1,128)S(1)}, f32[1,1,3,1024]{3,1,2,0:T(1,128)}, u32[]{:S(2)}) copy-start(f32[1,1,3,1024]{3,1,2,0:T(1,128)} %param.24) | copy-start | bytes 36868
  14.5 8.5 %copy-start.2 = (bf16[48,1408]{1,0:T(8,128)(2,1)S(1)}, bf16[48,1408]{1,0:T(8,128)(2,1)}, u32[]{:S(2)}) copy-start(bf16[48,1408]{1,0:T(8,128)(2,1)} %constant.22.clone.basis_ref) | copy-start | bytes 405508
  15.1 7.9 %copy-start.4 = (bf16[128,128]{1,0:T(8,128)(2,1)S(1)}, bf16[128,128]{1,0:T(8,128)(2,1)}, u32[]{:S(2)}) copy-start(bf16[128,128]{1,0:T(8,128)(2,1)} %constant.25.clone.back_ref) | copy-start | bytes 98308
  15.2 4.2 %collective-permute-start.4 = (f32[36,128]{1,0:T(8,128)S(1)}, f32[36,128]{1,0:T(8,128)S(1)}, u32[]{:S(2)}, u32[]{:S(2)}) collective-permute-start(f32[36,128]{1,0:T(8,128)S(1)} %get-tuple-element.14), channel_id=1, source_target_pairs={{0,1},{1,0},{2,3},{3,2},{4,5},{5,4},{6,7},{7,6},{8,9},{9,8},{10,11... | collective-permute-start | bytes 55304 | tf_op jit(solution)/shard_map/ppermute | solution.py:699
  16.8 3.8 %collective-permute-start.5 = (f32[36,128]{1,0:T(8,128)S(1)}, f32[36,128]{1,0:T(8,128)S(1)}, u32[]{:S(2)}, u32[]{:S(2)}) collective-permute-start(f32[36,128]{1,0:T(8,128)S(1)} %get-tuple-element.15), channel_id=1, source_target_pairs={{0,2},{1,3},{2,0},{3,1},{4,6},{5,7},{6,4},{7,5},{8,10},{9,11},{10,... | collective-permute-start | bytes 55304 | tf_op jit(solution)/shard_map/ppermute | solution.py:699
  18.3 4.7 %collective-permute-start.6 = (f32[36,128]{1,0:T(8,128)S(1)}, f32[36,128]{1,0:T(8,128)S(1)}, u32[]{:S(2)}, u32[]{:S(2)}) collective-permute-start(f32[36,128]{1,0:T(8,128)S(1)} %get-tuple-element.16), channel_id=1, source_target_pairs={{0,3},{1,2},{2,1},{3,0},{4,7},{5,6},{6,5},{7,4},{8,11},{9,10},{10,... | collective-permute-start | bytes 55304 | tf_op jit(solution)/shard_map/ppermute | solution.py:699
  23.0 0.7 %copy-start.7 = (bf16[8,128]{1,0:T(8,128)(2,1)S(1)}, bf16[8,128]{1,0:T(8,128)(2,1)}, u32[]{:S(2)}) copy-start(bf16[8,128]{1,0:T(8,128)(2,1)} %constant.23.clone.xmom_ref) | copy-start | bytes 6148
  23.0 0.7 %copy-start.10 = (s32[1,1,16]{2,1,0:T(1,128)S(1)}, s32[1,1,16]{2,1,0:T(1,128)}, u32[]{:S(2)}) copy-start(s32[1,1,16]{2,1,0:T(1,128)} %param.22) | copy-start | bytes 196
  39.9 6.5 %copy-start.1 = (f32[1,2,59,128]{3,1,2,0:T(2,128)S(1)}, f32[1,2,59,128]{3,1,2,0:T(2,128)}, u32[]{:S(2)}) copy-start(f32[1,2,59,128]{3,1,2,0:T(2,128)} %param.17) | copy-start | bytes 181252
  39.9 6.5 %copy-start.3 = (f32[1,2,59,128]{3,1,2,0:T(2,128)S(1)}, f32[1,2,59,128]{3,1,2,0:T(2,128)}, u32[]{:S(2)}) copy-start(f32[1,2,59,128]{3,1,2,0:T(2,128)} %param.16) | copy-start | bytes 181252
  40.0 12.4 %all-to-all-start = ((f32[16,16,128]{2,1,0:T(8,128)}), f32[16,16,128]{2,1,0:T(8,128)S(1)}, u32[]{:S(2)}, u32[]{:S(2)}) async-start(f32[16,16,128]{2,1,0:T(8,128)} %render.1), calls=%async_computation | async-start | bytes 262144 | tf_op jit(solution)/shard_map/all_to_all | solution.py:791
  44.6 0.7 %copy-start.9 = (s32[1,1,2,64]{3,2,1,0:T(2,128)S(1)}, s32[1,1,2,64]{3,2,1,0:T(2,128)}, u32[]{:S(2)}) copy-start(s32[1,1,2,64]{3,2,1,0:T(2,128)} %param.25) | copy-start | bytes 1540
  45.3 1.1 %collective-permute-start.7 = (s32[2,64]{1,0:T(2,128)S(1)}, s32[2,64]{1,0:T(2,128)S(1)}, u32[]{:S(2)}, u32[]{:S(2)}) collective-permute-start(s32[2,64]{1,0:T(2,128)S(1)} %bitcast.49), channel_id=1, source_target_pairs={{0,16},{16,0},{1,17},{17,1},{2,18},{18,2},{3,19},{19,3},{4,20},{20... | collective-permute-start | bytes 1544 | tf_op jit(solution)/shard_map/ppermute | solution.py:729
  46.4 0.7 %copy-start.11 = (f32[59]{0:T(128)S(1)}, f32[59]{0:T(128)}, u32[]{:S(2)}) copy-start(f32[59]{0:T(128)} %step_ref.1) | copy-start | bytes 712
  53.5 1.2 %collective-permute-start.8 = (f32[59,2,128]{2,1,0:T(2,128)S(1)}, f32[59,2,128]{2,1,0:T(2,128)S(1)}, u32[]{:S(2)}, u32[]{:S(2)}) collective-permute-start(f32[59,2,128]{2,1,0:T(2,128)S(1)} %bitcast.52), channel_id=1, source_target_pairs={{0,16},{16,0},{1,17},{17,1},{2,18},{18,2},{3,19},{19,3},{4,20},{20... | collective-permute-start | bytes 181256 | tf_op jit(solution)/shard_map/ppermute | solution.py:807

commit v5 on v4

--- a/solution.py
+++ b/solution.py
@@ -140,6 +140,13 @@
     return (dot(high, pick) + dot(mid, pick)) + dot(low, pick)
 
 
+def segment_order(back):
+    shape = (LANES, LANES)
+    gauss = lax.broadcasted_iota(jnp.int32, shape, int(back))
+    place = lax.broadcasted_iota(jnp.int32, shape, 1 - int(back))
+    return (gauss == (place % SUB) * (LANES // SUB) + place // SUB).astype(jnp.bfloat16)
+
+
 def sub_roll(value, shift):
     return pltpu.roll(value, shift % SUB, 0)
 
@@ -174,7 +181,20 @@
             mask_ref[n, b : b + 1, :] = mask[0:1, b * LANES : (b + 1) * LANES]
 
 
-def project_kernel(masks, yrows, me_ref, raw_ref, ids_ref, cameras_ref, order_ref, *refs):
+def pack_kernel(
+    camera_ref, count_ref, list_ref, depth_ref, cameras_ref, own_ref, mine_ref, pack_ref, held_ref
+):
+    held_ref[...] = own_ref[...]
+    listed = list_ref.shape[1]
+    blocks = list_ref[...]
+    mine_ref[:, :16] = cameras_ref[pl.ds(camera_ref[0, 0], 1), :]
+    mine_ref[:, 16:] = blocks.astype(jnp.float32)
+    pack_ref[:, :listed] = blocks
+    pack_ref[:, listed : 2 * listed] = depth_ref[...]
+    pack_ref[:, 2 * listed :] = jnp.full((1, listed), count_ref[0, 0], jnp.int32)
+
+
+def project_kernel(masks, yrows, listed, me_ref, raw_ref, ids_ref, *refs):
     outs, feat = refs[:INNER], refs[INNER]
     outer = len(masks)
     blocks = raw_ref.shape[2]
@@ -182,19 +202,16 @@
     ids = jnp.concatenate([ids_ref[...]] * (SUB // INNER), axis=0)
     lane = lax.broadcasted_iota(jnp.int32, (SUB, LANES), 1)
     sub = lax.broadcasted_iota(jnp.int32, (SUB, LANES), 0)
-    ncam = cameras_ref.shape[0]
-    chosen = lax.broadcasted_iota(jnp.int32, (SUB, ncam), 1) == ids[:, 0:1]
-    shots = jnp.dot(chosen.astype(jnp.float32), cameras_ref[...], precision=highest)
-    cam = [jnp.broadcast_to(shots[:, k : k + 1], (SUB, LANES)) for k in range(16)]
+    cam = [jnp.broadcast_to(ids[:, k : k + 1], (SUB, LANES)) for k in range(16)]
     top = (((me & 3) ^ (sub & 3)) * yrows).astype(jnp.float32)
-    lists = ids[:, LANES:]
+    lists = ids[:, 16 : 16 + listed]
     rows = outer * INNER
     for v in range(rows // SUB):
         owners = [2 * v, 2 * v + 1]
         first = jnp.where(sub < INNER, (me ^ masks[owners[0]]) * blocks, (me ^ masks[owners[1]]) * blocks)
         found = []
         for b in range(1, blocks):
-            same = (lists == first[:, : lists.shape[1]] + b).astype(jnp.float32)
+            same = (lists == (first[:, :listed] + b).astype(jnp.float32)).astype(jnp.float32)
             found.append(jnp.broadcast_to(jnp.max(same, axis=1, keepdims=True), (SUB, LANES)) > 0.5)
 
         def row(p):
@@ -225,31 +242,29 @@
         k1 = kxx * sx * sx + kxy * sx * sy + kyy * sy * sy + lo
         for m, value in enumerate([kxx, kxy, kyy, kx, ky, k1, *tint]):
             feat[m * rows + v * SUB : m * rows + (v + 1) * SUB, :] = value
-    feat[...] = exact_pick(feat[...], order_ref[...])
+    feat[...] = exact_pick(feat[...], segment_order(False))
     for j in range(INNER):
         outs[j][...] = feat[pl.ds(j, COEFS * outer, stride=INNER), :]
 
 
 def render_kernel(
-    pixels, blocks, hop_bits, me_ref, cam_id_ref, count_ref, list_ref, depth_ref, cameras_ref,
-    src0, src1, src2, src3, target_ref, basis_ref, xmom_ref, back_ref, out_ref,
+    pixels, blocks, listed, hop_bits, me_ref, pack_ref, ids_ref, src0, src1, src2, src3, target_ref,
+    basis_ref, out_ref,
     raw, coef, shade, stage_a, stage_b, gaps_a, gaps_b, alphas, weights, carry, before, passed,
     colours, resid, mirror, pulls, behind, sums_a, sums_b, found, rows, slots,
 ):
-    listed = list_ref.shape[0]
     peers = out_ref.shape[0]
     outer = peers // INNER
     per_owner = blocks
     yrows = pixels // LANES
     groups = LANES // SUB
     me = me_ref[0]
-    count = count_ref[0]
-    cam_id = cam_id_ref[0]
+    count = pack_ref[0, 2 * listed]
     top = ((me % 4) * yrows).astype(jnp.float32)
 
     def place_slot(j, ends):
         live_end, dead_end = ends
-        slot = depth_ref[j]
+        slot = pack_ref[0, listed + j]
         live = slot < count
         slots[jnp.where(live, live_end, dead_end)] = slot
         return jnp.where(live, live_end + 1, live_end), jnp.where(live, dead_end, dead_end + 1)
@@ -263,7 +278,7 @@
         coef[k * KDIM + 5 : k * KDIM + 6, :] = jnp.full((1, LANES), -4096.0)
 
     def fetch(k, _):
-        apart = me ^ (list_ref[slots[k]] // per_owner)
+        apart = me ^ (pack_ref[0, slots[k]] // per_owner)
         near = sum((((apart >> bit) & 1) << t) for t, bit in enumerate(hop_bits))
         start = (apart & (INNER - 1)) * (COEFS * outer) + near
         value = raw[pl.ds(start, COEFS, stride=outer), :]
@@ -427,12 +442,18 @@
             for m, value in enumerate(run):
                 sums[m * LANES + i * SUB : m * LANES + (i + 1) * SUB, :] = value
 
+    across = (lax.broadcasted_iota(jnp.int32, (SUB, LANES), 1) - 64).astype(jnp.float32)
+    square = across * across
+    coarse = square.astype(jnp.bfloat16).astype(jnp.float32)
+    xmom = jnp.where(sub == 0, one, jnp.where(sub == 1, across, none))
+    xmom = jnp.where(sub == 2, coarse, jnp.where(sub == 3, square - coarse, xmom))
+    xmom = xmom.astype(jnp.bfloat16)
+
     def moments(k, sums):
         value = sums[...]
         high = value.astype(jnp.bfloat16)
         low = (value - high.astype(jnp.float32)).astype(jnp.bfloat16)
         contract = (((1,), (1,)), ((), ()))
-        xmom = xmom_ref[...]
         found[k] = lax.dot_general(
             xmom, high, contract, preferred_element_type=jnp.float32
         ) + lax.dot_general(xmom, low, contract, preferred_element_type=jnp.float32)
@@ -466,9 +487,8 @@
     moments(0, sums_b)
 
     lane = lax.broadcasted_iota(jnp.int32, (1, LANES), 1)
-    meta = jnp.where(lane == 17, top, 0.0)
-    for c in range(16):
-        meta = jnp.where(lane == c, cameras_ref[cam_id, c], meta)
+    camera = jnp.concatenate([ids_ref[...], jnp.zeros((1, LANES - ids_ref.shape[1]), jnp.float32)], 1)
+    meta = jnp.where(lane < 16, camera, jnp.where(lane == 17, top, 0.0))
 
     rows[...] = jnp.zeros(rows.shape, jnp.float32)
 
@@ -484,7 +504,7 @@
         return 0
 
     lax.fori_loop(0, count, gather_moments, 0)
-    rows[...] = exact_pick(rows[...], back_ref[...])
+    rows[...] = exact_pick(rows[...], segment_order(True))
 
     if peers > listed:
         absent = jnp.where(lane == 16, -1.0, 0.0)
@@ -492,7 +512,7 @@
             out_ref[peer] = jnp.broadcast_to(absent, (MSG, LANES))
 
     def send(k, _):
-        block = list_ref[slots[k]]
+        block = pack_ref[0, slots[k]]
         owner = block // per_owner
         place = (block % per_owner).astype(jnp.float32)
         rows[pl.ds(k * MSG + 9, 1), :] = jnp.where(lane == 16, place, meta)
@@ -658,13 +678,7 @@
     for c in range(3):
         part[COEFS - 3 + c, pixels + c * LANES : pixels + (c + 1) * LANES] = 1.0
     basis = np.concatenate([part] * 3)
-    xmom = np.zeros((SUB, LANES), np.float32)
-    xmom[:4] = [np.ones(LANES), x[:LANES], square[:LANES], (x * x - square)[:LANES]]
-    order = np.zeros((LANES, LANES), np.float32)
-    groups = LANES // SUB
-    for r in range(LANES):
-        order[(r % SUB) * groups + r // SUB, r] = 1.0
-    return [jnp.asarray(value, jnp.bfloat16) for value in (basis, xmom, order, order.T)]
+    return jnp.asarray(basis, jnp.bfloat16)
 
 
 def vmem(number=1):
@@ -693,19 +707,29 @@
     outer = peers // INNER
     f32 = jnp.float32
     shape_of = jax.ShapeDtypeStruct
-    basis, xmom, order, back = constants(pixels)
+    basis = constants(pixels)
 
     def swap(value, mask):
         return lax.ppermute(value, "tile", [(i, i ^ mask) for i in range(peers)])
 
     hop_bits = list(reversed(range(2, peers.bit_length() - 1)))
-    ids = jnp.concatenate(
-        [jnp.broadcast_to(camera_ids, (1, LANES)), block_lists[0]], axis=1
-    )
-    everything = own[None]
+    mine, pack, held = pl.pallas_call(
+        pack_kernel,
+        out_shape=(
+            shape_of((1, 16 + listed), f32),
+            shape_of((1, 3 * listed), jnp.int32),
+            shape_of(own.shape, f32),
+        ),
+        in_specs=smem(2) + vmem(4),
+        out_specs=tuple(vmem(3)),
+        compiler_params=params_with(8),
+        name="pack",
+    )(camera_ids, block_counts, block_lists[0], depth_order[0], cameras, own)
+    ids = mine
+    everything = held[None]
     masks = [0]
     for step, bit in enumerate(hop_bits):
-        arrived = swap(everything, 1 << bit)
+        arrived = swap(own[None] if step == 0 else everything, 1 << bit)
         if step < 2:
             ids = jnp.concatenate([ids, swap(ids, 1 << step)], 0)
         everything = jnp.concatenate([everything, arrived], 0)
@@ -740,23 +764,23 @@
         out_specs=tuple(vmem(4)),
         compiler_params=params_with(8),
         name="prepare",
-    )(group, own, prior, dual, step_sizes, share, *lists)
+    )(group, held, prior, dual, step_sizes, share, *lists)
 
     messages = pl.pallas_call(
-        functools.partial(project_kernel, masks, yrows),
+        functools.partial(project_kernel, masks, yrows, listed),
         out_shape=tuple([shape_of((COEFS * outer, LANES), f32)] * INNER),
-        in_specs=smem() + vmem(4),
+        in_specs=smem() + vmem(2),
         out_specs=tuple(vmem(INNER)),
         scratch_shapes=[pltpu.VMEM((COEFS * outer * INNER, LANES), f32)],
         compiler_params=params_with(8),
         name="project",
-    )(me, everything, ids, cameras, order)
+    )(me, everything, ids)
     sources = [messages[0]] + [swap(messages[j], j) for j in range(1, INNER)]
 
     outbox = pl.pallas_call(
-        functools.partial(render_kernel, pixels, blocks, hop_bits),
+        functools.partial(render_kernel, pixels, blocks, listed, hop_bits),
         out_shape=shape_of((peers, MSG, LANES), f32),
-        in_specs=smem(6) + vmem(INNER + 4),
+        in_specs=smem(2) + vmem(INNER + 3),
         out_specs=vmem()[0],
         scratch_shapes=[
             pltpu.VMEM((COEFS * peers, LANES), f32),
@@ -785,8 +809,7 @@
         compiler_params=params_with(48),
         name="render",
     )(
-        me, camera_ids[0], block_counts[0], block_lists[0, 0], depth_order[0, 0], cameras,
-        *sources, targets[0, 0], basis, xmom, back,
+        me, pack, mine, *sources, targets[0, 0], basis,
     )
     inbox = lax.all_to_all(outbox, "tile", split_axis=0, concat_axis=0, tiled=True)
     updated, shifted, sent = pl.pallas_call(
@@ -801,7 +824,7 @@
         scratch_shapes=[pltpu.VMEM((params * blocks, LANES), f32)] * 2,
         compiler_params=params_with(16),
         name="owner",
-    )(inbox.reshape(peers * MSG, LANES), own, base, dual, steps, pick)
+    )(inbox.reshape(peers * MSG, LANES), held, base, dual, steps, pick)
     new_duals = jnp.zeros_like(shifted)
     for n, route in enumerate(routes):
         theirs = lax.ppermute(sent[n], "scene", route)

time: 55.9 us -> 54 us (0.966)
  other arithmetic: 1.69 us -> 0.86 us
  starting transfers between devices: 16.8 us -> 16 us
  waiting for transfers between devices: 12.8 us -> 13.4 us
    all_to_all x1, starting transfers between devices: 4.63 us -> 3.64 us  [on_device(): lax.all_to_all(outbox, 'tile', split_axis=0, concat_axis=0, tiled=True)]
    concatenate x2, other arithmetic: 0.99 us -> 0.17 us  [on_device(): everything = jnp.concatenate([everything, arrived], 0)]
    ppermute x7, waiting for transfers between devices: 5.93 us -> 6.6 us  [swap(): return lax.ppermute(value, 'tile', [(i, i ^ mask) for i in range(peers)])]
    unnamed x27 -> x21, local copies, waits for them, and re-layouts: 3.29 us -> 2.83 us
    pallas_call x2 -> x3, Pallas kernels: 16.9 us -> 16.6 us  [the longest x1 16.1 us: on_device(): pl.pallas_call(functools.partial(render_kernel, pixels, blocks, listed, h...]
  transfers between devices with their start and end apart: 10 -> 10, of which waited for: 7 -> 8; matrix products, arithmetic and copies ran while one was open for 2% -> 0% of each run, Pallas kernels for 1% -> 2%
where the time goes in v5:
time: 54 us; the launch traced here: 53.8 us
  Pallas kernels  18.6 us (34%)
  starting transfers between devices  16 us (30%)
  waiting for transfers between devices  13.4 us (25%)
  local copies, waits for them, and re-layouts  2.83 us (5%)
  between operations  2.04 us (4%)
  other arithmetic  0.86 us (2%)
    pallas_call x1, Pallas kernels, on_device(): pl.pallas_call(functools.partial(render_kernel, pixels, blocks, listed, h...  16.1 us
    ppermute x7, starting transfers between devices, swap(): return lax.ppermute(value, 'tile', [(i, i ^ mask) for i in range(peers)])  12.4 us
    ppermute x7, waiting for transfers between devices, swap(): return lax.ppermute(value, 'tile', [(i, i ^ mask) for i in range(peers)])  6.6 us
    all_to_all x1, waiting for transfers between devices, on_device(): lax.all_to_all(outbox, 'tile', split_axis=0, concat_axis=0, tiled=True)  4.46 us
    all_to_all x1, starting transfers between devices, on_device(): lax.all_to_all(outbox, 'tile', split_axis=0, concat_axis=0, tiled=True)  3.64 us
    unnamed x21, local copies, waits for them, and re-layouts  2.83 us
    ppermute x1, waiting for transfers between devices, on_device(): theirs = lax.ppermute(sent[n], 'scene', route)  1.24 us
    pallas_call x1, Pallas kernels, on_device(): pl.pallas_call(owner_kernel, out_shape=(shape_of(own.shape, f32), shape_o...  1.16 us
  transfers between devices with their start and end apart: 10, of which 8 were waited for; matrix products, arithmetic and copies ran while one was open for 0% of the time, Pallas kernels for 2%

profile of v5, /device:TPU:0, one launch (start us, length us, event | category | flops | bytes accessed | tf_op | source)
XLA Modules:
  0.0 53.8 jit_solution(9194282511403771856)
XLA Ops:
  0.6 0.0 copy-start.4
  0.6 4.1 %collective-permute-start = (f32[1,59,2,128]{3,2,1,0:T(2,128)}, f32[1,59,2,128]{3,2,1,0:T(2,128)S(1)}, u32[]{:S(2)}, u32[]{:S(2)}) collective-permute-start(f32[1,59,2,128]{3,2,1,0:T(2,128)} %bitcast.38), channel_id=1, source_target_pairs={{0,8},{1,9},{2,10},{3,11},{4,12},{5,13},{6,14},{7,15},{8,0},{9,1},... | collective-permute-start | bytes 181256 | tf_op jit(solution)/shard_map/ppermute | solution.py:713
  6.0 0.0 copy-start.6
  6.0 0.0 copy-start.7
  6.1 0.0 copy-done.4
  6.1 0.6 %copy-done.6 = s32[1,1,16]{2,1,0:T(1,128)S(1)} copy-done((s32[1,1,16]{2,1,0:T(1,128)S(1)}, s32[1,1,16]{2,1,0:T(1,128)}, u32[]{:S(2)}) %copy-start.6) | copy-done | bytes 88
  6.7 0.0 copy-done.7
  6.7 0.0 copy-start.3
  6.7 0.8 %copy-done.3 = f32[1,2,59,128]{3,1,2,0:T(2,128)S(1)} copy-done((f32[1,2,59,128]{3,1,2,0:T(2,128)S(1)}, f32[1,2,59,128]{3,1,2,0:T(2,128)}, u32[]{:S(2)}) %copy-start.3) | copy-done | bytes 60440
  7.5 0.1 pack.1
  7.6 1.5 %collective-permute-start.2 = (f32[1,32]{1,0:T(1,128)S(1)}, f32[1,32]{1,0:T(1,128)S(1)}, u32[]{:S(2)}, u32[]{:S(2)}) collective-permute-start(f32[1,32]{1,0:T(1,128)S(1)} %get-tuple-element.17.ids_ref), channel_id=1, source_target_pairs={{0,1},{1,0},{2,3},{3,2},{4,5},{5,4},{6,7},{7,6},{8,9},{9,8},{10,11... | collective-permute-start | bytes 392 | tf_op jit(solution)/shard_map/ppermute | solution.py:713
  9.1 0.0 collective-permute-done
  9.1 0.1 pad_maximum_fusion.1
  9.2 1.6 %collective-permute-start.1 = (f32[2,59,2,128]{3,2,1,0:T(2,128)S(1)}, f32[2,59,2,128]{3,2,1,0:T(2,128)S(1)}, u32[]{:S(2)}, u32[]{:S(2)}) collective-permute-start(f32[2,59,2,128]{3,2,1,0:T(2,128)S(1)} %pad_maximum_fusion.1), channel_id=1, source_target_pairs={{0,4},{1,5},{2,6},{3,7},{4,0},{5,1},{6,2},{7,3},{8,12},{9,13},{10,... | collective-permute-start | bytes 362504 | tf_op jit(solution)/shard_map/ppermute | solution.py:713
  10.8 0.3 collective-permute-done.2
  11.2 1.6 %collective-permute-start.3 = (f32[2,32]{1,0:T(2,128)S(1)}, f32[2,32]{1,0:T(2,128)S(1)}, u32[]{:S(2)}, u32[]{:S(2)}) collective-permute-start(f32[2,32]{1,0:T(2,128)S(1)} %pad_maximum_fusion.3), channel_id=1, source_target_pairs={{0,2},{1,3},{2,0},{3,1},{4,6},{5,7},{6,4},{7,5},{8,10},{9,11},{10,... | collective-permute-start | bytes 776 | tf_op jit(solution)/shard_map/ppermute | solution.py:713
  12.7 2.0 %collective-permute-done.3 = f32[2,32]{1,0:T(2,128)S(1)} collective-permute-done((f32[2,32]{1,0:T(2,128)S(1)}, f32[2,32]{1,0:T(2,128)S(1)}, u32[]{:S(2)}, u32[]{:S(2)}) %collective-permute-start.3) | collective-permute-done | bytes 288 | tf_op jit(solution)/shard_map/ppermute | solution.py:713
  14.8 0.0 collective-permute-done.1
  14.8 0.1 pad_maximum_fusion.raw_ref
  14.9 0.0 copy-start.9
  14.9 0.0 copy-start.1
  15.0 0.4 project.1
  15.4 1.6 %collective-permute-start.4 = (f32[36,128]{1,0:T(8,128)S(1)}, f32[36,128]{1,0:T(8,128)S(1)}, u32[]{:S(2)}, u32[]{:S(2)}) collective-permute-start(f32[36,128]{1,0:T(8,128)S(1)} %get-tuple-element.20), channel_id=1, source_target_pairs={{0,1},{1,0},{2,3},{3,2},{4,5},{5,4},{6,7},{7,6},{8,9},{9,8},{10,11... | collective-permute-start | bytes 55304 | tf_op jit(solution)/shard_map/ppermute | solution.py:713
  17.0 1.5 %collective-permute-start.5 = (f32[36,128]{1,0:T(8,128)S(1)}, f32[36,128]{1,0:T(8,128)S(1)}, u32[]{:S(2)}, u32[]{:S(2)}) collective-permute-start(f32[36,128]{1,0:T(8,128)S(1)} %get-tuple-element.21), channel_id=1, source_target_pairs={{0,2},{1,3},{2,0},{3,1},{4,6},{5,7},{6,4},{7,5},{8,10},{9,11},{10,... | collective-permute-start | bytes 55304 | tf_op jit(solution)/shard_map/ppermute | solution.py:713
  18.5 0.5 collective-permute-start.6
  19.0 0.0 copy-done.9
  19.0 0.3 collective-permute-done.4.src1
  19.3 1.5 %collective-permute-done.5.src2 = f32[36,128]{1,0:T(8,128)S(1)} collective-permute-done((f32[36,128]{1,0:T(8,128)S(1)}, f32[36,128]{1,0:T(8,128)S(1)}, u32[]{:S(2)}, u32[]{:S(2)}) %collective-permute-start.5) | collective-permute-done | bytes 18464 | tf_op jit(solution)/shard_map/ppermute | solution.py:713
  20.7 2.4 %collective-permute-done.6.src3 = f32[36,128]{1,0:T(8,128)S(1)} collective-permute-done((f32[36,128]{1,0:T(8,128)S(1)}, f32[36,128]{1,0:T(8,128)S(1)}, u32[]{:S(2)}, u32[]{:S(2)}) %collective-permute-start.6) | collective-permute-done | bytes 18464 | tf_op jit(solution)/shard_map/ppermute | solution.py:713
  23.2 0.0 copy-done.1
  23.2 16.1 %render.1 = f32[16,16,128]{2,1,0:T(8,128)} custom-call(s32[1]{0:T(128)} %bitcast.me_ref, s32[1,48]{1,0:T(1,128)S(1)} %get-tuple-element.16.pack_ref, f32[1,32]{1,0:T(1,128)S(1)} %get-tuple-element.17.ids_ref, f32[36,128]{1,0:T(8,128)S(1)} %get-tuple-element.19.src0, f32[36,128]{1,0:T(8,128)S(1)} %collective-permute-done.4.src1, ...), custom_call_target="tpu_custom_call" | custom-call | tf_op jit(solution)/shard_map/render/pallas_call | solution.py:780
  39.3 0.0 copy-start
  39.3 0.0 copy-start.2
  39.3 3.6 %all-to-all-start = ((f32[16,16,128]{2,1,0:T(8,128)}), f32[16,16,128]{2,1,0:T(8,128)S(1)}, u32[]{:S(2)}, u32[]{:S(2)}) async-start(f32[16,16,128]{2,1,0:T(8,128)} %render.1), calls=%async_computation | async-start | bytes 262144 | tf_op jit(solution)/shard_map/all_to_all | solution.py:814
  42.9 0.0 copy-start.5
  42.9 0.7 %copy-done.5 = s32[1,1,2,64]{3,2,1,0:T(2,128)S(1)} copy-done((s32[1,1,2,64]{3,2,1,0:T(2,128)S(1)}, s32[1,1,2,64]{3,2,1,0:T(2,128)}, u32[]{:S(2)}) %copy-start.5) | copy-done | bytes 536
  43.6 0.0 collective-permute-start.7
  43.6 1.1 %collective-permute-done.7.refs_0_ = s32[2,64]{1,0:T(2,128)S(1)} collective-permute-done((s32[2,64]{1,0:T(2,128)S(1)}, s32[2,64]{1,0:T(2,128)S(1)}, u32[]{:S(2)}, u32[]{:S(2)}) %collective-permute-start.7) | collective-permute-done | bytes 544 | tf_op jit(solution)/shard_map/ppermute | solution.py:753
  44.8 0.0 copy-start.8
  44.8 0.0 copy-done
  44.8 0.0 copy-done.2
  44.8 0.6 %copy-done.8 = f32[59]{0:T(128)S(1)} copy-done((f32[59]{0:T(128)S(1)}, f32[59]{0:T(128)}, u32[]{:S(2)}) %copy-start.8) | copy-done | bytes 260
  45.4 0.8 %prepare.1 = (f32[59,2,128]{2,1,0:T(2,128)S(1)}, f32[59,2,128]{2,1,0:T(2,128)S(1)}, bf16[1,256,256]{2,1,0:T(8,128)(2,1)S(1)}, f32[1,2,128]{2,1,0:T(2,128)S(1)}) custom-call(s32[1]{0:T(128)} %bitcast.9.group_ref, f32[59,2,128]{2,1,0:T(2,128)S(1)} %get-tuple-element.18.own_ref, f32[59,2,128]{2,1,0:T(2,128)S(1)} %bitcast.37, f32[59,2,128]{2,1,0:T(2,128)S(1)} %bitcast.34, ...), custom_call_target="tpu_custom_call" | custom-call | tf_op jit(solution)/shard_map/prepare/pallas_call | solution.py:755
  46.2 4.5 %all-to-all-done = f32[16,16,128]{2,1,0:T(8,128)S(1)} async-done(((f32[16,16,128]{2,1,0:T(8,128)}), f32[16,16,128]{2,1,0:T(8,128)S(1)}, u32[]{:S(2)}, u32[]{:S(2)}) %all-to-all-start) | async-done | bytes 131104 | tf_op jit(solution)/shard_map/all_to_all | solution.py:814
  50.7 1.2 %owner.1 = (f32[59,2,128]{2,1,0:T(2,128)}, f32[59,2,128]{2,1,0:T(2,128)S(1)}, f32[1,59,2,128]{3,2,1,0:T(2,128)S(1)}) custom-call(f32[256,128]{1,0:T(8,128)S(1)} %bitcast.33, f32[59,2,128]{2,1,0:T(2,128)S(1)} %get-tuple-element.18.own_ref, f32[59,2,128]{2,1,0:T(2,128)S(1)} %get-tuple-element.23.base_ref, f32[59,2,128]{2,1,0:T(2,128)S(1)} %bitcast.35, ...), custom_call_target="tpu_custom_call" | custom-call | tf_op jit(solution)/shard_map/owner/pallas_call | solution.py:815
  51.9 0.0 collective-permute-start.8
  51.9 1.2 %collective-permute-done.8 = f32[59,2,128]{2,1,0:T(2,128)S(1)} collective-permute-done((f32[59,2,128]{2,1,0:T(2,128)S(1)}, f32[59,2,128]{2,1,0:T(2,128)S(1)}, u32[]{:S(2)}, u32[]{:S(2)}) %collective-permute-start.8) | collective-permute-done | bytes 60448 | tf_op jit(solution)/shard_map/ppermute | solution.py:830
  53.1 0.7 %select_bitcast_fusion = f32[1,2,59,128]{3,1,2,0:T(2,128)} fusion(f32[59,2,128]{2,1,0:T(2,128)S(1)} %get-tuple-element.28, f32[59,2,128]{2,1,0:T(2,128)S(1)} %collective-permute-done.8, pred[2,128]{1,0:T(4,128)(4,1)S(1)} %compare_bitcast_fusion), kind=kLoop, calls=%fused_computation.2 | loop fusion | flops 60416 | bytes 181504 | tf_op jit(solution)/shard_map/broadcast_in_dim | solution.py:833
  (4 shorter events, 0.0 us)
Async XLA Ops:
  0.6 5.4 %copy-start.4 = (f32[16,16]{1,0:T(8,128)S(1)}, f32[16,16]{1,0:T(8,128)}, u32[]{:S(2)}) copy-start(f32[16,16]{1,0:T(8,128)} %cameras_ref.1) | copy-start | bytes 3076
  0.6 8.5 %collective-permute-start = (f32[1,59,2,128]{3,2,1,0:T(2,128)}, f32[1,59,2,128]{3,2,1,0:T(2,128)S(1)}, u32[]{:S(2)}, u32[]{:S(2)}) collective-permute-start(f32[1,59,2,128]{3,2,1,0:T(2,128)} %bitcast.38), channel_id=1, source_target_pairs={{0,8},{1,9},{2,10},{3,11},{4,12},{5,13},{6,14},{7,15},{8,0},{9,1},... | collective-permute-start | bytes 181256 | tf_op jit(solution)/shard_map/ppermute | solution.py:713
  6.0 0.7 %copy-start.6 = (s32[1,1,16]{2,1,0:T(1,128)S(1)}, s32[1,1,16]{2,1,0:T(1,128)}, u32[]{:S(2)}) copy-start(s32[1,1,16]{2,1,0:T(1,128)} %param.18) | copy-start | bytes 196
  6.0 0.7 %copy-start.7 = (s32[1,1,16]{2,1,0:T(1,128)S(1)}, s32[1,1,16]{2,1,0:T(1,128)}, u32[]{:S(2)}) copy-start(s32[1,1,16]{2,1,0:T(1,128)} %param.19) | copy-start | bytes 196
  6.7 0.8 %copy-start.3 = (f32[1,2,59,128]{3,1,2,0:T(2,128)S(1)}, f32[1,2,59,128]{3,1,2,0:T(2,128)}, u32[]{:S(2)}) copy-start(f32[1,2,59,128]{3,1,2,0:T(2,128)} %param.12) | copy-start | bytes 181252
  7.6 3.5 %collective-permute-start.2 = (f32[1,32]{1,0:T(1,128)S(1)}, f32[1,32]{1,0:T(1,128)S(1)}, u32[]{:S(2)}, u32[]{:S(2)}) collective-permute-start(f32[1,32]{1,0:T(1,128)S(1)} %get-tuple-element.17.ids_ref), channel_id=1, source_target_pairs={{0,1},{1,0},{2,3},{3,2},{4,5},{5,4},{6,7},{7,6},{8,9},{9,8},{10,11... | collective-permute-start | bytes 392 | tf_op jit(solution)/shard_map/ppermute | solution.py:713
  9.2 5.6 %collective-permute-start.1 = (f32[2,59,2,128]{3,2,1,0:T(2,128)S(1)}, f32[2,59,2,128]{3,2,1,0:T(2,128)S(1)}, u32[]{:S(2)}, u32[]{:S(2)}) collective-permute-start(f32[2,59,2,128]{3,2,1,0:T(2,128)S(1)} %pad_maximum_fusion.1), channel_id=1, source_target_pairs={{0,4},{1,5},{2,6},{3,7},{4,0},{5,1},{6,2},{7,3},{8,12},{9,13},{10,... | collective-permute-start | bytes 362504 | tf_op jit(solution)/shard_map/ppermute | solution.py:713
  11.2 3.6 %collective-permute-start.3 = (f32[2,32]{1,0:T(2,128)S(1)}, f32[2,32]{1,0:T(2,128)S(1)}, u32[]{:S(2)}, u32[]{:S(2)}) collective-permute-start(f32[2,32]{1,0:T(2,128)S(1)} %pad_maximum_fusion.3), channel_id=1, source_target_pairs={{0,2},{1,3},{2,0},{3,1},{4,6},{5,7},{6,4},{7,5},{8,10},{9,11},{10,... | collective-permute-start | bytes 776 | tf_op jit(solution)/shard_map/ppermute | solution.py:713
  14.9 4.0 %copy-start.9 = (f32[1,1,3,1024]{3,1,2,0:T(1,128)S(1)}, f32[1,1,3,1024]{3,1,2,0:T(1,128)}, u32[]{:S(2)}) copy-start(f32[1,1,3,1024]{3,1,2,0:T(1,128)} %param.21) | copy-start | bytes 36868
  14.9 8.2 %copy-start.1 = (bf16[48,1408]{1,0:T(8,128)(2,1)S(1)}, bf16[48,1408]{1,0:T(8,128)(2,1)}, u32[]{:S(2)}) copy-start(bf16[48,1408]{1,0:T(8,128)(2,1)} %constant.16.clone.basis_ref) | copy-start | bytes 405508
  15.4 3.8 %collective-permute-start.4 = (f32[36,128]{1,0:T(8,128)S(1)}, f32[36,128]{1,0:T(8,128)S(1)}, u32[]{:S(2)}, u32[]{:S(2)}) collective-permute-start(f32[36,128]{1,0:T(8,128)S(1)} %get-tuple-element.20), channel_id=1, source_target_pairs={{0,1},{1,0},{2,3},{3,2},{4,5},{5,4},{6,7},{7,6},{8,9},{9,8},{10,11... | collective-permute-start | bytes 55304 | tf_op jit(solution)/shard_map/ppermute | solution.py:713
  17.0 3.8 %collective-permute-start.5 = (f32[36,128]{1,0:T(8,128)S(1)}, f32[36,128]{1,0:T(8,128)S(1)}, u32[]{:S(2)}, u32[]{:S(2)}) collective-permute-start(f32[36,128]{1,0:T(8,128)S(1)} %get-tuple-element.21), channel_id=1, source_target_pairs={{0,2},{1,3},{2,0},{3,1},{4,6},{5,7},{6,4},{7,5},{8,10},{9,11},{10,... | collective-permute-start | bytes 55304 | tf_op jit(solution)/shard_map/ppermute | solution.py:713
  18.5 4.7 %collective-permute-start.6 = (f32[36,128]{1,0:T(8,128)S(1)}, f32[36,128]{1,0:T(8,128)S(1)}, u32[]{:S(2)}, u32[]{:S(2)}) collective-permute-start(f32[36,128]{1,0:T(8,128)S(1)} %get-tuple-element.22), channel_id=1, source_target_pairs={{0,3},{1,2},{2,1},{3,0},{4,7},{5,6},{6,5},{7,4},{8,11},{9,10},{10,... | collective-permute-start | bytes 55304 | tf_op jit(solution)/shard_map/ppermute | solution.py:713
  39.3 5.5 %copy-start = (f32[1,2,59,128]{3,1,2,0:T(2,128)S(1)}, f32[1,2,59,128]{3,1,2,0:T(2,128)}, u32[]{:S(2)}) copy-start(f32[1,2,59,128]{3,1,2,0:T(2,128)} %param.14) | copy-start | bytes 181252
  39.3 5.5 %copy-start.2 = (f32[1,2,59,128]{3,1,2,0:T(2,128)S(1)}, f32[1,2,59,128]{3,1,2,0:T(2,128)}, u32[]{:S(2)}) copy-start(f32[1,2,59,128]{3,1,2,0:T(2,128)} %param.13) | copy-start | bytes 181252
  39.3 11.4 %all-to-all-start = ((f32[16,16,128]{2,1,0:T(8,128)}), f32[16,16,128]{2,1,0:T(8,128)S(1)}, u32[]{:S(2)}, u32[]{:S(2)}) async-start(f32[16,16,128]{2,1,0:T(8,128)} %render.1), calls=%async_computation | async-start | bytes 262144 | tf_op jit(solution)/shard_map/all_to_all | solution.py:814
  42.9 0.7 %copy-start.5 = (s32[1,1,2,64]{3,2,1,0:T(2,128)S(1)}, s32[1,1,2,64]{3,2,1,0:T(2,128)}, u32[]{:S(2)}) copy-start(s32[1,1,2,64]{3,2,1,0:T(2,128)} %param.22) | copy-start | bytes 1540
  43.6 1.1 %collective-permute-start.7 = (s32[2,64]{1,0:T(2,128)S(1)}, s32[2,64]{1,0:T(2,128)S(1)}, u32[]{:S(2)}, u32[]{:S(2)}) collective-permute-start(s32[2,64]{1,0:T(2,128)S(1)} %bitcast.40), channel_id=1, source_target_pairs={{0,16},{16,0},{1,17},{17,1},{2,18},{18,2},{3,19},{19,3},{4,20},{20... | collective-permute-start | bytes 1544 | tf_op jit(solution)/shard_map/ppermute | solution.py:753
  44.8 0.7 %copy-start.8 = (f32[59]{0:T(128)S(1)}, f32[59]{0:T(128)}, u32[]{:S(2)}) copy-start(f32[59]{0:T(128)} %step_ref.1) | copy-start | bytes 712
  51.9 1.2 %collective-permute-start.8 = (f32[59,2,128]{2,1,0:T(2,128)S(1)}, f32[59,2,128]{2,1,0:T(2,128)S(1)}, u32[]{:S(2)}, u32[]{:S(2)}) collective-permute-start(f32[59,2,128]{2,1,0:T(2,128)S(1)} %bitcast.44), channel_id=1, source_target_pairs={{0,16},{16,0},{1,17},{17,1},{2,18},{18,2},{3,19},{19,3},{4,20},{20... | collective-permute-start | bytes 181256 | tf_op jit(solution)/shard_map/ppermute | solution.py:830

commit v6 on v5

--- a/solution.py
+++ b/solution.py
@@ -250,7 +250,7 @@
 def render_kernel(
     pixels, blocks, listed, hop_bits, me_ref, pack_ref, ids_ref, src0, src1, src2, src3, target_ref,
     basis_ref, out_ref,
-    raw, coef, shade, stage_a, stage_b, gaps_a, gaps_b, alphas, weights, carry, before, passed,
+    raw, coef, lefts, shade, gaps_a, gaps_b, alphas, weights, carry, before, passed,
     colours, resid, mirror, pulls, behind, sums_a, sums_b, found, rows, slots,
 ):
     peers = out_ref.shape[0]
@@ -307,38 +307,35 @@
     def rows_at(start, size, step):
         return pl.ds(pl.multiple_of(start, step), size)
 
-    def product(k, right, out, finish):
-        mine = coef[rows_at(k * KDIM, KDIM, PART), :].T.astype(jnp.bfloat16)
+    for k in range(coef.shape[0] // KDIM):
+        mine = coef[k * KDIM : (k + 1) * KDIM, :].T
+        lefts[k * LANES : (k + 1) * LANES, :] = mine.astype(jnp.bfloat16)
+
+    def left(k):
+        return lefts[rows_at(k * LANES, LANES, LANES), :]
+
+    def times(mine, right, start, width):
+        here = slice(start, start + width)
+        return jnp.dot(mine, right[:, here], preferred_element_type=jnp.float32)
+
+    def chain(k):
+        base = pl.multiple_of(k * LANES, LANES)
+        mine = left(k)
         for start in range(0, pixels, WIDE):
-            here = slice(start, start + WIDE)
-            out[:, here] = finish(
-                jnp.dot(mine, right[:, here], preferred_element_type=jnp.float32)
-            )
-        if right.shape[1] > pixels:
-            shade[rows_at(k * LANES, LANES, LANES), :] = jnp.dot(
-                mine, right[:, pixels:], preferred_element_type=jnp.float32
-            )
-
-    def to_alpha(value):
-        return jnp.minimum(alpha_ceiling, jnp.exp2(value))
-
-    def as_it_is(value):
-        return value
-
-    def chain(k, stage):
-        base = pl.multiple_of(k * LANES, LANES)
-        kept = [one] * yrows
-        for i in range(groups):
-            here = rows_at(base + i * SUB, SUB, SUB)
-            for y in range(yrows):
-                lanes = slice(y * LANES, (y + 1) * LANES)
-                alpha = stage[i * SUB : (i + 1) * SUB, lanes]
-                weight = alpha * kept[y]
-                alphas[here, lanes] = alpha
-                weights[here, lanes] = weight
-                kept[y] = kept[y] - weight
-        for y in range(yrows):
-            passed[k, y] = kept[y]
+            value = jnp.minimum(alpha_ceiling, jnp.exp2(times(mine, basis_ref, start, WIDE)))
+            kept = [one] * (WIDE // LANES)
+            for i in range(groups):
+                here = rows_at(base + i * SUB, SUB, SUB)
+                for j in range(WIDE // LANES):
+                    alpha = value[i * SUB : (i + 1) * SUB, j * LANES : (j + 1) * LANES]
+                    weight = alpha * kept[j]
+                    lanes = slice(start + j * LANES, start + (j + 1) * LANES)
+                    alphas[here, lanes] = alpha
+                    weights[here, lanes] = weight
+                    kept[j] = kept[j] - weight
+            for j in range(WIDE // LANES):
+                passed[k, start // LANES + j] = kept[j]
+        shade[rows_at(k * LANES, LANES, LANES), :] = times(mine, basis_ref, pixels, 3 * LANES)
 
     def tally(k, ended):
         base = pl.multiple_of(k * LANES, LANES)
@@ -367,21 +364,15 @@
 
     pairs = (count + 1) // 2
     fresh = [[none] * (yrows // 2)] * 3
-    product(0, basis_ref, stage_a, to_alpha)
-    product(1, basis_ref, stage_b, to_alpha)
-
-    def advance(pair):
-        chain(2 * pair, stage_a)
-        product(2 * pair + 2, basis_ref, stage_a, to_alpha)
-        chain(2 * pair + 1, stage_b)
-        product(2 * pair + 3, basis_ref, stage_b, to_alpha)
+    chain(0)
+    chain(1)
 
     def forward(pair, _):
         tally(2 * pair - 1, tally(2 * pair - 2, fresh))
-        advance(pair)
+        chain(2 * pair)
+        chain(2 * pair + 1)
         return 0
 
-    advance(0)
     lax.fori_loop(1, pairs, forward, 0)
     tally(2 * pairs - 1, tally(2 * pairs - 2, fresh))
 
@@ -400,7 +391,7 @@
                     mirror[at + 4 : at + 5, lanes] = low
     pulls[...] = mirror[...].astype(jnp.bfloat16)
 
-    def follow(k, stage, gaps):
+    def follow(k, gaps):
         base = pl.multiple_of(k * LANES, LANES)
         rear = [None] * yrows
         for y in range(yrows):
@@ -415,13 +406,17 @@
                 sub < SUB - 1, sub_roll(value, -1) + sub_roll(gain, -1) * last, last
             )
             behind[y] = spread_row(value + gain * last, 0)
-        for i in reversed(range(groups)):
-            here = slice(i * SUB, (i + 1) * SUB)
-            for y in range(yrows):
-                lanes = slice(y * LANES, (y + 1) * LANES)
-                gap = stage[here, lanes] - rear[y]
-                gaps[here, lanes] = gap
-                rear[y] = rear[y] + alphas[rows_at(base + i * SUB, SUB, SUB), lanes] * gap
+        mine = left(k)
+        for start in range(0, pixels, WIDE):
+            value = times(mine, pulls, start, WIDE)
+            for i in reversed(range(groups)):
+                here = slice(i * SUB, (i + 1) * SUB)
+                for j in range(WIDE // LANES):
+                    y = start // LANES + j
+                    lanes = slice(y * LANES, (y + 1) * LANES)
+                    gap = value[here, j * LANES : (j + 1) * LANES] - rear[y]
+                    gaps[here, lanes] = gap
+                    rear[y] = rear[y] + alphas[rows_at(base + i * SUB, SUB, SUB), lanes] * gap
 
     def weigh(k, gaps, sums):
         base = pl.multiple_of(k * LANES, LANES)
@@ -459,14 +454,10 @@
         ) + lax.dot_general(xmom, low, contract, preferred_element_type=jnp.float32)
 
     rearmost = 2 * pairs - 1
-    product(rearmost, pulls, stage_a, as_it_is)
-    product(rearmost - 1, pulls, stage_b, as_it_is)
 
     def retreat(k):
-        follow(k, stage_a, gaps_a)
-        product(jnp.maximum(k - 2, 0), pulls, stage_a, as_it_is)
-        follow(k - 1, stage_b, gaps_b)
-        product(jnp.maximum(k - 3, 0), pulls, stage_b, as_it_is)
+        follow(k, gaps_a)
+        follow(k - 1, gaps_b)
 
     def collect(k):
         moments(k + 2, sums_a)
@@ -784,10 +775,9 @@
         out_specs=vmem()[0],
         scratch_shapes=[
             pltpu.VMEM((COEFS * peers, LANES), f32),
-            pltpu.VMEM(((listed + 2) * KDIM, LANES), f32),
-            pltpu.VMEM(((listed + 2) * LANES, 3 * LANES), f32),
-            pltpu.VMEM((LANES, pixels), f32),
-            pltpu.VMEM((LANES, pixels), f32),
+            pltpu.VMEM(((listed + 1) * KDIM, LANES), f32),
+            pltpu.VMEM(((listed + 1) * LANES, KDIM), jnp.bfloat16),
+            pltpu.VMEM(((listed + 1) * LANES, 3 * LANES), f32),
             pltpu.VMEM((LANES, pixels), f32),
             pltpu.VMEM((LANES, pixels), f32),
             pltpu.VMEM(((listed + 1) * LANES, pixels), f32),

time: 54 us -> 52.1 us (0.965)
  Pallas kernels: 18.6 us -> 16.7 us
    pallas_call x1, Pallas kernels: 16.1 us -> 14.2 us  [on_device(): pl.pallas_call(functools.partial(render_kernel, pixels, blocks, listed, h...]
where the time goes in v6:
time: 52.1 us; the launch traced here: 51.9 us
  Pallas kernels  16.7 us (32%)
  starting transfers between devices  16 us (31%)
  waiting for transfers between devices  13.4 us (26%)
  local copies, waits for them, and re-layouts  2.83 us (5%)
  between operations  2.04 us (4%)
  other arithmetic  0.86 us (2%)
    pallas_call x1, Pallas kernels, on_device(): pl.pallas_call(functools.partial(render_kernel, pixels, blocks, listed, h...  14.2 us
    ppermute x7, starting transfers between devices, swap(): return lax.ppermute(value, 'tile', [(i, i ^ mask) for i in range(peers)])  12.4 us
    ppermute x7, waiting for transfers between devices, swap(): return lax.ppermute(value, 'tile', [(i, i ^ mask) for i in range(peers)])  6.6 us
    all_to_all x1, waiting for transfers between devices, on_device(): lax.all_to_all(outbox, 'tile', split_axis=0, concat_axis=0, tiled=True)  4.46 us
    all_to_all x1, starting transfers between devices, on_device(): lax.all_to_all(outbox, 'tile', split_axis=0, concat_axis=0, tiled=True)  3.64 us
    unnamed x21, local copies, waits for them, and re-layouts  2.83 us
    ppermute x1, waiting for transfers between devices, on_device(): theirs = lax.ppermute(sent[n], 'scene', route)  1.24 us
    pallas_call x1, Pallas kernels, on_device(): pl.pallas_call(owner_kernel, out_shape=(shape_of(own.shape, f32), shape_o...  1.16 us
  transfers between devices with their start and end apart: 10, of which 8 were waited for; matrix products, arithmetic and copies ran while one was open for 0% of the time, Pallas kernels for 2%

profile of v6, /device:TPU:0, one launch (start us, length us, event | category | flops | bytes accessed | tf_op | source)
XLA Modules:
  0.0 51.9 jit_solution(2110027671922983882)
XLA Ops:
  0.6 0.0 copy-start.4
  0.6 4.1 %collective-permute-start = (f32[1,59,2,128]{3,2,1,0:T(2,128)}, f32[1,59,2,128]{3,2,1,0:T(2,128)S(1)}, u32[]{:S(2)}, u32[]{:S(2)}) collective-permute-start(f32[1,59,2,128]{3,2,1,0:T(2,128)} %bitcast.38), channel_id=1, source_target_pairs={{0,8},{1,9},{2,10},{3,11},{4,12},{5,13},{6,14},{7,15},{8,0},{9,1},... | collective-permute-start | bytes 181256 | tf_op jit(solution)/shard_map/ppermute | solution.py:704
  6.0 0.0 copy-start.6
  6.0 0.0 copy-start.7
  6.1 0.0 copy-done.4
  6.1 0.6 %copy-done.6 = s32[1,1,16]{2,1,0:T(1,128)S(1)} copy-done((s32[1,1,16]{2,1,0:T(1,128)S(1)}, s32[1,1,16]{2,1,0:T(1,128)}, u32[]{:S(2)}) %copy-start.6) | copy-done | bytes 88
  6.7 0.0 copy-done.7
  6.7 0.0 copy-start.3
  6.7 0.8 %copy-done.3 = f32[1,2,59,128]{3,1,2,0:T(2,128)S(1)} copy-done((f32[1,2,59,128]{3,1,2,0:T(2,128)S(1)}, f32[1,2,59,128]{3,1,2,0:T(2,128)}, u32[]{:S(2)}) %copy-start.3) | copy-done | bytes 60440
  7.5 0.1 pack.1
  7.6 1.5 %collective-permute-start.2 = (f32[1,32]{1,0:T(1,128)S(1)}, f32[1,32]{1,0:T(1,128)S(1)}, u32[]{:S(2)}, u32[]{:S(2)}) collective-permute-start(f32[1,32]{1,0:T(1,128)S(1)} %get-tuple-element.17.ids_ref), channel_id=1, source_target_pairs={{0,1},{1,0},{2,3},{3,2},{4,5},{5,4},{6,7},{7,6},{8,9},{9,8},{10,11... | collective-permute-start | bytes 392 | tf_op jit(solution)/shard_map/ppermute | solution.py:704
  9.1 0.0 collective-permute-done
  9.1 0.1 pad_maximum_fusion.1
  9.2 1.6 %collective-permute-start.1 = (f32[2,59,2,128]{3,2,1,0:T(2,128)S(1)}, f32[2,59,2,128]{3,2,1,0:T(2,128)S(1)}, u32[]{:S(2)}, u32[]{:S(2)}) collective-permute-start(f32[2,59,2,128]{3,2,1,0:T(2,128)S(1)} %pad_maximum_fusion.1), channel_id=1, source_target_pairs={{0,4},{1,5},{2,6},{3,7},{4,0},{5,1},{6,2},{7,3},{8,12},{9,13},{10,... | collective-permute-start | bytes 362504 | tf_op jit(solution)/shard_map/ppermute | solution.py:704
  10.8 0.3 collective-permute-done.2
  11.2 1.6 %collective-permute-start.3 = (f32[2,32]{1,0:T(2,128)S(1)}, f32[2,32]{1,0:T(2,128)S(1)}, u32[]{:S(2)}, u32[]{:S(2)}) collective-permute-start(f32[2,32]{1,0:T(2,128)S(1)} %pad_maximum_fusion.3), channel_id=1, source_target_pairs={{0,2},{1,3},{2,0},{3,1},{4,6},{5,7},{6,4},{7,5},{8,10},{9,11},{10,... | collective-permute-start | bytes 776 | tf_op jit(solution)/shard_map/ppermute | solution.py:704
  12.7 2.0 %collective-permute-done.3 = f32[2,32]{1,0:T(2,128)S(1)} collective-permute-done((f32[2,32]{1,0:T(2,128)S(1)}, f32[2,32]{1,0:T(2,128)S(1)}, u32[]{:S(2)}, u32[]{:S(2)}) %collective-permute-start.3) | collective-permute-done | bytes 288 | tf_op jit(solution)/shard_map/ppermute | solution.py:704
  14.8 0.0 collective-permute-done.1
  14.8 0.1 pad_maximum_fusion.raw_ref
  14.9 0.0 copy-start.9
  14.9 0.0 copy-start.1
  15.0 0.4 project.1
  15.4 1.6 %collective-permute-start.4 = (f32[36,128]{1,0:T(8,128)S(1)}, f32[36,128]{1,0:T(8,128)S(1)}, u32[]{:S(2)}, u32[]{:S(2)}) collective-permute-start(f32[36,128]{1,0:T(8,128)S(1)} %get-tuple-element.20), channel_id=1, source_target_pairs={{0,1},{1,0},{2,3},{3,2},{4,5},{5,4},{6,7},{7,6},{8,9},{9,8},{10,11... | collective-permute-start | bytes 55304 | tf_op jit(solution)/shard_map/ppermute | solution.py:704
  17.0 1.5 %collective-permute-start.5 = (f32[36,128]{1,0:T(8,128)S(1)}, f32[36,128]{1,0:T(8,128)S(1)}, u32[]{:S(2)}, u32[]{:S(2)}) collective-permute-start(f32[36,128]{1,0:T(8,128)S(1)} %get-tuple-element.21), channel_id=1, source_target_pairs={{0,2},{1,3},{2,0},{3,1},{4,6},{5,7},{6,4},{7,5},{8,10},{9,11},{10,... | collective-permute-start | bytes 55304 | tf_op jit(solution)/shard_map/ppermute | solution.py:704
  18.5 0.5 collective-permute-start.6
  19.0 0.0 copy-done.9
  19.0 0.3 collective-permute-done.4.src1
  19.3 1.5 %collective-permute-done.5.src2 = f32[36,128]{1,0:T(8,128)S(1)} collective-permute-done((f32[36,128]{1,0:T(8,128)S(1)}, f32[36,128]{1,0:T(8,128)S(1)}, u32[]{:S(2)}, u32[]{:S(2)}) %collective-permute-start.5) | collective-permute-done | bytes 18464 | tf_op jit(solution)/shard_map/ppermute | solution.py:704
  20.7 2.4 %collective-permute-done.6.src3 = f32[36,128]{1,0:T(8,128)S(1)} collective-permute-done((f32[36,128]{1,0:T(8,128)S(1)}, f32[36,128]{1,0:T(8,128)S(1)}, u32[]{:S(2)}, u32[]{:S(2)}) %collective-permute-start.6) | collective-permute-done | bytes 18464 | tf_op jit(solution)/shard_map/ppermute | solution.py:704
  23.2 0.0 copy-done.1
  23.2 14.2 %render.1 = f32[16,16,128]{2,1,0:T(8,128)} custom-call(s32[1]{0:T(128)} %bitcast.me_ref, s32[1,48]{1,0:T(1,128)S(1)} %get-tuple-element.16.pack_ref, f32[1,32]{1,0:T(1,128)S(1)} %get-tuple-element.17.ids_ref, f32[36,128]{1,0:T(8,128)S(1)} %get-tuple-element.19.src0, f32[36,128]{1,0:T(8,128)S(1)} %collective-permute-done.4.src1, ...), custom_call_target="tpu_custom_call" | custom-call | tf_op jit(solution)/shard_map/render/pallas_call | solution.py:771
  37.4 0.0 copy-start
  37.4 0.0 copy-start.2
  37.4 3.6 %all-to-all-start = ((f32[16,16,128]{2,1,0:T(8,128)}), f32[16,16,128]{2,1,0:T(8,128)S(1)}, u32[]{:S(2)}, u32[]{:S(2)}) async-start(f32[16,16,128]{2,1,0:T(8,128)} %render.1), calls=%async_computation | async-start | bytes 262144 | tf_op jit(solution)/shard_map/all_to_all | solution.py:804
  41.0 0.0 copy-start.5
  41.0 0.7 %copy-done.5 = s32[1,1,2,64]{3,2,1,0:T(2,128)S(1)} copy-done((s32[1,1,2,64]{3,2,1,0:T(2,128)S(1)}, s32[1,1,2,64]{3,2,1,0:T(2,128)}, u32[]{:S(2)}) %copy-start.5) | copy-done | bytes 536
  41.7 0.0 collective-permute-start.7
  41.7 1.1 %collective-permute-done.7.refs_0_ = s32[2,64]{1,0:T(2,128)S(1)} collective-permute-done((s32[2,64]{1,0:T(2,128)S(1)}, s32[2,64]{1,0:T(2,128)S(1)}, u32[]{:S(2)}, u32[]{:S(2)}) %collective-permute-start.7) | collective-permute-done | bytes 544 | tf_op jit(solution)/shard_map/ppermute | solution.py:744
  42.9 0.0 copy-start.8
  42.9 0.0 copy-done
  42.9 0.0 copy-done.2
  42.9 0.6 %copy-done.8 = f32[59]{0:T(128)S(1)} copy-done((f32[59]{0:T(128)S(1)}, f32[59]{0:T(128)}, u32[]{:S(2)}) %copy-start.8) | copy-done | bytes 260
  43.5 0.8 %prepare.1 = (f32[59,2,128]{2,1,0:T(2,128)S(1)}, f32[59,2,128]{2,1,0:T(2,128)S(1)}, bf16[1,256,256]{2,1,0:T(8,128)(2,1)S(1)}, f32[1,2,128]{2,1,0:T(2,128)S(1)}) custom-call(s32[1]{0:T(128)} %bitcast.9.group_ref, f32[59,2,128]{2,1,0:T(2,128)S(1)} %get-tuple-element.18.own_ref, f32[59,2,128]{2,1,0:T(2,128)S(1)} %bitcast.37, f32[59,2,128]{2,1,0:T(2,128)S(1)} %bitcast.34, ...), custom_call_target="tpu_custom_call" | custom-call | tf_op jit(solution)/shard_map/prepare/pallas_call | solution.py:746
  44.3 4.5 %all-to-all-done = f32[16,16,128]{2,1,0:T(8,128)S(1)} async-done(((f32[16,16,128]{2,1,0:T(8,128)}), f32[16,16,128]{2,1,0:T(8,128)S(1)}, u32[]{:S(2)}, u32[]{:S(2)}) %all-to-all-start) | async-done | bytes 131104 | tf_op jit(solution)/shard_map/all_to_all | solution.py:804
  48.8 1.2 %owner.1 = (f32[59,2,128]{2,1,0:T(2,128)}, f32[59,2,128]{2,1,0:T(2,128)S(1)}, f32[1,59,2,128]{3,2,1,0:T(2,128)S(1)}) custom-call(f32[256,128]{1,0:T(8,128)S(1)} %bitcast.33, f32[59,2,128]{2,1,0:T(2,128)S(1)} %get-tuple-element.18.own_ref, f32[59,2,128]{2,1,0:T(2,128)S(1)} %get-tuple-element.23.base_ref, f32[59,2,128]{2,1,0:T(2,128)S(1)} %bitcast.35, ...), custom_call_target="tpu_custom_call" | custom-call | tf_op jit(solution)/shard_map/owner/pallas_call | solution.py:805
  50.0 0.0 collective-permute-start.8
  50.0 1.2 %collective-permute-done.8 = f32[59,2,128]{2,1,0:T(2,128)S(1)} collective-permute-done((f32[59,2,128]{2,1,0:T(2,128)S(1)}, f32[59,2,128]{2,1,0:T(2,128)S(1)}, u32[]{:S(2)}, u32[]{:S(2)}) %collective-permute-start.8) | collective-permute-done | bytes 60448 | tf_op jit(solution)/shard_map/ppermute | solution.py:820
  51.2 0.7 %select_bitcast_fusion = f32[1,2,59,128]{3,1,2,0:T(2,128)} fusion(f32[59,2,128]{2,1,0:T(2,128)S(1)} %get-tuple-element.28, f32[59,2,128]{2,1,0:T(2,128)S(1)} %collective-permute-done.8, pred[2,128]{1,0:T(4,128)(4,1)S(1)} %compare_bitcast_fusion), kind=kLoop, calls=%fused_computation.2 | loop fusion | flops 60416 | bytes 181504 | tf_op jit(solution)/shard_map/broadcast_in_dim | solution.py:823
  (4 shorter events, 0.0 us)
Async XLA Ops:
  0.6 5.4 %copy-start.4 = (f32[16,16]{1,0:T(8,128)S(1)}, f32[16,16]{1,0:T(8,128)}, u32[]{:S(2)}) copy-start(f32[16,16]{1,0:T(8,128)} %cameras_ref.1) | copy-start | bytes 3076
  0.6 8.5 %collective-permute-start = (f32[1,59,2,128]{3,2,1,0:T(2,128)}, f32[1,59,2,128]{3,2,1,0:T(2,128)S(1)}, u32[]{:S(2)}, u32[]{:S(2)}) collective-permute-start(f32[1,59,2,128]{3,2,1,0:T(2,128)} %bitcast.38), channel_id=1, source_target_pairs={{0,8},{1,9},{2,10},{3,11},{4,12},{5,13},{6,14},{7,15},{8,0},{9,1},... | collective-permute-start | bytes 181256 | tf_op jit(solution)/shard_map/ppermute | solution.py:704
  6.0 0.7 %copy-start.6 = (s32[1,1,16]{2,1,0:T(1,128)S(1)}, s32[1,1,16]{2,1,0:T(1,128)}, u32[]{:S(2)}) copy-start(s32[1,1,16]{2,1,0:T(1,128)} %param.18) | copy-start | bytes 196
  6.0 0.7 %copy-start.7 = (s32[1,1,16]{2,1,0:T(1,128)S(1)}, s32[1,1,16]{2,1,0:T(1,128)}, u32[]{:S(2)}) copy-start(s32[1,1,16]{2,1,0:T(1,128)} %param.19) | copy-start | bytes 196
  6.7 0.8 %copy-start.3 = (f32[1,2,59,128]{3,1,2,0:T(2,128)S(1)}, f32[1,2,59,128]{3,1,2,0:T(2,128)}, u32[]{:S(2)}) copy-start(f32[1,2,59,128]{3,1,2,0:T(2,128)} %param.12) | copy-start | bytes 181252
  7.6 3.5 %collective-permute-start.2 = (f32[1,32]{1,0:T(1,128)S(1)}, f32[1,32]{1,0:T(1,128)S(1)}, u32[]{:S(2)}, u32[]{:S(2)}) collective-permute-start(f32[1,32]{1,0:T(1,128)S(1)} %get-tuple-element.17.ids_ref), channel_id=1, source_target_pairs={{0,1},{1,0},{2,3},{3,2},{4,5},{5,4},{6,7},{7,6},{8,9},{9,8},{10,11... | collective-permute-start | bytes 392 | tf_op jit(solution)/shard_map/ppermute | solution.py:704
  9.2 5.6 %collective-permute-start.1 = (f32[2,59,2,128]{3,2,1,0:T(2,128)S(1)}, f32[2,59,2,128]{3,2,1,0:T(2,128)S(1)}, u32[]{:S(2)}, u32[]{:S(2)}) collective-permute-start(f32[2,59,2,128]{3,2,1,0:T(2,128)S(1)} %pad_maximum_fusion.1), channel_id=1, source_target_pairs={{0,4},{1,5},{2,6},{3,7},{4,0},{5,1},{6,2},{7,3},{8,12},{9,13},{10,... | collective-permute-start | bytes 362504 | tf_op jit(solution)/shard_map/ppermute | solution.py:704
  11.2 3.6 %collective-permute-start.3 = (f32[2,32]{1,0:T(2,128)S(1)}, f32[2,32]{1,0:T(2,128)S(1)}, u32[]{:S(2)}, u32[]{:S(2)}) collective-permute-start(f32[2,32]{1,0:T(2,128)S(1)} %pad_maximum_fusion.3), channel_id=1, source_target_pairs={{0,2},{1,3},{2,0},{3,1},{4,6},{5,7},{6,4},{7,5},{8,10},{9,11},{10,... | collective-permute-start | bytes 776 | tf_op jit(solution)/shard_map/ppermute | solution.py:704
  14.9 4.0 %copy-start.9 = (f32[1,1,3,1024]{3,1,2,0:T(1,128)S(1)}, f32[1,1,3,1024]{3,1,2,0:T(1,128)}, u32[]{:S(2)}) copy-start(f32[1,1,3,1024]{3,1,2,0:T(1,128)} %param.21) | copy-start | bytes 36868
  14.9 8.2 %copy-start.1 = (bf16[48,1408]{1,0:T(8,128)(2,1)S(1)}, bf16[48,1408]{1,0:T(8,128)(2,1)}, u32[]{:S(2)}) copy-start(bf16[48,1408]{1,0:T(8,128)(2,1)} %constant.16.clone.basis_ref) | copy-start | bytes 405508
  15.4 3.8 %collective-permute-start.4 = (f32[36,128]{1,0:T(8,128)S(1)}, f32[36,128]{1,0:T(8,128)S(1)}, u32[]{:S(2)}, u32[]{:S(2)}) collective-permute-start(f32[36,128]{1,0:T(8,128)S(1)} %get-tuple-element.20), channel_id=1, source_target_pairs={{0,1},{1,0},{2,3},{3,2},{4,5},{5,4},{6,7},{7,6},{8,9},{9,8},{10,11... | collective-permute-start | bytes 55304 | tf_op jit(solution)/shard_map/ppermute | solution.py:704
  17.0 3.8 %collective-permute-start.5 = (f32[36,128]{1,0:T(8,128)S(1)}, f32[36,128]{1,0:T(8,128)S(1)}, u32[]{:S(2)}, u32[]{:S(2)}) collective-permute-start(f32[36,128]{1,0:T(8,128)S(1)} %get-tuple-element.21), channel_id=1, source_target_pairs={{0,2},{1,3},{2,0},{3,1},{4,6},{5,7},{6,4},{7,5},{8,10},{9,11},{10,... | collective-permute-start | bytes 55304 | tf_op jit(solution)/shard_map/ppermute | solution.py:704
  18.5 4.7 %collective-permute-start.6 = (f32[36,128]{1,0:T(8,128)S(1)}, f32[36,128]{1,0:T(8,128)S(1)}, u32[]{:S(2)}, u32[]{:S(2)}) collective-permute-start(f32[36,128]{1,0:T(8,128)S(1)} %get-tuple-element.22), channel_id=1, source_target_pairs={{0,3},{1,2},{2,1},{3,0},{4,7},{5,6},{6,5},{7,4},{8,11},{9,10},{10,... | collective-permute-start | bytes 55304 | tf_op jit(solution)/shard_map/ppermute | solution.py:704
  37.4 5.5 %copy-start = (f32[1,2,59,128]{3,1,2,0:T(2,128)S(1)}, f32[1,2,59,128]{3,1,2,0:T(2,128)}, u32[]{:S(2)}) copy-start(f32[1,2,59,128]{3,1,2,0:T(2,128)} %param.14) | copy-start | bytes 181252
  37.4 5.5 %copy-start.2 = (f32[1,2,59,128]{3,1,2,0:T(2,128)S(1)}, f32[1,2,59,128]{3,1,2,0:T(2,128)}, u32[]{:S(2)}) copy-start(f32[1,2,59,128]{3,1,2,0:T(2,128)} %param.13) | copy-start | bytes 181252
  37.4 11.4 %all-to-all-start = ((f32[16,16,128]{2,1,0:T(8,128)}), f32[16,16,128]{2,1,0:T(8,128)S(1)}, u32[]{:S(2)}, u32[]{:S(2)}) async-start(f32[16,16,128]{2,1,0:T(8,128)} %render.1), calls=%async_computation | async-start | bytes 262144 | tf_op jit(solution)/shard_map/all_to_all | solution.py:804
  41.0 0.7 %copy-start.5 = (s32[1,1,2,64]{3,2,1,0:T(2,128)S(1)}, s32[1,1,2,64]{3,2,1,0:T(2,128)}, u32[]{:S(2)}) copy-start(s32[1,1,2,64]{3,2,1,0:T(2,128)} %param.22) | copy-start | bytes 1540
  41.7 1.1 %collective-permute-start.7 = (s32[2,64]{1,0:T(2,128)S(1)}, s32[2,64]{1,0:T(2,128)S(1)}, u32[]{:S(2)}, u32[]{:S(2)}) collective-permute-start(s32[2,64]{1,0:T(2,128)S(1)} %bitcast.40), channel_id=1, source_target_pairs={{0,16},{16,0},{1,17},{17,1},{2,18},{18,2},{3,19},{19,3},{4,20},{20... | collective-permute-start | bytes 1544 | tf_op jit(solution)/shard_map/ppermute | solution.py:744
  42.9 0.7 %copy-start.8 = (f32[59]{0:T(128)S(1)}, f32[59]{0:T(128)}, u32[]{:S(2)}) copy-start(f32[59]{0:T(128)} %step_ref.1) | copy-start | bytes 712
  50.0 1.2 %collective-permute-start.8 = (f32[59,2,128]{2,1,0:T(2,128)S(1)}, f32[59,2,128]{2,1,0:T(2,128)S(1)}, u32[]{:S(2)}, u32[]{:S(2)}) collective-permute-start(f32[59,2,128]{2,1,0:T(2,128)S(1)} %bitcast.44), channel_id=1, source_target_pairs={{0,16},{16,0},{1,17},{17,1},{2,18},{18,2},{3,19},{19,3},{4,20},{20... | collective-permute-start | bytes 181256 | tf_op jit(solution)/shard_map/ppermute | solution.py:820

commit v7 on v6

--- a/solution.py
+++ b/solution.py
@@ -181,17 +181,20 @@
             mask_ref[n, b : b + 1, :] = mask[0:1, b * LANES : (b + 1) * LANES]
 
 
-def pack_kernel(
-    camera_ref, count_ref, list_ref, depth_ref, cameras_ref, own_ref, mine_ref, pack_ref, held_ref
-):
+def hold_kernel(own_ref, held_ref):
     held_ref[...] = own_ref[...]
+
+
+def pack_kernel(camera_ref, count_ref, list_ref, depth_ref, cameras_ref, mine_ref, pack_ref):
     listed = list_ref.shape[1]
     blocks = list_ref[...]
-    mine_ref[:, :16] = cameras_ref[pl.ds(camera_ref[0, 0], 1), :]
+    shape = cameras_ref.shape
+    chosen = lax.broadcasted_iota(jnp.int32, shape, 0) == jnp.broadcast_to(camera_ref[...], shape)
+    mine_ref[:, :16] = jnp.sum(jnp.where(chosen, cameras_ref[...], 0.0), axis=0, keepdims=True)
     mine_ref[:, 16:] = blocks.astype(jnp.float32)
     pack_ref[:, :listed] = blocks
     pack_ref[:, listed : 2 * listed] = depth_ref[...]
-    pack_ref[:, 2 * listed :] = jnp.full((1, listed), count_ref[0, 0], jnp.int32)
+    pack_ref[:, 2 * listed :] = jnp.broadcast_to(count_ref[...], (1, listed))
 
 
 def project_kernel(masks, yrows, listed, me_ref, raw_ref, ids_ref, *refs):
@@ -455,25 +458,23 @@
 
     rearmost = 2 * pairs - 1
 
-    def retreat(k):
-        follow(k, gaps_a)
-        follow(k - 1, gaps_b)
-
-    def collect(k):
-        moments(k + 2, sums_a)
-        weigh(k, gaps_a, sums_a)
-        moments(k + 1, sums_b)
-        weigh(k - 1, gaps_b, sums_b)
-
     def backward(pair, _):
         k = rearmost - 2 * pair
-        collect(k + 2)
-        retreat(k)
+        moments(k + 4, sums_a)
+        weigh(k + 2, gaps_a, sums_a)
+        follow(k, gaps_a)
+        moments(k + 3, sums_b)
+        weigh(k + 1, gaps_b, sums_b)
+        follow(k - 1, gaps_b)
         return 0
 
-    retreat(rearmost)
+    follow(rearmost, gaps_a)
+    follow(rearmost - 1, gaps_b)
     lax.fori_loop(1, pairs, backward, 0)
-    collect(jnp.int32(1))
+    moments(3, sums_a)
+    weigh(1, gaps_a, sums_a)
+    moments(2, sums_b)
+    weigh(0, gaps_b, sums_b)
     moments(1, sums_a)
     moments(0, sums_b)
 
@@ -704,18 +705,25 @@
         return lax.ppermute(value, "tile", [(i, i ^ mask) for i in range(peers)])
 
     hop_bits = list(reversed(range(2, peers.bit_length() - 1)))
-    mine, pack, held = pl.pallas_call(
+    mine, pack = pl.pallas_call(
         pack_kernel,
         out_shape=(
             shape_of((1, 16 + listed), f32),
             shape_of((1, 3 * listed), jnp.int32),
-            shape_of(own.shape, f32),
         ),
-        in_specs=smem(2) + vmem(4),
-        out_specs=tuple(vmem(3)),
+        in_specs=vmem(5),
+        out_specs=tuple(vmem(2)),
         compiler_params=params_with(8),
         name="pack",
-    )(camera_ids, block_counts, block_lists[0], depth_order[0], cameras, own)
+    )(camera_ids, block_counts, block_lists[0], depth_order[0], cameras)
+    held = pl.pallas_call(
+        hold_kernel,
+        out_shape=shape_of(own.shape, f32),
+        in_specs=vmem(),
+        out_specs=vmem()[0],
+        compiler_params=params_with(8),
+        name="hold",
+    )(own)
     ids = mine
     everything = held[None]
     masks = [0]

time: 52.1 us -> 51.4 us (0.987)
  Pallas kernels: 16.7 us -> 10.5 us
  starting transfers between devices: 16 us -> 22.2 us
  waiting for transfers between devices: 13.4 us -> 12.6 us
    pallas_call x1, Pallas kernels: 14.2 us -> 8.03 us  [on_device(): pl.pallas_call(functools.partial(render_kernel, pixels, blocks, listed, h...]
    all_to_all x1, starting transfers between devices: 3.64 us -> 9.73 us  [on_device(): lax.all_to_all(outbox, 'tile', split_axis=0, concat_axis=0, tiled=True)]
    ppermute x7, waiting for transfers between devices: 6.6 us -> 5.75 us  [swap(): return lax.ppermute(value, 'tile', [(i, i ^ mask) for i in range(peers)])]
  transfers between devices with their start and end apart: 10 -> 10, of which waited for: 8 -> 7; matrix products, arithmetic and copies ran while one was open for 0% -> 0% of each run, Pallas kernels for 2% -> 2%
where the time goes in v7:
time: 51.4 us; the launch traced here: 51.1 us
  starting transfers between devices  22.2 us (43%)
  waiting for transfers between devices  12.6 us (25%)
  Pallas kernels  10.5 us (20%)
  local copies, waits for them, and re-layouts  2.83 us (6%)
  between operations  2.05 us (4%)
  other arithmetic  0.86 us (2%)
    ppermute x7, starting transfers between devices, swap(): return lax.ppermute(value, 'tile', [(i, i ^ mask) for i in range(peers)])  12.4 us
    all_to_all x1, starting transfers between devices, on_device(): lax.all_to_all(outbox, 'tile', split_axis=0, concat_axis=0, tiled=True)  9.73 us
    pallas_call x1, Pallas kernels, on_device(): pl.pallas_call(functools.partial(render_kernel, pixels, blocks, listed, h...  8.03 us
    ppermute x7, waiting for transfers between devices, swap(): return lax.ppermute(value, 'tile', [(i, i ^ mask) for i in range(peers)])  5.75 us
    all_to_all x1, waiting for transfers between devices, on_device(): lax.all_to_all(outbox, 'tile', split_axis=0, concat_axis=0, tiled=True)  4.49 us
    unnamed x21, local copies, waits for them, and re-layouts  2.83 us
    ppermute x1, waiting for transfers between devices, on_device(): theirs = lax.ppermute(sent[n], 'scene', route)  1.24 us
    pallas_call x1, Pallas kernels, on_device(): pl.pallas_call(owner_kernel, out_shape=(shape_of(own.shape, f32), shape_o...  1.16 us
  transfers between devices with their start and end apart: 10, of which 7 were waited for; matrix products, arithmetic and copies ran while one was open for 0% of the time, Pallas kernels for 2%

profile of v7, /device:TPU:0, one launch (start us, length us, event | category | flops | bytes accessed | tf_op | source)
XLA Modules:
  0.0 51.1 jit_solution(18343067266321394750)
XLA Ops:
  0.6 0.0 copy-start.4
  0.6 4.1 %collective-permute-start = (f32[1,59,2,128]{3,2,1,0:T(2,128)}, f32[1,59,2,128]{3,2,1,0:T(2,128)S(1)}, u32[]{:S(2)}, u32[]{:S(2)}) collective-permute-start(f32[1,59,2,128]{3,2,1,0:T(2,128)} %bitcast.38), channel_id=1, source_target_pairs={{0,8},{1,9},{2,10},{3,11},{4,12},{5,13},{6,14},{7,15},{8,0},{9,1},... | collective-permute-start | bytes 181256 | tf_op jit(solution)/shard_map/ppermute | solution.py:705
  6.0 0.0 copy-start.7
  6.0 0.0 copy-start.8
  6.1 0.0 copy-done.4
  6.1 0.6 %copy-done.7 = s32[1,1,16]{2,1,0:T(1,128)S(1)} copy-done((s32[1,1,16]{2,1,0:T(1,128)S(1)}, s32[1,1,16]{2,1,0:T(1,128)}, u32[]{:S(2)}) %copy-start.7) | copy-done | bytes 88
  6.7 0.0 copy-done.8
  6.7 0.1 pack.1
  6.8 1.5 %collective-permute-start.2 = (f32[1,32]{1,0:T(1,128)S(1)}, f32[1,32]{1,0:T(1,128)S(1)}, u32[]{:S(2)}, u32[]{:S(2)}) collective-permute-start(f32[1,32]{1,0:T(1,128)S(1)} %get-tuple-element.16.ids_ref), channel_id=1, source_target_pairs={{0,1},{1,0},{2,3},{3,2},{4,5},{5,4},{6,7},{7,6},{8,9},{9,8},{10,11... | collective-permute-start | bytes 392 | tf_op jit(solution)/shard_map/ppermute | solution.py:705
  8.3 0.0 copy-start.3
  8.3 0.8 %copy-done.3 = f32[1,2,59,128]{3,1,2,0:T(2,128)S(1)} copy-done((f32[1,2,59,128]{3,1,2,0:T(2,128)S(1)}, f32[1,2,59,128]{3,1,2,0:T(2,128)}, u32[]{:S(2)}) %copy-start.3) | copy-done | bytes 60440
  9.2 0.0 collective-permute-done
  9.2 0.1 pad_maximum_fusion.1
  9.2 1.6 %collective-permute-start.1 = (f32[2,59,2,128]{3,2,1,0:T(2,128)S(1)}, f32[2,59,2,128]{3,2,1,0:T(2,128)S(1)}, u32[]{:S(2)}, u32[]{:S(2)}) collective-permute-start(f32[2,59,2,128]{3,2,1,0:T(2,128)S(1)} %pad_maximum_fusion.1), channel_id=1, source_target_pairs={{0,4},{1,5},{2,6},{3,7},{4,0},{5,1},{6,2},{7,3},{8,12},{9,13},{10,... | collective-permute-start | bytes 362504 | tf_op jit(solution)/shard_map/ppermute | solution.py:705
  10.9 0.0 collective-permute-done.2
  10.9 1.6 %collective-permute-start.3 = (f32[2,32]{1,0:T(2,128)S(1)}, f32[2,32]{1,0:T(2,128)S(1)}, u32[]{:S(2)}, u32[]{:S(2)}) collective-permute-start(f32[2,32]{1,0:T(2,128)S(1)} %pad_maximum_fusion.3), channel_id=1, source_target_pairs={{0,2},{1,3},{2,0},{3,1},{4,6},{5,7},{6,4},{7,5},{8,10},{9,11},{10,... | collective-permute-start | bytes 776 | tf_op jit(solution)/shard_map/ppermute | solution.py:705
  12.5 2.0 %collective-permute-done.3 = f32[2,32]{1,0:T(2,128)S(1)} collective-permute-done((f32[2,32]{1,0:T(2,128)S(1)}, f32[2,32]{1,0:T(2,128)S(1)}, u32[]{:S(2)}, u32[]{:S(2)}) %collective-permute-start.3) | collective-permute-done | bytes 288 | tf_op jit(solution)/shard_map/ppermute | solution.py:705
  14.5 0.0 collective-permute-done.1
  14.6 0.1 pad_maximum_fusion.raw_ref
  14.7 0.0 copy-start.9
  14.7 0.0 copy-start.1
  14.7 0.4 project.1
  15.1 1.1 %collective-permute-start.4 = (f32[36,128]{1,0:T(8,128)S(1)}, f32[36,128]{1,0:T(8,128)S(1)}, u32[]{:S(2)}, u32[]{:S(2)}) collective-permute-start(f32[36,128]{1,0:T(8,128)S(1)} %get-tuple-element.18), channel_id=1, source_target_pairs={{0,1},{1,0},{2,3},{3,2},{4,5},{5,4},{6,7},{7,6},{8,9},{9,8},{10,11... | collective-permute-start | bytes 55304 | tf_op jit(solution)/shard_map/ppermute | solution.py:705
  16.2 1.5 %collective-permute-start.5 = (f32[36,128]{1,0:T(8,128)S(1)}, f32[36,128]{1,0:T(8,128)S(1)}, u32[]{:S(2)}, u32[]{:S(2)}) collective-permute-start(f32[36,128]{1,0:T(8,128)S(1)} %get-tuple-element.19), channel_id=1, source_target_pairs={{0,2},{1,3},{2,0},{3,1},{4,6},{5,7},{6,4},{7,5},{8,10},{9,11},{10,... | collective-permute-start | bytes 55304 | tf_op jit(solution)/shard_map/ppermute | solution.py:705
  17.7 1.0 %collective-permute-start.6 = (f32[36,128]{1,0:T(8,128)S(1)}, f32[36,128]{1,0:T(8,128)S(1)}, u32[]{:S(2)}, u32[]{:S(2)}) collective-permute-start(f32[36,128]{1,0:T(8,128)S(1)} %get-tuple-element.20), channel_id=1, source_target_pairs={{0,3},{1,2},{2,1},{3,0},{4,7},{5,6},{6,5},{7,4},{8,11},{9,10},{10,... | collective-permute-start | bytes 55304 | tf_op jit(solution)/shard_map/ppermute | solution.py:705
  18.7 0.0 copy-done.9
  18.7 0.3 collective-permute-done.4.src1
  19.0 1.0 %collective-permute-done.5.src2 = f32[36,128]{1,0:T(8,128)S(1)} collective-permute-done((f32[36,128]{1,0:T(8,128)S(1)}, f32[36,128]{1,0:T(8,128)S(1)}, u32[]{:S(2)}, u32[]{:S(2)}) %collective-permute-start.5) | collective-permute-done | bytes 18464 | tf_op jit(solution)/shard_map/ppermute | solution.py:705
  20.0 2.4 %collective-permute-done.6.src3 = f32[36,128]{1,0:T(8,128)S(1)} collective-permute-done((f32[36,128]{1,0:T(8,128)S(1)}, f32[36,128]{1,0:T(8,128)S(1)}, u32[]{:S(2)}, u32[]{:S(2)}) %collective-permute-start.6) | collective-permute-done | bytes 18464 | tf_op jit(solution)/shard_map/ppermute | solution.py:705
  22.4 0.0 copy-done.1
  22.4 8.0 %render.1 = f32[16,16,128]{2,1,0:T(8,128)} custom-call(s32[1]{0:T(128)} %bitcast.me_ref, s32[1,48]{1,0:T(1,128)S(1)} %get-tuple-element.15.pack_ref, f32[1,32]{1,0:T(1,128)S(1)} %get-tuple-element.16.ids_ref, f32[36,128]{1,0:T(8,128)S(1)} %get-tuple-element.17.src0, f32[36,128]{1,0:T(8,128)S(1)} %collective-permute-done.4.src1, ...), custom_call_target="tpu_custom_call" | custom-call | tf_op jit(solution)/shard_map/render/pallas_call | solution.py:779
  30.4 0.0 copy-start
  30.4 0.0 copy-start.2
  30.4 9.7 %all-to-all-start = ((f32[16,16,128]{2,1,0:T(8,128)}), f32[16,16,128]{2,1,0:T(8,128)S(1)}, u32[]{:S(2)}, u32[]{:S(2)}) async-start(f32[16,16,128]{2,1,0:T(8,128)} %render.1), calls=%async_computation | async-start | bytes 262144 | tf_op jit(solution)/shard_map/all_to_all | solution.py:812
  40.2 0.0 copy-start.5
  40.2 0.7 %copy-done.5 = s32[1,1,2,64]{3,2,1,0:T(2,128)S(1)} copy-done((s32[1,1,2,64]{3,2,1,0:T(2,128)S(1)}, s32[1,1,2,64]{3,2,1,0:T(2,128)}, u32[]{:S(2)}) %copy-start.5) | copy-done | bytes 536
  40.9 0.0 collective-permute-start.7
  40.9 1.1 %collective-permute-done.7.refs_0_ = s32[2,64]{1,0:T(2,128)S(1)} collective-permute-done((s32[2,64]{1,0:T(2,128)S(1)}, s32[2,64]{1,0:T(2,128)S(1)}, u32[]{:S(2)}, u32[]{:S(2)}) %collective-permute-start.7) | collective-permute-done | bytes 544 | tf_op jit(solution)/shard_map/ppermute | solution.py:752
  42.0 0.0 copy-start.6
  42.0 0.0 copy-done
  42.0 0.0 copy-done.2
  42.0 0.6 %copy-done.6 = f32[59]{0:T(128)S(1)} copy-done((f32[59]{0:T(128)S(1)}, f32[59]{0:T(128)}, u32[]{:S(2)}) %copy-start.6) | copy-done | bytes 260
  42.7 0.8 %prepare.1 = (f32[59,2,128]{2,1,0:T(2,128)S(1)}, f32[59,2,128]{2,1,0:T(2,128)S(1)}, bf16[1,256,256]{2,1,0:T(8,128)(2,1)S(1)}, f32[1,2,128]{2,1,0:T(2,128)S(1)}) custom-call(s32[1]{0:T(128)} %bitcast.9.group_ref, f32[59,2,128]{2,1,0:T(2,128)S(1)} %hold.1.own_ref, f32[59,2,128]{2,1,0:T(2,128)S(1)} %bitcast.37, f32[59,2,128]{2,1,0:T(2,128)S(1)} %bitcast.34, ...), custom_call_target="tpu_custom_call" | custom-call | tf_op jit(solution)/shard_map/prepare/pallas_call | solution.py:754
  43.5 4.5 %all-to-all-done = f32[16,16,128]{2,1,0:T(8,128)S(1)} async-done(((f32[16,16,128]{2,1,0:T(8,128)}), f32[16,16,128]{2,1,0:T(8,128)S(1)}, u32[]{:S(2)}, u32[]{:S(2)}) %all-to-all-start) | async-done | bytes 131104 | tf_op jit(solution)/shard_map/all_to_all | solution.py:812
  48.0 1.2 %owner.1 = (f32[59,2,128]{2,1,0:T(2,128)}, f32[59,2,128]{2,1,0:T(2,128)S(1)}, f32[1,59,2,128]{3,2,1,0:T(2,128)S(1)}) custom-call(f32[256,128]{1,0:T(8,128)S(1)} %bitcast.33, f32[59,2,128]{2,1,0:T(2,128)S(1)} %hold.1.own_ref, f32[59,2,128]{2,1,0:T(2,128)S(1)} %get-tuple-element.21.base_ref, f32[59,2,128]{2,1,0:T(2,128)S(1)} %bitcast.35, ...), custom_call_target="tpu_custom_call" | custom-call | tf_op jit(solution)/shard_map/owner/pallas_call | solution.py:813
  49.1 0.0 collective-permute-start.8
  49.1 1.2 %collective-permute-done.8 = f32[59,2,128]{2,1,0:T(2,128)S(1)} collective-permute-done((f32[59,2,128]{2,1,0:T(2,128)S(1)}, f32[59,2,128]{2,1,0:T(2,128)S(1)}, u32[]{:S(2)}, u32[]{:S(2)}) %collective-permute-start.8) | collective-permute-done | bytes 60448 | tf_op jit(solution)/shard_map/ppermute | solution.py:828
  50.4 0.7 %select_bitcast_fusion = f32[1,2,59,128]{3,1,2,0:T(2,128)} fusion(f32[59,2,128]{2,1,0:T(2,128)S(1)} %get-tuple-element.26, f32[59,2,128]{2,1,0:T(2,128)S(1)} %collective-permute-done.8, pred[2,128]{1,0:T(4,128)(4,1)S(1)} %compare_bitcast_fusion), kind=kLoop, calls=%fused_computation.2 | loop fusion | flops 60416 | bytes 181504 | tf_op jit(solution)/shard_map/broadcast_in_dim | solution.py:831
  (5 shorter events, 0.0 us)
Async XLA Ops:
  0.6 5.4 %copy-start.4 = (f32[16,16]{1,0:T(8,128)S(1)}, f32[16,16]{1,0:T(8,128)}, u32[]{:S(2)}) copy-start(f32[16,16]{1,0:T(8,128)} %cameras_ref.1) | copy-start | bytes 3076
  0.6 8.5 %collective-permute-start = (f32[1,59,2,128]{3,2,1,0:T(2,128)}, f32[1,59,2,128]{3,2,1,0:T(2,128)S(1)}, u32[]{:S(2)}, u32[]{:S(2)}) collective-permute-start(f32[1,59,2,128]{3,2,1,0:T(2,128)} %bitcast.38), channel_id=1, source_target_pairs={{0,8},{1,9},{2,10},{3,11},{4,12},{5,13},{6,14},{7,15},{8,0},{9,1},... | collective-permute-start | bytes 181256 | tf_op jit(solution)/shard_map/ppermute | solution.py:705
  6.0 0.7 %copy-start.7 = (s32[1,1,16]{2,1,0:T(1,128)S(1)}, s32[1,1,16]{2,1,0:T(1,128)}, u32[]{:S(2)}) copy-start(s32[1,1,16]{2,1,0:T(1,128)} %param.18) | copy-start | bytes 196
  6.0 0.7 %copy-start.8 = (s32[1,1,16]{2,1,0:T(1,128)S(1)}, s32[1,1,16]{2,1,0:T(1,128)}, u32[]{:S(2)}) copy-start(s32[1,1,16]{2,1,0:T(1,128)} %param.19) | copy-start | bytes 196
  6.8 4.1 %collective-permute-start.2 = (f32[1,32]{1,0:T(1,128)S(1)}, f32[1,32]{1,0:T(1,128)S(1)}, u32[]{:S(2)}, u32[]{:S(2)}) collective-permute-start(f32[1,32]{1,0:T(1,128)S(1)} %get-tuple-element.16.ids_ref), channel_id=1, source_target_pairs={{0,1},{1,0},{2,3},{3,2},{4,5},{5,4},{6,7},{7,6},{8,9},{9,8},{10,11... | collective-permute-start | bytes 392 | tf_op jit(solution)/shard_map/ppermute | solution.py:705
  8.3 0.8 %copy-start.3 = (f32[1,2,59,128]{3,1,2,0:T(2,128)S(1)}, f32[1,2,59,128]{3,1,2,0:T(2,128)}, u32[]{:S(2)}) copy-start(f32[1,2,59,128]{3,1,2,0:T(2,128)} %param.12) | copy-start | bytes 181252
  9.2 5.3 %collective-permute-start.1 = (f32[2,59,2,128]{3,2,1,0:T(2,128)S(1)}, f32[2,59,2,128]{3,2,1,0:T(2,128)S(1)}, u32[]{:S(2)}, u32[]{:S(2)}) collective-permute-start(f32[2,59,2,128]{3,2,1,0:T(2,128)S(1)} %pad_maximum_fusion.1), channel_id=1, source_target_pairs={{0,4},{1,5},{2,6},{3,7},{4,0},{5,1},{6,2},{7,3},{8,12},{9,13},{10,... | collective-permute-start | bytes 362504 | tf_op jit(solution)/shard_map/ppermute | solution.py:705
  10.9 3.6 %collective-permute-start.3 = (f32[2,32]{1,0:T(2,128)S(1)}, f32[2,32]{1,0:T(2,128)S(1)}, u32[]{:S(2)}, u32[]{:S(2)}) collective-permute-start(f32[2,32]{1,0:T(2,128)S(1)} %pad_maximum_fusion.3), channel_id=1, source_target_pairs={{0,2},{1,3},{2,0},{3,1},{4,6},{5,7},{6,4},{7,5},{8,10},{9,11},{10,... | collective-permute-start | bytes 776 | tf_op jit(solution)/shard_map/ppermute | solution.py:705
  14.7 4.0 %copy-start.9 = (f32[1,1,3,1024]{3,1,2,0:T(1,128)S(1)}, f32[1,1,3,1024]{3,1,2,0:T(1,128)}, u32[]{:S(2)}) copy-start(f32[1,1,3,1024]{3,1,2,0:T(1,128)} %param.21) | copy-start | bytes 36868
  14.7 7.7 %copy-start.1 = (bf16[48,1408]{1,0:T(8,128)(2,1)S(1)}, bf16[48,1408]{1,0:T(8,128)(2,1)}, u32[]{:S(2)}) copy-start(bf16[48,1408]{1,0:T(8,128)(2,1)} %constant.16.clone.basis_ref) | copy-start | bytes 405508
  15.1 3.8 %collective-permute-start.4 = (f32[36,128]{1,0:T(8,128)S(1)}, f32[36,128]{1,0:T(8,128)S(1)}, u32[]{:S(2)}, u32[]{:S(2)}) collective-permute-start(f32[36,128]{1,0:T(8,128)S(1)} %get-tuple-element.18), channel_id=1, source_target_pairs={{0,1},{1,0},{2,3},{3,2},{4,5},{5,4},{6,7},{7,6},{8,9},{9,8},{10,11... | collective-permute-start | bytes 55304 | tf_op jit(solution)/shard_map/ppermute | solution.py:705
  16.2 3.8 %collective-permute-start.5 = (f32[36,128]{1,0:T(8,128)S(1)}, f32[36,128]{1,0:T(8,128)S(1)}, u32[]{:S(2)}, u32[]{:S(2)}) collective-permute-start(f32[36,128]{1,0:T(8,128)S(1)} %get-tuple-element.19), channel_id=1, source_target_pairs={{0,2},{1,3},{2,0},{3,1},{4,6},{5,7},{6,4},{7,5},{8,10},{9,11},{10,... | collective-permute-start | bytes 55304 | tf_op jit(solution)/shard_map/ppermute | solution.py:705
  17.7 4.7 %collective-permute-start.6 = (f32[36,128]{1,0:T(8,128)S(1)}, f32[36,128]{1,0:T(8,128)S(1)}, u32[]{:S(2)}, u32[]{:S(2)}) collective-permute-start(f32[36,128]{1,0:T(8,128)S(1)} %get-tuple-element.20), channel_id=1, source_target_pairs={{0,3},{1,2},{2,1},{3,0},{4,7},{5,6},{6,5},{7,4},{8,11},{9,10},{10,... | collective-permute-start | bytes 55304 | tf_op jit(solution)/shard_map/ppermute | solution.py:705
  30.4 11.6 %copy-start = (f32[1,2,59,128]{3,1,2,0:T(2,128)S(1)}, f32[1,2,59,128]{3,1,2,0:T(2,128)}, u32[]{:S(2)}) copy-start(f32[1,2,59,128]{3,1,2,0:T(2,128)} %param.14) | copy-start | bytes 181252
  30.4 11.6 %copy-start.2 = (f32[1,2,59,128]{3,1,2,0:T(2,128)S(1)}, f32[1,2,59,128]{3,1,2,0:T(2,128)}, u32[]{:S(2)}) copy-start(f32[1,2,59,128]{3,1,2,0:T(2,128)} %param.13) | copy-start | bytes 181252
  30.4 17.5 %all-to-all-start = ((f32[16,16,128]{2,1,0:T(8,128)}), f32[16,16,128]{2,1,0:T(8,128)S(1)}, u32[]{:S(2)}, u32[]{:S(2)}) async-start(f32[16,16,128]{2,1,0:T(8,128)} %render.1), calls=%async_computation | async-start | bytes 262144 | tf_op jit(solution)/shard_map/all_to_all | solution.py:812
  40.2 0.7 %copy-start.5 = (s32[1,1,2,64]{3,2,1,0:T(2,128)S(1)}, s32[1,1,2,64]{3,2,1,0:T(2,128)}, u32[]{:S(2)}) copy-start(s32[1,1,2,64]{3,2,1,0:T(2,128)} %param.22) | copy-start | bytes 1540
  40.9 1.1 %collective-permute-start.7 = (s32[2,64]{1,0:T(2,128)S(1)}, s32[2,64]{1,0:T(2,128)S(1)}, u32[]{:S(2)}, u32[]{:S(2)}) collective-permute-start(s32[2,64]{1,0:T(2,128)S(1)} %bitcast.40), channel_id=1, source_target_pairs={{0,16},{16,0},{1,17},{17,1},{2,18},{18,2},{3,19},{19,3},{4,20},{20... | collective-permute-start | bytes 1544 | tf_op jit(solution)/shard_map/ppermute | solution.py:752
  42.0 0.7 %copy-start.6 = (f32[59]{0:T(128)S(1)}, f32[59]{0:T(128)}, u32[]{:S(2)}) copy-start(f32[59]{0:T(128)} %step_ref.1) | copy-start | bytes 712
  49.1 1.2 %collective-permute-start.8 = (f32[59,2,128]{2,1,0:T(2,128)S(1)}, f32[59,2,128]{2,1,0:T(2,128)S(1)}, u32[]{:S(2)}, u32[]{:S(2)}) collective-permute-start(f32[59,2,128]{2,1,0:T(2,128)S(1)} %bitcast.44), channel_id=1, source_target_pairs={{0,16},{16,0},{1,17},{17,1},{2,18},{18,2},{3,19},{19,3},{4,20},{20... | collective-permute-start | bytes 181256 | tf_op jit(solution)/shard_map/ppermute | solution.py:828

commit v8 on v7

--- a/solution.py
+++ b/solution.py
@@ -776,6 +776,7 @@
     )(me, everything, ids)
     sources = [messages[0]] + [swap(messages[j], j) for j in range(1, INNER)]
 
+    pack, base, steps, pick, mask = lax.optimization_barrier((pack, base, steps, pick, mask))
     outbox = pl.pallas_call(
         functools.partial(render_kernel, pixels, blocks, listed, hop_bits),
         out_shape=shape_of((peers, MSG, LANES), f32),

time: 51.4 us -> 50.3 us (0.979)
  blocking collectives: 0 us -> 21.2 us
  starting transfers between devices: 22.2 us -> 12.4 us
  waiting for transfers between devices: 12.6 us -> 6.12 us
  Pallas kernels: 10.5 us -> 5.77 us
  local copies, waits for them, and re-layouts: 2.83 us -> 1.52 us
    all_to_all x0 -> x1, blocking collectives: none -> 21.2 us  [on_device(): lax.all_to_all(outbox, 'tile', split_axis=0, concat_axis=0, tiled=True)]
    all_to_all x1 -> x0, starting transfers between devices: 9.73 us -> none  [on_device(): lax.all_to_all(outbox, 'tile', split_axis=0, concat_axis=0, tiled=True)]
    pallas_call x1, Pallas kernels: 8.03 us -> 3.27 us  [on_device(): pl.pallas_call(functools.partial(render_kernel, pixels, blocks, listed, h...]
    all_to_all x1 -> x0, waiting for transfers between devices: 4.49 us -> none  [on_device(): lax.all_to_all(outbox, 'tile', split_axis=0, concat_axis=0, tiled=True)]
    ppermute x7, waiting for transfers between devices: 5.75 us -> 3.76 us  [swap(): return lax.ppermute(value, 'tile', [(i, i ^ mask) for i in range(peers)])]
    unnamed x21, local copies, waits for them, and re-layouts: 2.83 us -> 1.52 us
  transfers between devices with their start and end apart: 10 -> 9, of which waited for: 7 -> 4; matrix products, arithmetic and copies ran while one was open for 0% -> 0% of each run, Pallas kernels for 2% -> 2%
where the time goes in v8:
time: 50.3 us; the launch traced here: 50 us
  blocking collectives  21.2 us (42%)
  starting transfers between devices  12.4 us (25%)
  waiting for transfers between devices  6.12 us (12%)
  Pallas kernels  5.77 us (11%)
  between operations  2.1 us (4%)
  local copies, waits for them, and re-layouts  1.52 us (3%)
  other arithmetic  0.86 us (2%)
    all_to_all x1, blocking collectives, on_device(): lax.all_to_all(outbox, 'tile', split_axis=0, concat_axis=0, tiled=True)  21.2 us
    ppermute x7, starting transfers between devices, swap(): return lax.ppermute(value, 'tile', [(i, i ^ mask) for i in range(peers)])  12.4 us
    ppermute x7, waiting for transfers between devices, swap(): return lax.ppermute(value, 'tile', [(i, i ^ mask) for i in range(peers)])  3.76 us
    pallas_call x1, Pallas kernels, on_device(): pl.pallas_call(functools.partial(render_kernel, pixels, blocks, listed, h...  3.27 us
    unnamed x21, local copies, waits for them, and re-layouts  1.52 us
    ppermute x1, waiting for transfers between devices, on_device(): theirs = lax.ppermute(sent[n], 'scene', route)  1.24 us
    pallas_call x1, Pallas kernels, on_device(): pl.pallas_call(owner_kernel, out_shape=(shape_of(own.shape, f32), shape_o...  1.15 us
    ppermute x1, waiting for transfers between devices, on_device(): lists = [lax.ppermute(share, 'scene', route) for route in routes]  1.12 us
  transfers between devices with their start and end apart: 9, of which 4 were waited for; matrix products, arithmetic and copies ran while one was open for 0% of the time, Pallas kernels for 2%

profile of v8, /device:TPU:0, one launch (start us, length us, event | category | flops | bytes accessed | tf_op | source)
XLA Modules:
  0.0 50.0 jit_solution(10366211928834596090)
XLA Ops:
  0.6 0.0 copy-start.4
  0.6 4.1 %collective-permute-start.1 = (f32[1,59,2,128]{3,2,1,0:T(2,128)}, f32[1,59,2,128]{3,2,1,0:T(2,128)S(1)}, u32[]{:S(2)}, u32[]{:S(2)}) collective-permute-start(f32[1,59,2,128]{3,2,1,0:T(2,128)} %bitcast.38), channel_id=1, source_target_pairs={{0,8},{1,9},{2,10},{3,11},{4,12},{5,13},{6,14},{7,15},{8,0},{9,1},... | collective-permute-start | bytes 181256 | tf_op jit(solution)/shard_map/ppermute | solution.py:705
  6.0 0.0 copy-start.7
  6.0 0.0 copy-start.8
  6.1 0.0 copy-done.4
  6.1 0.6 %copy-done.7 = s32[1,1,16]{2,1,0:T(1,128)S(1)} copy-done((s32[1,1,16]{2,1,0:T(1,128)S(1)}, s32[1,1,16]{2,1,0:T(1,128)}, u32[]{:S(2)}) %copy-start.7) | copy-done | bytes 88
  6.7 0.0 copy-done.8
  6.7 0.1 pack.1
  6.8 1.5 %collective-permute-start.3 = (f32[1,32]{1,0:T(1,128)S(1)}, f32[1,32]{1,0:T(1,128)S(1)}, u32[]{:S(2)}, u32[]{:S(2)}) collective-permute-start(f32[1,32]{1,0:T(1,128)S(1)} %get-tuple-element.26.ids_ref), channel_id=1, source_target_pairs={{0,1},{1,0},{2,3},{3,2},{4,5},{5,4},{6,7},{7,6},{8,9},{9,8},{10,11... | collective-permute-start | bytes 392 | tf_op jit(solution)/shard_map/ppermute | solution.py:705
  8.3 0.0 copy-start.3
  8.3 0.8 %copy-done.3 = f32[1,2,59,128]{3,1,2,0:T(2,128)S(1)} copy-done((f32[1,2,59,128]{3,1,2,0:T(2,128)S(1)}, f32[1,2,59,128]{3,1,2,0:T(2,128)}, u32[]{:S(2)}) %copy-start.3) | copy-done | bytes 60440
  9.2 0.0 collective-permute-done.1
  9.2 0.1 pad_maximum_fusion.1
  9.2 1.6 %collective-permute-start.2 = (f32[2,59,2,128]{3,2,1,0:T(2,128)S(1)}, f32[2,59,2,128]{3,2,1,0:T(2,128)S(1)}, u32[]{:S(2)}, u32[]{:S(2)}) collective-permute-start(f32[2,59,2,128]{3,2,1,0:T(2,128)S(1)} %pad_maximum_fusion.1), channel_id=1, source_target_pairs={{0,4},{1,5},{2,6},{3,7},{4,0},{5,1},{6,2},{7,3},{8,12},{9,13},{10,... | collective-permute-start | bytes 362504 | tf_op jit(solution)/shard_map/ppermute | solution.py:705
  10.9 0.0 collective-permute-done.3
  10.9 1.6 %collective-permute-start.4 = (f32[2,32]{1,0:T(2,128)S(1)}, f32[2,32]{1,0:T(2,128)S(1)}, u32[]{:S(2)}, u32[]{:S(2)}) collective-permute-start(f32[2,32]{1,0:T(2,128)S(1)} %pad_maximum_fusion.3), channel_id=1, source_target_pairs={{0,2},{1,3},{2,0},{3,1},{4,6},{5,7},{6,4},{7,5},{8,10},{9,11},{10,... | collective-permute-start | bytes 776 | tf_op jit(solution)/shard_map/ppermute | solution.py:705
  12.5 2.0 %collective-permute-done.4 = f32[2,32]{1,0:T(2,128)S(1)} collective-permute-done((f32[2,32]{1,0:T(2,128)S(1)}, f32[2,32]{1,0:T(2,128)S(1)}, u32[]{:S(2)}, u32[]{:S(2)}) %collective-permute-start.4) | collective-permute-done | bytes 288 | tf_op jit(solution)/shard_map/ppermute | solution.py:705
  14.5 0.0 collective-permute-done.2
  14.6 0.1 pad_maximum_fusion.raw_ref
  14.7 0.0 copy-start.5
  14.7 0.0 copy-start.9
  14.7 0.0 copy-start
  14.7 0.0 copy-start.2
  14.7 0.0 copy-start.6
  14.7 0.4 project.1
  15.2 0.0 copy-start.1
  15.2 1.1 %collective-permute-start.5 = (f32[36,128]{1,0:T(8,128)S(1)}, f32[36,128]{1,0:T(8,128)S(1)}, u32[]{:S(2)}, u32[]{:S(2)}) collective-permute-start(f32[36,128]{1,0:T(8,128)S(1)} %get-tuple-element.28), channel_id=1, source_target_pairs={{0,1},{1,0},{2,3},{3,2},{4,5},{5,4},{6,7},{7,6},{8,9},{9,8},{10,11... | collective-permute-start | bytes 55304 | tf_op jit(solution)/shard_map/ppermute | solution.py:705
  16.2 1.5 %collective-permute-start.6 = (f32[36,128]{1,0:T(8,128)S(1)}, f32[36,128]{1,0:T(8,128)S(1)}, u32[]{:S(2)}, u32[]{:S(2)}) collective-permute-start(f32[36,128]{1,0:T(8,128)S(1)} %get-tuple-element.29), channel_id=1, source_target_pairs={{0,2},{1,3},{2,0},{3,1},{4,6},{5,7},{6,4},{7,5},{8,10},{9,11},{10,... | collective-permute-start | bytes 55304 | tf_op jit(solution)/shard_map/ppermute | solution.py:705
  17.8 1.0 %collective-permute-start.7 = (f32[36,128]{1,0:T(8,128)S(1)}, f32[36,128]{1,0:T(8,128)S(1)}, u32[]{:S(2)}, u32[]{:S(2)}) collective-permute-start(f32[36,128]{1,0:T(8,128)S(1)} %get-tuple-element.30), channel_id=1, source_target_pairs={{0,3},{1,2},{2,1},{3,0},{4,7},{5,6},{6,5},{7,4},{8,11},{9,10},{10,... | collective-permute-start | bytes 55304 | tf_op jit(solution)/shard_map/ppermute | solution.py:705
  18.7 0.0 copy-done.5
  18.8 0.0 collective-permute-start
  18.8 0.0 copy-done.9
  18.8 1.1 %collective-permute-done.refs_0_ = s32[2,64]{1,0:T(2,128)S(1)} collective-permute-done((s32[2,64]{1,0:T(2,128)S(1)}, s32[2,64]{1,0:T(2,128)S(1)}, u32[]{:S(2)}, u32[]{:S(2)}) %collective-permute-start) | collective-permute-done | bytes 544 | tf_op jit(solution)/shard_map/ppermute | solution.py:752
  19.9 0.0 copy-done
  19.9 0.0 copy-done.2
  19.9 0.0 copy-done.6
  19.9 0.8 %prepare.1 = (f32[59,2,128]{2,1,0:T(2,128)S(1)}, f32[59,2,128]{2,1,0:T(2,128)S(1)}, bf16[1,256,256]{2,1,0:T(8,128)(2,1)S(1)}, f32[1,2,128]{2,1,0:T(2,128)S(1)}) custom-call(s32[1]{0:T(128)} %bitcast.3.group_ref, f32[59,2,128]{2,1,0:T(2,128)S(1)} %hold.1.own_ref, f32[59,2,128]{2,1,0:T(2,128)S(1)} %bitcast.37, f32[59,2,128]{2,1,0:T(2,128)S(1)} %bitcast.34, ...), custom_call_target="tpu_custom_call" | custom-call | tf_op jit(solution)/shard_map/prepare/pallas_call | solution.py:754
  20.7 0.0 collective-permute-done.5.src1
  20.7 0.0 collective-permute-done.6.src2
  20.7 1.7 %collective-permute-done.7.src3 = f32[36,128]{1,0:T(8,128)S(1)} collective-permute-done((f32[36,128]{1,0:T(8,128)S(1)}, f32[36,128]{1,0:T(8,128)S(1)}, u32[]{:S(2)}, u32[]{:S(2)}) %collective-permute-start.7) | collective-permute-done | bytes 18464 | tf_op jit(solution)/shard_map/ppermute | solution.py:705
  22.4 0.0 copy-done.1
  22.5 3.3 %render.1 = f32[16,16,128]{2,1,0:T(8,128)S(1)} custom-call(s32[1]{0:T(128)} %bitcast.me_ref, s32[1,48]{1,0:T(1,128)S(1)} %get-tuple-element.25.pack_ref, f32[1,32]{1,0:T(1,128)S(1)} %get-tuple-element.26.ids_ref, f32[36,128]{1,0:T(8,128)S(1)} %get-tuple-element.27.src0, f32[36,128]{1,0:T(8,128)S(1)} %collective-permute-done.5.src1, ...), custom_call_target="tpu_custom_call" | custom-call | tf_op jit(solution)/shard_map/render/pallas_call | solution.py:780
  25.7 21.2 %all_to_all.5 = f32[16,16,128]{2,1,0:T(8,128)S(1)} all-to-all(f32[16,16,128]{2,1,0:T(8,128)S(1)} %render.1), channel_id=1, replica_groups=mesh['scene'=2,'tile'=16] {'tile'}, dimensions={0} | all-to-all | bytes 262144 | tf_op jit(solution)/shard_map/all_to_all | solution.py:813
  47.0 1.2 %owner.1 = (f32[59,2,128]{2,1,0:T(2,128)}, f32[59,2,128]{2,1,0:T(2,128)S(1)}, f32[1,59,2,128]{3,2,1,0:T(2,128)S(1)}) custom-call(f32[256,128]{1,0:T(8,128)S(1)} %bitcast.33, f32[59,2,128]{2,1,0:T(2,128)S(1)} %hold.1.own_ref, f32[59,2,128]{2,1,0:T(2,128)S(1)} %get-tuple-element.31.base_ref, f32[59,2,128]{2,1,0:T(2,128)S(1)} %bitcast.35, ...), custom_call_target="tpu_custom_call" | custom-call | tf_op jit(solution)/shard_map/owner/pallas_call | solution.py:814
  48.1 0.0 collective-permute-start.8
  48.1 1.2 %collective-permute-done.8 = f32[59,2,128]{2,1,0:T(2,128)S(1)} collective-permute-done((f32[59,2,128]{2,1,0:T(2,128)S(1)}, f32[59,2,128]{2,1,0:T(2,128)S(1)}, u32[]{:S(2)}, u32[]{:S(2)}) %collective-permute-start.8) | collective-permute-done | bytes 60448 | tf_op jit(solution)/shard_map/ppermute | solution.py:829
  49.4 0.7 %select_bitcast_fusion = f32[1,2,59,128]{3,1,2,0:T(2,128)} fusion(f32[59,2,128]{2,1,0:T(2,128)S(1)} %get-tuple-element.36, f32[59,2,128]{2,1,0:T(2,128)S(1)} %collective-permute-done.8, pred[2,128]{1,0:T(4,128)(4,1)S(1)} %compare_bitcast_fusion), kind=kLoop, calls=%fused_computation.2 | loop fusion | flops 60416 | bytes 181504 | tf_op jit(solution)/shard_map/broadcast_in_dim | solution.py:832
  (5 shorter events, 0.0 us)
Async XLA Ops:
  0.6 5.4 %copy-start.4 = (f32[16,16]{1,0:T(8,128)S(1)}, f32[16,16]{1,0:T(8,128)}, u32[]{:S(2)}) copy-start(f32[16,16]{1,0:T(8,128)} %cameras_ref.1) | copy-start | bytes 3076
  0.6 8.5 %collective-permute-start.1 = (f32[1,59,2,128]{3,2,1,0:T(2,128)}, f32[1,59,2,128]{3,2,1,0:T(2,128)S(1)}, u32[]{:S(2)}, u32[]{:S(2)}) collective-permute-start(f32[1,59,2,128]{3,2,1,0:T(2,128)} %bitcast.38), channel_id=1, source_target_pairs={{0,8},{1,9},{2,10},{3,11},{4,12},{5,13},{6,14},{7,15},{8,0},{9,1},... | collective-permute-start | bytes 181256 | tf_op jit(solution)/shard_map/ppermute | solution.py:705
  6.0 0.7 %copy-start.7 = (s32[1,1,16]{2,1,0:T(1,128)S(1)}, s32[1,1,16]{2,1,0:T(1,128)}, u32[]{:S(2)}) copy-start(s32[1,1,16]{2,1,0:T(1,128)} %param.18) | copy-start | bytes 196
  6.0 0.7 %copy-start.8 = (s32[1,1,16]{2,1,0:T(1,128)S(1)}, s32[1,1,16]{2,1,0:T(1,128)}, u32[]{:S(2)}) copy-start(s32[1,1,16]{2,1,0:T(1,128)} %param.19) | copy-start | bytes 196
  6.8 4.1 %collective-permute-start.3 = (f32[1,32]{1,0:T(1,128)S(1)}, f32[1,32]{1,0:T(1,128)S(1)}, u32[]{:S(2)}, u32[]{:S(2)}) collective-permute-start(f32[1,32]{1,0:T(1,128)S(1)} %get-tuple-element.26.ids_ref), channel_id=1, source_target_pairs={{0,1},{1,0},{2,3},{3,2},{4,5},{5,4},{6,7},{7,6},{8,9},{9,8},{10,11... | collective-permute-start | bytes 392 | tf_op jit(solution)/shard_map/ppermute | solution.py:705
  8.3 0.8 %copy-start.3 = (f32[1,2,59,128]{3,1,2,0:T(2,128)S(1)}, f32[1,2,59,128]{3,1,2,0:T(2,128)}, u32[]{:S(2)}) copy-start(f32[1,2,59,128]{3,1,2,0:T(2,128)} %param.12) | copy-start | bytes 181252
  9.2 5.3 %collective-permute-start.2 = (f32[2,59,2,128]{3,2,1,0:T(2,128)S(1)}, f32[2,59,2,128]{3,2,1,0:T(2,128)S(1)}, u32[]{:S(2)}, u32[]{:S(2)}) collective-permute-start(f32[2,59,2,128]{3,2,1,0:T(2,128)S(1)} %pad_maximum_fusion.1), channel_id=1, source_target_pairs={{0,4},{1,5},{2,6},{3,7},{4,0},{5,1},{6,2},{7,3},{8,12},{9,13},{10,... | collective-permute-start | bytes 362504 | tf_op jit(solution)/shard_map/ppermute | solution.py:705
  10.9 3.6 %collective-permute-start.4 = (f32[2,32]{1,0:T(2,128)S(1)}, f32[2,32]{1,0:T(2,128)S(1)}, u32[]{:S(2)}, u32[]{:S(2)}) collective-permute-start(f32[2,32]{1,0:T(2,128)S(1)} %pad_maximum_fusion.3), channel_id=1, source_target_pairs={{0,2},{1,3},{2,0},{3,1},{4,6},{5,7},{6,4},{7,5},{8,10},{9,11},{10,... | collective-permute-start | bytes 776 | tf_op jit(solution)/shard_map/ppermute | solution.py:705
  14.7 4.1 %copy-start.5 = (s32[1,1,2,64]{3,2,1,0:T(2,128)S(1)}, s32[1,1,2,64]{3,2,1,0:T(2,128)}, u32[]{:S(2)}) copy-start(s32[1,1,2,64]{3,2,1,0:T(2,128)} %param.22) | copy-start | bytes 1540
  14.7 4.1 %copy-start.9 = (f32[1,1,3,1024]{3,1,2,0:T(1,128)S(1)}, f32[1,1,3,1024]{3,1,2,0:T(1,128)}, u32[]{:S(2)}) copy-start(f32[1,1,3,1024]{3,1,2,0:T(1,128)} %param.21) | copy-start | bytes 36868
  14.7 5.2 %copy-start = (f32[1,2,59,128]{3,1,2,0:T(2,128)S(1)}, f32[1,2,59,128]{3,1,2,0:T(2,128)}, u32[]{:S(2)}) copy-start(f32[1,2,59,128]{3,1,2,0:T(2,128)} %param.14) | copy-start | bytes 181252
  14.7 5.2 %copy-start.2 = (f32[1,2,59,128]{3,1,2,0:T(2,128)S(1)}, f32[1,2,59,128]{3,1,2,0:T(2,128)}, u32[]{:S(2)}) copy-start(f32[1,2,59,128]{3,1,2,0:T(2,128)} %param.13) | copy-start | bytes 181252
  14.7 5.2 %copy-start.6 = (f32[59]{0:T(128)S(1)}, f32[59]{0:T(128)}, u32[]{:S(2)}) copy-start(f32[59]{0:T(128)} %step_ref.1) | copy-start | bytes 712
  15.2 7.3 %copy-start.1 = (bf16[48,1408]{1,0:T(8,128)(2,1)S(1)}, bf16[48,1408]{1,0:T(8,128)(2,1)}, u32[]{:S(2)}) copy-start(bf16[48,1408]{1,0:T(8,128)(2,1)} %constant.16.clone.basis_ref) | copy-start | bytes 405508
  15.2 5.5 %collective-permute-start.5 = (f32[36,128]{1,0:T(8,128)S(1)}, f32[36,128]{1,0:T(8,128)S(1)}, u32[]{:S(2)}, u32[]{:S(2)}) collective-permute-start(f32[36,128]{1,0:T(8,128)S(1)} %get-tuple-element.28), channel_id=1, source_target_pairs={{0,1},{1,0},{2,3},{3,2},{4,5},{5,4},{6,7},{7,6},{8,9},{9,8},{10,11... | collective-permute-start | bytes 55304 | tf_op jit(solution)/shard_map/ppermute | solution.py:705
  16.2 4.5 %collective-permute-start.6 = (f32[36,128]{1,0:T(8,128)S(1)}, f32[36,128]{1,0:T(8,128)S(1)}, u32[]{:S(2)}, u32[]{:S(2)}) collective-permute-start(f32[36,128]{1,0:T(8,128)S(1)} %get-tuple-element.29), channel_id=1, source_target_pairs={{0,2},{1,3},{2,0},{3,1},{4,6},{5,7},{6,4},{7,5},{8,10},{9,11},{10,... | collective-permute-start | bytes 55304 | tf_op jit(solution)/shard_map/ppermute | solution.py:705
  17.8 4.7 %collective-permute-start.7 = (f32[36,128]{1,0:T(8,128)S(1)}, f32[36,128]{1,0:T(8,128)S(1)}, u32[]{:S(2)}, u32[]{:S(2)}) collective-permute-start(f32[36,128]{1,0:T(8,128)S(1)} %get-tuple-element.30), channel_id=1, source_target_pairs={{0,3},{1,2},{2,1},{3,0},{4,7},{5,6},{6,5},{7,4},{8,11},{9,10},{10,... | collective-permute-start | bytes 55304 | tf_op jit(solution)/shard_map/ppermute | solution.py:705
  18.8 1.1 %collective-permute-start = (s32[2,64]{1,0:T(2,128)S(1)}, s32[2,64]{1,0:T(2,128)S(1)}, u32[]{:S(2)}, u32[]{:S(2)}) collective-permute-start(s32[2,64]{1,0:T(2,128)S(1)} %bitcast.40), channel_id=1, source_target_pairs={{0,16},{16,0},{1,17},{17,1},{2,18},{18,2},{3,19},{19,3},{4,20},{20... | collective-permute-start | bytes 1544 | tf_op jit(solution)/shard_map/ppermute | solution.py:752
  48.1 1.2 %collective-permute-start.8 = (f32[59,2,128]{2,1,0:T(2,128)S(1)}, f32[59,2,128]{2,1,0:T(2,128)S(1)}, u32[]{:S(2)}, u32[]{:S(2)}) collective-permute-start(f32[59,2,128]{2,1,0:T(2,128)S(1)} %bitcast.44), channel_id=1, source_target_pairs={{0,16},{16,0},{1,17},{17,1},{2,18},{18,2},{3,19},{19,3},{4,20},{20... | collective-permute-start | bytes 181256 | tf_op jit(solution)/shard_map/ppermute | solution.py:829

commit v9 on v8

--- a/solution.py
+++ b/solution.py
@@ -272,27 +272,30 @@
         slots[jnp.where(live, live_end, dead_end)] = slot
         return jnp.where(live, live_end + 1, live_end), jnp.where(live, dead_end, dead_end + 1)
 
-    lax.fori_loop(0, listed, place_slot, (jnp.int32(0), count))
+    ends = (jnp.int32(0), count)
+    for j in range(listed):
+        ends = place_slot(j, ends)
 
     for j, src in enumerate((src0, src1, src2, src3)):
         raw[j * COEFS * outer : (j + 1) * COEFS * outer, :] = src[...]
-    coef[...] = jnp.zeros(coef.shape, jnp.float32)
+    place = lax.broadcasted_iota(jnp.int32, (PART, LANES), 0)
+    blank = jnp.where(place == 5, -4096.0, 0.0)
     for k in range(coef.shape[0] // KDIM):
-        coef[k * KDIM + 5 : k * KDIM + 6, :] = jnp.full((1, LANES), -4096.0)
-
-    def fetch(k, _):
+        for part in range(3):
+            at = k * KDIM + part * PART
+            coef[at : at + PART, :] = jnp.zeros_like(blank) if part else blank
+    for k in range(listed):
         apart = me ^ (pack_ref[0, slots[k]] // per_owner)
-        near = sum((((apart >> bit) & 1) << t) for t, bit in enumerate(hop_bits))
-        start = (apart & (INNER - 1)) * (COEFS * outer) + near
+        near_by = sum((((apart >> bit) & 1) << t) for t, bit in enumerate(hop_bits))
+        start = (apart & (INNER - 1)) * (COEFS * outer) + near_by
         value = raw[pl.ds(start, COEFS, stride=outer), :]
+        live = k < count
         for part, piece in enumerate(three_parts(value)):
-            base = pl.multiple_of(k * KDIM + part * PART, PART)
-            coef[pl.ds(base, COEFS), :] = piece
-            coef[pl.ds(base + COEFS, 1), :] = piece[0:1, :]
-            coef[pl.ds(base + COEFS + 1, 3), :] = piece[COEFS - 3 : COEFS, :]
-        return 0
-
-    lax.fori_loop(0, count, fetch, 0)
+            at = k * KDIM + part * PART
+            piece = jnp.where(live, piece, blank[:COEFS, :] if part == 0 else 0.0)
+            coef[at : at + COEFS, :] = piece
+            coef[at + COEFS : at + COEFS + 1, :] = piece[0:1, :]
+            coef[at + COEFS + 1 : at + COEFS + 4, :] = piece[COEFS - 3 : COEFS, :]
 
     sub = lax.broadcasted_iota(jnp.int32, (SUB, LANES), 0)
     one = jnp.ones((SUB, LANES), jnp.float32)
@@ -484,7 +487,7 @@
 
     rows[...] = jnp.zeros(rows.shape, jnp.float32)
 
-    def gather_moments(k, _):
+    def gather_moments(k):
         part = lambda order, m: found[k, order : order + 1, m * LANES : (m + 1) * LANES]
         rise = yrows - 4.0
         s0, x1, x2 = part(0, 0), part(1, 0), part(2, 0) + part(3, 0)
@@ -492,10 +495,10 @@
         answer = [s0, x1, rise * s0 - t1, x2, rise * x1 - tx, rise * (rise * s0 - 2.0 * t1) + t2]
         answer += [part(0, 3 + c) for c in range(3)]
         for m, value in enumerate(answer):
-            rows[pl.ds(k * MSG + m, 1), :] = value
-        return 0
-
-    lax.fori_loop(0, count, gather_moments, 0)
+            rows[k * MSG + m : k * MSG + m + 1, :] = jnp.where(k < count, value, 0.0)
+
+    for k in range(listed):
+        gather_moments(k)
     rows[...] = exact_pick(rows[...], segment_order(True))
 
     if peers > listed:
@@ -503,15 +506,11 @@
         for peer in range(peers):
             out_ref[peer] = jnp.broadcast_to(absent, (MSG, LANES))
 
-    def send(k, _):
+    for k in range(listed):
         block = pack_ref[0, slots[k]]
-        owner = block // per_owner
         place = (block % per_owner).astype(jnp.float32)
-        rows[pl.ds(k * MSG + 9, 1), :] = jnp.where(lane == 16, place, meta)
-        out_ref[owner] = rows[pl.ds(pl.multiple_of(k * MSG, MSG), MSG), :]
-        return 0
-
-    lax.fori_loop(0, listed, send, 0)
+        rows[k * MSG + 9 : k * MSG + 10, :] = jnp.where(lane == 16, place, meta)
+        out_ref[block // per_owner] = rows[k * MSG : (k + 1) * MSG, :]
 
 
 def owner_kernel(

time: 50.3 us -> 49.5 us (0.984)
  blocking collectives: 21.2 us -> 11.7 us
  Pallas kernels: 5.77 us -> 14.6 us
    all_to_all x1, blocking collectives: 21.2 us -> 11.7 us  [on_device(): lax.all_to_all(outbox, 'tile', split_axis=0, concat_axis=0, tiled=True)]
    pallas_call x1, Pallas kernels: 3.27 us -> 12.1 us  [on_device(): pl.pallas_call(functools.partial(render_kernel, pixels, blocks, listed, h...]
where the time goes in v9:
time: 49.5 us; the launch traced here: 49.3 us
  Pallas kernels  14.6 us (29%)
  starting transfers between devices  12.4 us (25%)
  blocking collectives  11.7 us (24%)
  waiting for transfers between devices  6.12 us (12%)
  between operations  2.1 us (4%)
  local copies, waits for them, and re-layouts  1.52 us (3%)
  other arithmetic  0.86 us (2%)
    ppermute x7, starting transfers between devices, swap(): return lax.ppermute(value, 'tile', [(i, i ^ mask) for i in range(peers)])  12.4 us
    pallas_call x1, Pallas kernels, on_device(): pl.pallas_call(functools.partial(render_kernel, pixels, blocks, listed, h...  12.1 us
    all_to_all x1, blocking collectives, on_device(): lax.all_to_all(outbox, 'tile', split_axis=0, concat_axis=0, tiled=True)  11.7 us
    ppermute x7, waiting for transfers between devices, swap(): return lax.ppermute(value, 'tile', [(i, i ^ mask) for i in range(peers)])  3.76 us
    unnamed x21, local copies, waits for them, and re-layouts  1.52 us
    ppermute x1, waiting for transfers between devices, on_device(): theirs = lax.ppermute(sent[n], 'scene', route)  1.24 us
    pallas_call x1, Pallas kernels, on_device(): pl.pallas_call(owner_kernel, out_shape=(shape_of(own.shape, f32), shape_o...  1.15 us
    ppermute x1, waiting for transfers between devices, on_device(): lists = [lax.ppermute(share, 'scene', route) for route in routes]  1.12 us
  transfers between devices with their start and end apart: 9, of which 4 were waited for; matrix products, arithmetic and copies ran while one was open for 0% of the time, Pallas kernels for 2%

profile of v9, /device:TPU:0, one launch (start us, length us, event | category | flops | bytes accessed | tf_op | source)
XLA Modules:
  0.0 49.3 jit_solution(13078408112370248504)
XLA Ops:
  0.6 0.0 copy-start.4
  0.6 4.1 %collective-permute-start.1 = (f32[1,59,2,128]{3,2,1,0:T(2,128)}, f32[1,59,2,128]{3,2,1,0:T(2,128)S(1)}, u32[]{:S(2)}, u32[]{:S(2)}) collective-permute-start(f32[1,59,2,128]{3,2,1,0:T(2,128)} %bitcast.38), channel_id=1, source_target_pairs={{0,8},{1,9},{2,10},{3,11},{4,12},{5,13},{6,14},{7,15},{8,0},{9,1},... | collective-permute-start | bytes 181256 | tf_op jit(solution)/shard_map/ppermute | solution.py:704
  6.0 0.0 copy-start.7
  6.0 0.0 copy-start.8
  6.1 0.0 copy-done.4
  6.1 0.6 %copy-done.7 = s32[1,1,16]{2,1,0:T(1,128)S(1)} copy-done((s32[1,1,16]{2,1,0:T(1,128)S(1)}, s32[1,1,16]{2,1,0:T(1,128)}, u32[]{:S(2)}) %copy-start.7) | copy-done | bytes 88
  6.7 0.0 copy-done.8
  6.7 0.1 pack.1
  6.8 1.5 %collective-permute-start.3 = (f32[1,32]{1,0:T(1,128)S(1)}, f32[1,32]{1,0:T(1,128)S(1)}, u32[]{:S(2)}, u32[]{:S(2)}) collective-permute-start(f32[1,32]{1,0:T(1,128)S(1)} %get-tuple-element.26.ids_ref), channel_id=1, source_target_pairs={{0,1},{1,0},{2,3},{3,2},{4,5},{5,4},{6,7},{7,6},{8,9},{9,8},{10,11... | collective-permute-start | bytes 392 | tf_op jit(solution)/shard_map/ppermute | solution.py:704
  8.3 0.0 copy-start.3
  8.3 0.8 %copy-done.3 = f32[1,2,59,128]{3,1,2,0:T(2,128)S(1)} copy-done((f32[1,2,59,128]{3,1,2,0:T(2,128)S(1)}, f32[1,2,59,128]{3,1,2,0:T(2,128)}, u32[]{:S(2)}) %copy-start.3) | copy-done | bytes 60440
  9.2 0.0 collective-permute-done.1
  9.2 0.1 pad_maximum_fusion.1
  9.2 1.6 %collective-permute-start.2 = (f32[2,59,2,128]{3,2,1,0:T(2,128)S(1)}, f32[2,59,2,128]{3,2,1,0:T(2,128)S(1)}, u32[]{:S(2)}, u32[]{:S(2)}) collective-permute-start(f32[2,59,2,128]{3,2,1,0:T(2,128)S(1)} %pad_maximum_fusion.1), channel_id=1, source_target_pairs={{0,4},{1,5},{2,6},{3,7},{4,0},{5,1},{6,2},{7,3},{8,12},{9,13},{10,... | collective-permute-start | bytes 362504 | tf_op jit(solution)/shard_map/ppermute | solution.py:704
  10.9 0.0 collective-permute-done.3
  10.9 1.6 %collective-permute-start.4 = (f32[2,32]{1,0:T(2,128)S(1)}, f32[2,32]{1,0:T(2,128)S(1)}, u32[]{:S(2)}, u32[]{:S(2)}) collective-permute-start(f32[2,32]{1,0:T(2,128)S(1)} %pad_maximum_fusion.3), channel_id=1, source_target_pairs={{0,2},{1,3},{2,0},{3,1},{4,6},{5,7},{6,4},{7,5},{8,10},{9,11},{10,... | collective-permute-start | bytes 776 | tf_op jit(solution)/shard_map/ppermute | solution.py:704
  12.5 2.0 %collective-permute-done.4 = f32[2,32]{1,0:T(2,128)S(1)} collective-permute-done((f32[2,32]{1,0:T(2,128)S(1)}, f32[2,32]{1,0:T(2,128)S(1)}, u32[]{:S(2)}, u32[]{:S(2)}) %collective-permute-start.4) | collective-permute-done | bytes 288 | tf_op jit(solution)/shard_map/ppermute | solution.py:704
  14.5 0.0 collective-permute-done.2
  14.6 0.1 pad_maximum_fusion.raw_ref
  14.7 0.0 copy-start.5
  14.7 0.0 copy-start.9
  14.7 0.0 copy-start
  14.7 0.0 copy-start.2
  14.7 0.0 copy-start.6
  14.7 0.4 project.1
  15.2 0.0 copy-start.1
  15.2 1.1 %collective-permute-start.5 = (f32[36,128]{1,0:T(8,128)S(1)}, f32[36,128]{1,0:T(8,128)S(1)}, u32[]{:S(2)}, u32[]{:S(2)}) collective-permute-start(f32[36,128]{1,0:T(8,128)S(1)} %get-tuple-element.28), channel_id=1, source_target_pairs={{0,1},{1,0},{2,3},{3,2},{4,5},{5,4},{6,7},{7,6},{8,9},{9,8},{10,11... | collective-permute-start | bytes 55304 | tf_op jit(solution)/shard_map/ppermute | solution.py:704
  16.2 1.5 %collective-permute-start.6 = (f32[36,128]{1,0:T(8,128)S(1)}, f32[36,128]{1,0:T(8,128)S(1)}, u32[]{:S(2)}, u32[]{:S(2)}) collective-permute-start(f32[36,128]{1,0:T(8,128)S(1)} %get-tuple-element.29), channel_id=1, source_target_pairs={{0,2},{1,3},{2,0},{3,1},{4,6},{5,7},{6,4},{7,5},{8,10},{9,11},{10,... | collective-permute-start | bytes 55304 | tf_op jit(solution)/shard_map/ppermute | solution.py:704
  17.8 1.0 %collective-permute-start.7 = (f32[36,128]{1,0:T(8,128)S(1)}, f32[36,128]{1,0:T(8,128)S(1)}, u32[]{:S(2)}, u32[]{:S(2)}) collective-permute-start(f32[36,128]{1,0:T(8,128)S(1)} %get-tuple-element.30), channel_id=1, source_target_pairs={{0,3},{1,2},{2,1},{3,0},{4,7},{5,6},{6,5},{7,4},{8,11},{9,10},{10,... | collective-permute-start | bytes 55304 | tf_op jit(solution)/shard_map/ppermute | solution.py:704
  18.7 0.0 copy-done.5
  18.8 0.0 collective-permute-start
  18.8 0.0 copy-done.9
  18.8 1.1 %collective-permute-done.refs_0_ = s32[2,64]{1,0:T(2,128)S(1)} collective-permute-done((s32[2,64]{1,0:T(2,128)S(1)}, s32[2,64]{1,0:T(2,128)S(1)}, u32[]{:S(2)}, u32[]{:S(2)}) %collective-permute-start) | collective-permute-done | bytes 544 | tf_op jit(solution)/shard_map/ppermute | solution.py:751
  19.9 0.0 copy-done
  19.9 0.0 copy-done.2
  19.9 0.0 copy-done.6
  19.9 0.8 %prepare.1 = (f32[59,2,128]{2,1,0:T(2,128)S(1)}, f32[59,2,128]{2,1,0:T(2,128)S(1)}, bf16[1,256,256]{2,1,0:T(8,128)(2,1)S(1)}, f32[1,2,128]{2,1,0:T(2,128)S(1)}) custom-call(s32[1]{0:T(128)} %bitcast.3.group_ref, f32[59,2,128]{2,1,0:T(2,128)S(1)} %hold.1.own_ref, f32[59,2,128]{2,1,0:T(2,128)S(1)} %bitcast.37, f32[59,2,128]{2,1,0:T(2,128)S(1)} %bitcast.34, ...), custom_call_target="tpu_custom_call" | custom-call | tf_op jit(solution)/shard_map/prepare/pallas_call | solution.py:753
  20.7 0.0 collective-permute-done.5.src1
  20.7 0.0 collective-permute-done.6.src2
  20.7 1.7 %collective-permute-done.7.src3 = f32[36,128]{1,0:T(8,128)S(1)} collective-permute-done((f32[36,128]{1,0:T(8,128)S(1)}, f32[36,128]{1,0:T(8,128)S(1)}, u32[]{:S(2)}, u32[]{:S(2)}) %collective-permute-start.7) | collective-permute-done | bytes 18464 | tf_op jit(solution)/shard_map/ppermute | solution.py:704
  22.4 0.0 copy-done.1
  22.5 12.1 %render.1 = f32[16,16,128]{2,1,0:T(8,128)S(1)} custom-call(s32[1]{0:T(128)} %bitcast.me_ref, s32[1,48]{1,0:T(1,128)S(1)} %get-tuple-element.25.pack_ref, f32[1,32]{1,0:T(1,128)S(1)} %get-tuple-element.26.ids_ref, f32[36,128]{1,0:T(8,128)S(1)} %get-tuple-element.27.src0, f32[36,128]{1,0:T(8,128)S(1)} %collective-permute-done.5.src1, ...), custom_call_target="tpu_custom_call" | custom-call | tf_op jit(solution)/shard_map/render/pallas_call | solution.py:779
  34.5 11.7 %all_to_all.5 = f32[16,16,128]{2,1,0:T(8,128)S(1)} all-to-all(f32[16,16,128]{2,1,0:T(8,128)S(1)} %render.1), channel_id=1, replica_groups=mesh['scene'=2,'tile'=16] {'tile'}, dimensions={0} | all-to-all | bytes 262144 | tf_op jit(solution)/shard_map/all_to_all | solution.py:812
  46.2 1.2 %owner.1 = (f32[59,2,128]{2,1,0:T(2,128)}, f32[59,2,128]{2,1,0:T(2,128)S(1)}, f32[1,59,2,128]{3,2,1,0:T(2,128)S(1)}) custom-call(f32[256,128]{1,0:T(8,128)S(1)} %bitcast.33, f32[59,2,128]{2,1,0:T(2,128)S(1)} %hold.1.own_ref, f32[59,2,128]{2,1,0:T(2,128)S(1)} %get-tuple-element.31.base_ref, f32[59,2,128]{2,1,0:T(2,128)S(1)} %bitcast.35, ...), custom_call_target="tpu_custom_call" | custom-call | tf_op jit(solution)/shard_map/owner/pallas_call | solution.py:813
  47.4 0.0 collective-permute-start.8
  47.4 1.2 %collective-permute-done.8 = f32[59,2,128]{2,1,0:T(2,128)S(1)} collective-permute-done((f32[59,2,128]{2,1,0:T(2,128)S(1)}, f32[59,2,128]{2,1,0:T(2,128)S(1)}, u32[]{:S(2)}, u32[]{:S(2)}) %collective-permute-start.8) | collective-permute-done | bytes 60448 | tf_op jit(solution)/shard_map/ppermute | solution.py:828
  48.6 0.7 %select_bitcast_fusion = f32[1,2,59,128]{3,1,2,0:T(2,128)} fusion(f32[59,2,128]{2,1,0:T(2,128)S(1)} %get-tuple-element.36, f32[59,2,128]{2,1,0:T(2,128)S(1)} %collective-permute-done.8, pred[2,128]{1,0:T(4,128)(4,1)S(1)} %compare_bitcast_fusion), kind=kLoop, calls=%fused_computation.2 | loop fusion | flops 60416 | bytes 181504 | tf_op jit(solution)/shard_map/broadcast_in_dim | solution.py:831
  (5 shorter events, 0.0 us)
Async XLA Ops:
  0.6 5.4 %copy-start.4 = (f32[16,16]{1,0:T(8,128)S(1)}, f32[16,16]{1,0:T(8,128)}, u32[]{:S(2)}) copy-start(f32[16,16]{1,0:T(8,128)} %cameras_ref.1) | copy-start | bytes 3076
  0.6 8.5 %collective-permute-start.1 = (f32[1,59,2,128]{3,2,1,0:T(2,128)}, f32[1,59,2,128]{3,2,1,0:T(2,128)S(1)}, u32[]{:S(2)}, u32[]{:S(2)}) collective-permute-start(f32[1,59,2,128]{3,2,1,0:T(2,128)} %bitcast.38), channel_id=1, source_target_pairs={{0,8},{1,9},{2,10},{3,11},{4,12},{5,13},{6,14},{7,15},{8,0},{9,1},... | collective-permute-start | bytes 181256 | tf_op jit(solution)/shard_map/ppermute | solution.py:704
  6.0 0.7 %copy-start.7 = (s32[1,1,16]{2,1,0:T(1,128)S(1)}, s32[1,1,16]{2,1,0:T(1,128)}, u32[]{:S(2)}) copy-start(s32[1,1,16]{2,1,0:T(1,128)} %param.18) | copy-start | bytes 196
  6.0 0.7 %copy-start.8 = (s32[1,1,16]{2,1,0:T(1,128)S(1)}, s32[1,1,16]{2,1,0:T(1,128)}, u32[]{:S(2)}) copy-start(s32[1,1,16]{2,1,0:T(1,128)} %param.19) | copy-start | bytes 196
  6.8 4.1 %collective-permute-start.3 = (f32[1,32]{1,0:T(1,128)S(1)}, f32[1,32]{1,0:T(1,128)S(1)}, u32[]{:S(2)}, u32[]{:S(2)}) collective-permute-start(f32[1,32]{1,0:T(1,128)S(1)} %get-tuple-element.26.ids_ref), channel_id=1, source_target_pairs={{0,1},{1,0},{2,3},{3,2},{4,5},{5,4},{6,7},{7,6},{8,9},{9,8},{10,11... | collective-permute-start | bytes 392 | tf_op jit(solution)/shard_map/ppermute | solution.py:704
  8.3 0.8 %copy-start.3 = (f32[1,2,59,128]{3,1,2,0:T(2,128)S(1)}, f32[1,2,59,128]{3,1,2,0:T(2,128)}, u32[]{:S(2)}) copy-start(f32[1,2,59,128]{3,1,2,0:T(2,128)} %param.12) | copy-start | bytes 181252
  9.2 5.3 %collective-permute-start.2 = (f32[2,59,2,128]{3,2,1,0:T(2,128)S(1)}, f32[2,59,2,128]{3,2,1,0:T(2,128)S(1)}, u32[]{:S(2)}, u32[]{:S(2)}) collective-permute-start(f32[2,59,2,128]{3,2,1,0:T(2,128)S(1)} %pad_maximum_fusion.1), channel_id=1, source_target_pairs={{0,4},{1,5},{2,6},{3,7},{4,0},{5,1},{6,2},{7,3},{8,12},{9,13},{10,... | collective-permute-start | bytes 362504 | tf_op jit(solution)/shard_map/ppermute | solution.py:704
  10.9 3.6 %collective-permute-start.4 = (f32[2,32]{1,0:T(2,128)S(1)}, f32[2,32]{1,0:T(2,128)S(1)}, u32[]{:S(2)}, u32[]{:S(2)}) collective-permute-start(f32[2,32]{1,0:T(2,128)S(1)} %pad_maximum_fusion.3), channel_id=1, source_target_pairs={{0,2},{1,3},{2,0},{3,1},{4,6},{5,7},{6,4},{7,5},{8,10},{9,11},{10,... | collective-permute-start | bytes 776 | tf_op jit(solution)/shard_map/ppermute | solution.py:704
  14.7 4.1 %copy-start.5 = (s32[1,1,2,64]{3,2,1,0:T(2,128)S(1)}, s32[1,1,2,64]{3,2,1,0:T(2,128)}, u32[]{:S(2)}) copy-start(s32[1,1,2,64]{3,2,1,0:T(2,128)} %param.22) | copy-start | bytes 1540
  14.7 4.1 %copy-start.9 = (f32[1,1,3,1024]{3,1,2,0:T(1,128)S(1)}, f32[1,1,3,1024]{3,1,2,0:T(1,128)}, u32[]{:S(2)}) copy-start(f32[1,1,3,1024]{3,1,2,0:T(1,128)} %param.21) | copy-start | bytes 36868
  14.7 5.2 %copy-start = (f32[1,2,59,128]{3,1,2,0:T(2,128)S(1)}, f32[1,2,59,128]{3,1,2,0:T(2,128)}, u32[]{:S(2)}) copy-start(f32[1,2,59,128]{3,1,2,0:T(2,128)} %param.14) | copy-start | bytes 181252
  14.7 5.2 %copy-start.2 = (f32[1,2,59,128]{3,1,2,0:T(2,128)S(1)}, f32[1,2,59,128]{3,1,2,0:T(2,128)}, u32[]{:S(2)}) copy-start(f32[1,2,59,128]{3,1,2,0:T(2,128)} %param.13) | copy-start | bytes 181252
  14.7 5.2 %copy-start.6 = (f32[59]{0:T(128)S(1)}, f32[59]{0:T(128)}, u32[]{:S(2)}) copy-start(f32[59]{0:T(128)} %step_ref.1) | copy-start | bytes 712
  15.2 7.3 %copy-start.1 = (bf16[48,1408]{1,0:T(8,128)(2,1)S(1)}, bf16[48,1408]{1,0:T(8,128)(2,1)}, u32[]{:S(2)}) copy-start(bf16[48,1408]{1,0:T(8,128)(2,1)} %constant.16.clone.basis_ref) | copy-start | bytes 405508
  15.2 5.5 %collective-permute-start.5 = (f32[36,128]{1,0:T(8,128)S(1)}, f32[36,128]{1,0:T(8,128)S(1)}, u32[]{:S(2)}, u32[]{:S(2)}) collective-permute-start(f32[36,128]{1,0:T(8,128)S(1)} %get-tuple-element.28), channel_id=1, source_target_pairs={{0,1},{1,0},{2,3},{3,2},{4,5},{5,4},{6,7},{7,6},{8,9},{9,8},{10,11... | collective-permute-start | bytes 55304 | tf_op jit(solution)/shard_map/ppermute | solution.py:704
  16.2 4.5 %collective-permute-start.6 = (f32[36,128]{1,0:T(8,128)S(1)}, f32[36,128]{1,0:T(8,128)S(1)}, u32[]{:S(2)}, u32[]{:S(2)}) collective-permute-start(f32[36,128]{1,0:T(8,128)S(1)} %get-tuple-element.29), channel_id=1, source_target_pairs={{0,2},{1,3},{2,0},{3,1},{4,6},{5,7},{6,4},{7,5},{8,10},{9,11},{10,... | collective-permute-start | bytes 55304 | tf_op jit(solution)/shard_map/ppermute | solution.py:704
  17.8 4.7 %collective-permute-start.7 = (f32[36,128]{1,0:T(8,128)S(1)}, f32[36,128]{1,0:T(8,128)S(1)}, u32[]{:S(2)}, u32[]{:S(2)}) collective-permute-start(f32[36,128]{1,0:T(8,128)S(1)} %get-tuple-element.30), channel_id=1, source_target_pairs={{0,3},{1,2},{2,1},{3,0},{4,7},{5,6},{6,5},{7,4},{8,11},{9,10},{10,... | collective-permute-start | bytes 55304 | tf_op jit(solution)/shard_map/ppermute | solution.py:704
  18.8 1.1 %collective-permute-start = (s32[2,64]{1,0:T(2,128)S(1)}, s32[2,64]{1,0:T(2,128)S(1)}, u32[]{:S(2)}, u32[]{:S(2)}) collective-permute-start(s32[2,64]{1,0:T(2,128)S(1)} %bitcast.40), channel_id=1, source_target_pairs={{0,16},{16,0},{1,17},{17,1},{2,18},{18,2},{3,19},{19,3},{4,20},{20... | collective-permute-start | bytes 1544 | tf_op jit(solution)/shard_map/ppermute | solution.py:751
  47.4 1.2 %collective-permute-start.8 = (f32[59,2,128]{2,1,0:T(2,128)S(1)}, f32[59,2,128]{2,1,0:T(2,128)S(1)}, u32[]{:S(2)}, u32[]{:S(2)}) collective-permute-start(f32[59,2,128]{2,1,0:T(2,128)S(1)} %bitcast.44), channel_id=1, source_target_pairs={{0,16},{16,0},{1,17},{17,1},{2,18},{18,2},{3,19},{19,3},{4,20},{20... | collective-permute-start | bytes 181256 | tf_op jit(solution)/shard_map/ppermute | solution.py:828
